TPU v7x, 32 devices: a whole 2x2x4 slice. The times are simulated.
32 devices in a mesh: expert: 8 (over z, y), tensor: 4 (over x, core).
Axes of the slice: x: 2, y: 2, z: 4, core: 2. Of those that a mesh axis runs over, the one named last changes fastest.
Arguments:
- tokens: bfloat16 [6144, 768], P('expert'), may hold values from -6 to 6
- order: int32 [6144], replicated, may hold values from 0 to 6143, as said below
- lengths: int32 [8, 3], P('expert'), may hold values from 1 to 512, 768 in all within a row
- routes: int32 [6144, 2], P('expert'), may hold values from 0 to 15, all different within a row
- attn_gain: bfloat16 [768], replicated, may hold values from 0.5 to 1.5
- w_query: bfloat16 [768, 768], P(None, 'tensor'), may hold values from -0.21875 to 0.21875
- w_key: bfloat16 [768, 768], P(None, 'tensor'), may hold values from -0.21875 to 0.21875
- w_value: bfloat16 [768, 768], P(None, 'tensor'), may hold values from -0.21875 to 0.21875
- w_out: bfloat16 [768, 768], P('tensor'), may hold values from -1.25 to 1.25
- ffn_gain: bfloat16 [768], replicated, may hold values from 0.5 to 1.5
- w_router: bfloat16 [768, 16], replicated, may hold values from -0.21875 to 0.21875
- shared_gate: bfloat16 [768, 2048], P(None, 'tensor'), may hold values from -0.21875 to 0.21875
- shared_up: bfloat16 [768, 2048], P(None, 'tensor'), may hold values from -0.21875 to 0.21875
- shared_down: bfloat16 [2048, 768], P('tensor'), may hold values from -0.125 to 0.125
- expert_gate: bfloat16 [16, 768, 2048], P('expert', None, 'tensor'), may hold values from -0.21875 to 0.21875
- expert_up: bfloat16 [16, 768, 2048], P('expert', None, 'tensor'), may hold values from -0.21875 to 0.21875
- expert_down: bfloat16 [16, 2048, 768], P('expert', 'tensor'), may hold values from -0.125 to 0.125
- cotangent: bfloat16 [6144, 768], P('expert'), may hold values from -6 to 6
Outputs:
- output: bfloat16 [6144, 768], P('expert')
- d_tokens: bfloat16 [6144, 768], P('expert')
- g_attn_gain: float32 [768], replicated
- g_query: float32 [768, 768], P(None, 'tensor')
- g_key: float32 [768, 768], P(None, 'tensor')
- g_value: float32 [768, 768], P(None, 'tensor')
- g_out: float32 [768, 768], P('tensor')
- g_ffn_gain: float32 [768], replicated
- g_router: float32 [768, 16], replicated
- g_shared_gate: float32 [768, 2048], P(None, 'tensor')
- g_shared_up: float32 [768, 2048], P(None, 'tensor')
- g_shared_down: float32 [2048, 768], P('tensor')
- g_expert_gate: float32 [16, 768, 2048], P('expert', None, 'tensor')
- g_expert_up: float32 [16, 768, 2048], P('expert', None, 'tensor')
- g_expert_down: float32 [16, 2048, 768], P('expert', 'tensor')
Inputs may be any that keep to these rules, and one draw needn't show every extreme that they name: `order`: a permutation; of the 768 given rows of each aligned block, exactly 96 go to each group, group g being grouped rows g * 768 to (g + 1) * 768 - 1. Row g holds the lengths of group g's sequences, summing to 768, the largest exactly 512. `routes`: each row names two different experts.
All inputs are finite; a program needn't handle non-finite values.
Results may differ from a plain program's by a relative error of at most 0.015.
Values may be sent and summed in bfloat16 or wider, within the bound.
No kernel may reach another device: no remote copies, remote signals or barrier semaphores. Data moves between devices by JAX's collectives and lax.ppermute only.
A program may use at most 384 MiB of HBM per device.

v0:
```python
import jax
import jax.numpy as jnp
from jax import lax
from jax.sharding import PartitionSpec as P

HD = 64
EXPERTS = 16
CAP = 120


EPSILON = 1e-05
ROPE_BASE = 10000.0
MASKED = -1e30


def rms_scale(values):
    return lax.rsqrt(jnp.mean(values * values, axis=-1, keepdims=True) + EPSILON)


def matmul(left_side, right_side):
    return jnp.dot(left_side, right_side, preferred_element_type=jnp.float32)


def matmul_bt(left_side, right_side):
    return lax.dot_general(
        left_side, right_side, (((1,), (1,)), ((), ())), preferred_element_type=jnp.float32
    )


def matmul_at(left_side, right_side):
    return lax.dot_general(
        left_side, right_side, (((0,), (0,)), ((), ())), preferred_element_type=jnp.float32
    )


def silu_value(gate_in):
    return gate_in * jax.nn.sigmoid(gate_in)


def silu_slope(gate_in):
    sigma = jax.nn.sigmoid(gate_in)
    return sigma * (1.0 + gate_in * (1.0 - sigma))


def rotate(values, cos_table, sin_table):
    half_size = HD // 2
    shaped = values.reshape(values.shape[0], -1, HD)
    front_half = shaped[..., :half_size]
    back_half = shaped[..., half_size:]
    cos_wide = cos_table[:, None, :]
    sin_wide = sin_table[:, None, :]
    turned = jnp.concatenate(
        [
            front_half * cos_wide - back_half * sin_wide,
            back_half * cos_wide + front_half * sin_wide,
        ],
        axis=-1,
    )
    return turned.reshape(values.shape)


def block_scores(query, key, sequence_segment, block_index, block_rows, score_scale):
    start_row = block_index * block_rows
    end_row = start_row + block_rows
    q_part = query[start_row:end_row].reshape(block_rows, -1, HD)
    k_part = key[:end_row].reshape(end_row, -1, HD)
    scores = (
        jnp.einsum("qhd,khd->hqk", q_part, k_part, preferred_element_type=jnp.float32) * score_scale
    )
    q_rows = jnp.arange(start_row, end_row, dtype=jnp.int32)
    k_rows = jnp.arange(end_row, dtype=jnp.int32)
    allowed = (sequence_segment[start_row:end_row, None] == sequence_segment[None, :end_row]) & (
        q_rows[:, None] >= k_rows[None, :]
    )
    return (jnp.where(allowed[None], scores, MASKED), q_part, k_part)


def body(
    tokens,
    order,
    lengths,
    routes,
    attn_gain,
    w_query,
    w_key,
    w_value,
    w_out,
    ffn_gain,
    w_router,
    shared_gate,
    shared_up,
    shared_down,
    expert_gate,
    expert_up,
    expert_down,
    cotangent,
):
    row_count = tokens.shape[0]
    feat_width = tokens.shape[1]
    group_count = lax.axis_size("expert")
    share_rows = row_count // group_count
    all_rows = order.shape[0]
    my_group = lax.axis_index("expert")
    quarter = row_count // lax.axis_size("tensor")
    row_offset = lax.axis_index("tensor") * quarter
    replicas = max(1, group_count // EXPERTS)
    slab_dev = expert_gate.shape[0]
    slab_total = EXPERTS * replicas
    hidden_size = expert_gate.shape[2]
    block_rows = min(512, row_count)
    block_rows = 256
    block_count = row_count // block_rows
    score_scale = HD ** (-0.5)
    row_ids = jnp.arange(row_count, dtype=jnp.int32)
    local_order = lax.dynamic_slice_in_dim(order, my_group * row_count, row_count, 0)
    dest_group = local_order // row_count
    dest_onehot = (dest_group[:, None] == jnp.arange(group_count, dtype=jnp.int32)[None, :]).astype(
        jnp.int32
    )
    send_rank = jnp.sum(dest_onehot * jnp.cumsum(dest_onehot, axis=0), axis=1) - 1
    send_slot = dest_group * share_rows + send_rank
    send_source = jnp.zeros((row_count,), jnp.int32).at[send_slot].set(row_ids)
    arrived = (
        lax.all_to_all(
            tokens[send_source].reshape(group_count, share_rows, feat_width),
            "expert",
            split_axis=0,
            concat_axis=0,
            tiled=True,
        ),
        lax.all_to_all(
            cotangent[send_source].reshape(group_count, share_rows, feat_width),
            "expert",
            split_axis=0,
            concat_axis=0,
            tiled=True,
        ),
    )
    mine_mask = (order // row_count == my_group).astype(jnp.int32).reshape(group_count, row_count)
    all_rank = (jnp.cumsum(mine_mask, axis=1) - 1).reshape(-1)
    inverse = jnp.zeros((all_rows,), jnp.int32).at[order].set(jnp.arange(all_rows, dtype=jnp.int32))
    own_inverse = lax.dynamic_slice_in_dim(inverse, my_group * row_count, row_count, 0)
    pick = own_inverse // row_count * share_rows + all_rank[own_inverse]
    grouped = arrived[0].reshape(row_count, feat_width)[pick]
    grouped_cot = arrived[1].reshape(row_count, feat_width)[pick]
    seq_lengths = lengths[0]
    seq_ends = jnp.cumsum(seq_lengths)
    passed = row_ids[:, None] >= seq_ends[None, :]
    sequence_segment = jnp.sum(passed.astype(jnp.int32), axis=1)
    position = row_ids - jnp.sum(jnp.where(passed, seq_lengths[None, :], 0), axis=1)
    half_size = HD // 2
    frequency = ROPE_BASE ** (-jnp.arange(half_size, dtype=jnp.float32) / half_size)
    angles = position.astype(jnp.float32)[:, None] * frequency[None, :]
    cos_table = jnp.cos(angles)
    sin_table = jnp.sin(angles)
    resid = grouped.astype(jnp.float32)
    scale_one = rms_scale(resid)
    normed_one = resid * scale_one
    gain_one = attn_gain.astype(jnp.float32)
    hidden_one = (normed_one * gain_one).astype(jnp.bfloat16)
    query = rotate(matmul(hidden_one, w_query), cos_table, sin_table).astype(jnp.bfloat16)
    key = rotate(matmul(hidden_one, w_key), cos_table, sin_table).astype(jnp.bfloat16)
    value = matmul(hidden_one, w_value).astype(jnp.bfloat16)
    block_outputs = []
    log_totals = []
    for block_index in range(block_count):
        scores, q_part, k_part = block_scores(
            query, key, sequence_segment, block_index, block_rows, score_scale
        )
        row_max = jnp.max(scores, axis=-1, keepdims=True)
        log_total = row_max + jnp.log(jnp.sum(jnp.exp(scores - row_max), axis=-1, keepdims=True))
        weights = jnp.exp(scores - log_total).astype(jnp.bfloat16)
        end_row = (block_index + 1) * block_rows
        v_part = value[:end_row].reshape(end_row, -1, HD)
        mixture = jnp.einsum("hqk,khd->qhd", weights, v_part, preferred_element_type=jnp.float32)
        block_outputs.append(mixture.reshape(block_rows, -1))
        log_totals.append(log_total)
    attended = jnp.concatenate(block_outputs, axis=0).astype(jnp.bfloat16)
    attn_rows = lax.psum_scatter(matmul(attended, w_out), "tensor", scatter_dimension=0, tiled=True)
    resid_rows = lax.dynamic_slice_in_dim(resid, row_offset, quarter, 0) + attn_rows
    resid_two = lax.all_gather(resid_rows, "tensor", axis=0, tiled=True)
    scale_two = rms_scale(resid_two)
    normed_two = resid_two * scale_two
    gain_two = ffn_gain.astype(jnp.float32)
    hidden_two = (normed_two * gain_two).astype(jnp.bfloat16)
    gate_shared = matmul(hidden_two, shared_gate)
    up_shared = matmul(hidden_two, shared_up)
    act_shared = silu_value(gate_shared)
    shared_mid = (act_shared * up_shared).astype(jnp.bfloat16)
    shared_out = matmul(shared_mid, shared_down)
    logits = matmul(hidden_two, w_router)
    picked = routes[:, :, None] == jnp.arange(EXPERTS, dtype=jnp.int32)[None, None, :]
    chosen = jnp.sum(jnp.where(picked, logits[:, None, :], 0.0), axis=-1)
    raised = jnp.exp(chosen - jnp.max(chosen, axis=-1, keepdims=True))
    gate_weights = raised / jnp.sum(raised, axis=-1, keepdims=True)
    flat_routes = routes.reshape(-1)
    onehot = (flat_routes[:, None] == jnp.arange(EXPERTS, dtype=jnp.int32)[None, :]).astype(
        jnp.int32
    )
    slot_rank = jnp.sum(onehot * jnp.cumsum(onehot, axis=0), axis=1) - 1
    index_of_slot = jnp.where(slot_rank < CAP, flat_routes * CAP + slot_rank, EXPERTS * CAP)
    pair_rows = jnp.arange(2 * row_count, dtype=jnp.int32) // 2
    source_rows = (
        jnp.full((EXPERTS * CAP + 1,), row_count, jnp.int32)
        .at[index_of_slot]
        .set(pair_rows)[: EXPERTS * CAP]
    )
    padded_two = jnp.concatenate([hidden_two, jnp.zeros((1, feat_width), jnp.bfloat16)], axis=0)
    buffer = padded_two[source_rows].reshape(EXPERTS, CAP, feat_width)
    gathered_weights = (
        lax.all_gather(expert_gate, "expert", axis=0, tiled=True),
        lax.all_gather(expert_up, "expert", axis=0, tiled=True),
        lax.all_gather(expert_down, "expert", axis=0, tiled=True),
    )
    all_gate = gathered_weights[0].reshape(EXPERTS, replicas, feat_width, hidden_size)
    all_up = gathered_weights[1].reshape(EXPERTS, replicas, feat_width, hidden_size)
    all_down = gathered_weights[2].reshape(EXPERTS, replicas, hidden_size, feat_width)
    gate_all = jnp.einsum("kci,krif->krcf", buffer, all_gate, preferred_element_type=jnp.float32)
    up_all = jnp.einsum("kci,krif->krcf", buffer, all_up, preferred_element_type=jnp.float32)
    act_all = silu_value(gate_all)
    mid_all = (act_all * up_all).astype(jnp.bfloat16)
    expert_store = (
        jnp.einsum("krcf,krfd->kcd", mid_all, all_down, preferred_element_type=jnp.float32)
        .astype(jnp.bfloat16)
        .reshape(EXPERTS * CAP, feat_width)
    )
    expert_pad = jnp.concatenate([expert_store, jnp.zeros((1, feat_width), jnp.bfloat16)], axis=0)
    pair_out = expert_pad[index_of_slot].reshape(row_count, 2, feat_width).astype(jnp.float32)
    ffn_part = shared_out + jnp.sum(gate_weights[:, :, None] * pair_out, axis=1)
    ffn_rows = lax.psum_scatter(
        ffn_part.astype(jnp.bfloat16), "tensor", scatter_dimension=0, tiled=True
    ).astype(jnp.float32)
    output_rows = (resid_rows + ffn_rows).astype(jnp.bfloat16)
    grad_out = grouped_cot.astype(jnp.float32)
    d_mid_shared = matmul_bt(grouped_cot, shared_down)
    g_shared_down = matmul_at(shared_mid, grouped_cot)
    d_up_shared = (d_mid_shared * act_shared).astype(jnp.bfloat16)
    d_gate_shared = (d_mid_shared * up_shared * silu_slope(gate_shared)).astype(jnp.bfloat16)
    g_shared_gate = matmul_at(hidden_two, d_gate_shared)
    g_shared_up = matmul_at(hidden_two, d_up_shared)
    d_hidden = matmul_bt(d_gate_shared, shared_gate) + matmul_bt(d_up_shared, shared_up)
    d_gate_part = jnp.sum(grad_out[:, None, :] * pair_out, axis=-1)
    gate_slots = (
        jnp.zeros((EXPERTS * CAP + 1,), jnp.float32)
        .at[index_of_slot]
        .set(gate_weights.reshape(-1))[: EXPERTS * CAP]
    )
    padded_grad = jnp.concatenate([grad_out, jnp.zeros((1, feat_width), jnp.float32)], axis=0)
    grad_buffer = (
        (padded_grad[source_rows] * gate_slots[:, None])
        .astype(jnp.bfloat16)
        .reshape(EXPERTS, CAP, feat_width)
    )
    d_mid_all = jnp.einsum(
        "kcd,krfd->krcf", grad_buffer, all_down, preferred_element_type=jnp.float32
    )
    d_up_all = (d_mid_all * act_all).astype(jnp.bfloat16)
    d_gate_all = (d_mid_all * up_all * silu_slope(gate_all)).astype(jnp.bfloat16)
    back_rows = jnp.einsum(
        "krcf,krif->kci", d_gate_all, all_gate, preferred_element_type=jnp.float32
    )
    back_rows = back_rows + jnp.einsum(
        "krcf,krif->kci", d_up_all, all_up, preferred_element_type=jnp.float32
    )
    slab_grad = back_rows.astype(jnp.bfloat16).reshape(EXPERTS * CAP, feat_width)
    flat_gate = d_gate_all.reshape(slab_total, CAP, hidden_size)
    flat_up = d_up_all.reshape(slab_total, CAP, hidden_size)
    flat_mid = mid_all.reshape(slab_total, CAP, hidden_size)
    slab_count = lax.axis_size("expert") * slab_dev
    owners = jnp.arange(slab_count, dtype=jnp.int32) // replicas
    taken_rows = buffer[owners]
    grad_rows = grad_buffer[owners]
    term_gate = jnp.einsum(
        "sci,scf->sif", taken_rows, flat_gate, preferred_element_type=jnp.float32
    )
    term_up = jnp.einsum("sci,scf->sif", taken_rows, flat_up, preferred_element_type=jnp.float32)
    term_down = jnp.einsum("scf,scd->sfd", flat_mid, grad_rows, preferred_element_type=jnp.float32)
    own_terms = lax.psum_scatter(
        jnp.concatenate(
            [
                term_gate.reshape(slab_count, -1),
                term_up.reshape(slab_count, -1),
                term_down.reshape(slab_count, -1),
            ],
            axis=1,
        ),
        "expert",
        scatter_dimension=0,
        tiled=True,
    )
    piece_size = feat_width * hidden_size
    g_expert_gate = own_terms[:, :piece_size].reshape(slab_dev, feat_width, hidden_size)
    g_expert_up = own_terms[:, piece_size : 2 * piece_size].reshape(
        slab_dev, feat_width, hidden_size
    )
    g_expert_down = own_terms[:, 2 * piece_size :].reshape(slab_dev, hidden_size, feat_width)
    back_pad = jnp.concatenate(
        [slab_grad.astype(jnp.float32), jnp.zeros((1, feat_width), jnp.float32)], axis=0
    )
    d_hidden = d_hidden + jnp.sum(back_pad[index_of_slot].reshape(row_count, 2, feat_width), axis=1)
    d_hidden, d_gates = lax.psum((d_hidden, d_gate_part), "tensor")
    d_chosen = gate_weights * (d_gates - jnp.sum(gate_weights * d_gates, axis=-1, keepdims=True))
    d_logits = jnp.sum(jnp.where(picked, d_chosen[:, :, None], 0.0), axis=1).astype(jnp.bfloat16)
    g_router = matmul_at(hidden_two, d_logits)
    d_two = d_hidden + matmul_bt(d_logits, w_router)
    g_ffn_gain = jnp.sum(d_two * normed_two, axis=0)
    e_two = d_two * gain_two
    d_resid = grad_out + scale_two * (
        e_two - normed_two * jnp.mean(e_two * normed_two, axis=-1, keepdims=True)
    )
    d_proj = d_resid.astype(jnp.bfloat16)
    g_out = matmul_at(attended, d_proj)
    d_attended = matmul_bt(d_proj, w_out).astype(jnp.bfloat16)
    query_grads = []
    key_grad = jnp.zeros((row_count, query.shape[1]), jnp.float32)
    value_grad = jnp.zeros((row_count, query.shape[1]), jnp.float32)
    for block_index in range(block_count):
        scores, q_part, k_part = block_scores(
            query, key, sequence_segment, block_index, block_rows, score_scale
        )
        weights = jnp.exp(scores - log_totals[block_index])
        start_row = block_index * block_rows
        end_row = start_row + block_rows
        grad_part = d_attended[start_row:end_row].reshape(block_rows, -1, HD)
        v_part = value[:end_row].reshape(end_row, -1, HD)
        d_weights = jnp.einsum(
            "qhd,khd->hqk", grad_part, v_part, preferred_element_type=jnp.float32
        )
        row_inner = jnp.sum(weights * d_weights, axis=-1, keepdims=True)
        d_scores = (weights * (d_weights - row_inner)).astype(jnp.bfloat16)
        query_grads.append(
            (
                jnp.einsum("hqk,khd->qhd", d_scores, k_part, preferred_element_type=jnp.float32)
                * score_scale
            ).reshape(block_rows, -1)
        )
        key_term = (
            jnp.einsum("hqk,qhd->khd", d_scores, q_part, preferred_element_type=jnp.float32)
            * score_scale
        )
        key_grad = key_grad.at[:end_row].add(key_term.reshape(end_row, -1))
        value_term = jnp.einsum(
            "hqk,qhd->khd",
            weights.astype(jnp.bfloat16),
            grad_part,
            preferred_element_type=jnp.float32,
        )
        value_grad = value_grad.at[:end_row].add(value_term.reshape(end_row, -1))
    d_query = rotate(jnp.concatenate(query_grads, axis=0), cos_table, -sin_table).astype(
        jnp.bfloat16
    )
    d_key = rotate(key_grad, cos_table, -sin_table).astype(jnp.bfloat16)
    d_value = value_grad.astype(jnp.bfloat16)
    g_query = matmul_at(hidden_one, d_query)
    g_key = matmul_at(hidden_one, d_key)
    g_value = matmul_at(hidden_one, d_value)
    d_one = matmul_bt(d_query, w_query) + matmul_bt(d_key, w_key) + matmul_bt(d_value, w_value)
    d_one_rows = lax.psum_scatter(d_one, "tensor", scatter_dimension=0, tiled=True)
    normed_rows = lax.dynamic_slice_in_dim(normed_one, row_offset, quarter, 0)
    scale_rows = lax.dynamic_slice_in_dim(scale_one, row_offset, quarter, 0)
    resid_grad_rows = lax.dynamic_slice_in_dim(d_resid, row_offset, quarter, 0)
    gain_part = jnp.sum(d_one_rows * normed_rows, axis=0)
    e_one = d_one_rows * gain_one
    d_group_rows = (
        resid_grad_rows
        + scale_rows * (e_one - normed_rows * jnp.mean(e_one * normed_rows, axis=-1, keepdims=True))
    ).astype(jnp.bfloat16)
    whole_rows = (
        lax.all_gather(
            output_rows.astype(jnp.float32).astype(jnp.bfloat16), "tensor", axis=0, tiled=True
        ).astype(jnp.float32),
        lax.all_gather(
            d_group_rows.astype(jnp.float32).astype(jnp.bfloat16), "tensor", axis=0, tiled=True
        ).astype(jnp.float32),
        lax.all_gather(
            gain_part[None, :].astype(jnp.bfloat16), "tensor", axis=0, tiled=True
        ).astype(jnp.float32),
    )
    output_group = whole_rows[0].astype(jnp.bfloat16)
    d_group = whole_rows[1].astype(jnp.bfloat16)
    g_attn_gain = jnp.sum(whole_rows[2], axis=0)
    back_source = jnp.zeros((row_count,), jnp.int32).at[pick].set(row_ids)
    returned = (
        lax.all_to_all(
            output_group[back_source].reshape(group_count, share_rows, feat_width),
            "expert",
            split_axis=0,
            concat_axis=0,
            tiled=True,
        ),
        lax.all_to_all(
            d_group[back_source].reshape(group_count, share_rows, feat_width),
            "expert",
            split_axis=0,
            concat_axis=0,
            tiled=True,
        ),
    )
    output = returned[0].reshape(row_count, feat_width)[send_slot]
    d_tokens = returned[1].reshape(row_count, feat_width)[send_slot]
    members = [
        g_query,
        g_key,
        g_value,
        g_out,
        g_shared_gate,
        g_shared_up,
        g_shared_down,
        g_router,
        g_ffn_gain,
        g_attn_gain,
    ]
    flat_terms = jnp.concatenate([member.reshape(-1) for member in members], axis=0)
    summed_share = lax.psum_scatter(flat_terms, "expert", scatter_dimension=0, tiled=True)
    summed_flat = lax.all_gather(
        summed_share.astype(jnp.bfloat16), "expert", axis=0, tiled=True
    ).astype(summed_share.dtype)
    finished = []
    offset_at = 0
    for member in members:
        finished.append(summed_flat[offset_at : offset_at + member.size].reshape(member.shape))
        offset_at = offset_at + member.size
    (
        g_query,
        g_key,
        g_value,
        g_out,
        g_shared_gate,
        g_shared_up,
        g_shared_down,
        g_router,
        g_ffn_gain,
        g_attn_gain,
    ) = finished
    return (
        output,
        d_tokens,
        g_attn_gain,
        g_query,
        g_key,
        g_value,
        g_out,
        g_ffn_gain,
        g_router,
        g_shared_gate,
        g_shared_up,
        g_shared_down,
        g_expert_gate,
        g_expert_up,
        g_expert_down,
    )


def solution(mesh):
    return jax.shard_map(
        body,
        mesh=mesh,
        in_specs=(
            P("expert", None),
            P(),
            P("expert", None),
            P("expert", None),
            P(),
            P(None, "tensor"),
            P(None, "tensor"),
            P(None, "tensor"),
            P("tensor", None),
            P(),
            P(),
            P(None, "tensor"),
            P(None, "tensor"),
            P("tensor", None),
            P("expert", None, "tensor"),
            P("expert", None, "tensor"),
            P("expert", "tensor", None),
            P("expert", None),
        ),
        out_specs=(
            P("expert", None),
            P("expert", None),
            P(),
            P(None, "tensor"),
            P(None, "tensor"),
            P(None, "tensor"),
            P("tensor", None),
            P(),
            P(),
            P(None, "tensor"),
            P(None, "tensor"),
            P("tensor", None),
            P("expert", None, "tensor"),
            P("expert", None, "tensor"),
            P("expert", "tensor", None),
        ),
        check_vma=False,
    )
```

profile of v0, /device:TPU:0, one launch (start us, length us, event | category | flops | bytes accessed | tf_op | source)
XLA Modules:
  0.0 3694.2 jit_solution(1728767361818580013)
XLA Ops:
  8.0 23.0 scatter_custom_fusion.1
  41.0 7.4 all-to-all-start
  51.4 4.5 gather_fusion.1
  57.7 19.3 all-to-all-done
  91.9 30.6 reduce-scatter.4.cloned.1.call-done
  130.0 5.7 all-to-all-start.2
  137.2 4.5 reduce-window.43
  142.5 6.2 scatter_custom_fusion.2
  151.3 13.0 all-to-all-done.2
  171.2 7.0 gather_fusion.9
  184.2 7.0 gather_fusion.3
  192.2 6.6 scatter_custom_fusion.4
  210.6 4.7 multiply_convert_fusion
  215.3 4.3 gather_fusion.14
  225.8 101.9 %all-gather.11.cloned.1.call-done = bf16[16,768,512]{2,1,0:T(8,128)(2,1)} async-done(((bf16[2,768,512]{2,1,0:T(8,128)(2,1)}), bf16[16,768,512]{2,1,0:T(8,128)(2,1)}) %all-gather.11.cloned.1.call-update) | async-done | bytes 12582928 | tf_op jit(solution)/shard_map/all_gather | solution.py:211
  327.8 8.4 fusion.101
  336.2 168.5 %all-gather.13.cloned.1.call-done = bf16[16,768,512]{2,1,0:T(8,128)(2,1)} async-done(((bf16[2,768,512]{2,1,0:T(8,128)(2,1)}), bf16[16,768,512]{2,1,0:T(8,128)(2,1)}) %all-gather.13.cloned.1.call-update) | async-done | bytes 12582928 | tf_op jit(solution)/shard_map/all_gather | solution.py:212
  504.7 8.4 fusion.102
  513.1 168.5 %all-gather.15.cloned.1.call-done = bf16[16,512,768]{2,1,0:T(8,128)(2,1)} async-done(((bf16[2,512,768]{2,1,0:T(8,128)(2,1)}), bf16[16,512,768]{2,1,0:T(8,128)(2,1)}) %all-gather.15.cloned.1.call-update) | async-done | bytes 12582928 | tf_op jit(solution)/shard_map/all_gather | solution.py:213
  681.6 14.1 fusion.10
  695.7 7.2 convolution_convert_fusion
  703.1 5.6 gather_fusion.4
  708.7 6.3 reshape.995
  715.1 11.2 fusion.13
  726.3 10.9 add_convert_fusion
  740.2 9.5 gather_fusion.10
  749.7 6.9 reshape.969
  756.6 7.9 reduce_sum.228
  764.6 4.4 add_add_fusion.1
  769.0 13.8 multiply_reduce_fusion
  784.0 7.3 psum.15
  794.6 14.1 fusion.108
  808.7 25.5 copy.149
  834.2 10.2 fusion.107
  844.4 25.0 copy.148
  869.4 10.1 fusion.11
  879.5 25.1 copy.147
  961.8 20.3 reduce-scatter.8.cloned.1.call-done
  983.5 5.2 all-gather.1
  992.5 279.7 %all-reduce.19 = bf16[1783296]{0:T(1024)(128)(2,1)} all-reduce(f32[1783296]{0:T(1024)} %constant_dynamic-update-slice_fusion), channel_id=6, replica_groups=mesh['expert'=8,'tensor'=4] {'expert'}, use_global_device_ids=true, to_apply=%region_45.46.clone | all-reduce | flops 1783296 | bytes 10699776
  1275.4 7.6 dynamic-update-slice.16
  1283.0 61.4 %pad_maximum_fusion = f32[16,1179648]{1,0:T(8,128)} fusion(f32[16,393216]{1,0:T(8,128)} %bitcast.257, f32[16,393216]{1,0:T(8,128)} %bitcast.258, f32[16,393216]{1,0:T(8,128)} %bitcast.259), kind=kLoop, calls=%fused_computation.20 | loop fusion | flops 37748736 | bytes 150994944 | tf_op jit(solution)/shard_map/concatenate | solution.py:279
  1348.1 5.4 gather_fusion.5
  1357.9 40.1 %all-to-all-done.1 = bf16[8,96,768]{2,1,0:T(8,128)(2,1)S(1)} async-done(((bf16[8,96,768]{2,1,0:T(8,128)(2,1)}), bf16[8,96,768]{2,1,0:T(8,128)(2,1)S(1)}, u32[]{:S(2)}, u32[]{:S(2)}) %all-to-all-start.1) | async-done | bytes 1179680 | tf_op jit(solution)/shard_map/all_to_all | solution.py:384
  1401.4 5.4 gather_fusion.11
  1410.7 46.3 %all-reduce.16.cloned.1.call-done = bf16[1783296]{0:T(1024)(128)(2,1)} async-done(((bf16[1783296]{0:T(1024)(128)(2,1)}), bf16[1783296]{0:T(1024)(128)(2,1)}) %all-reduce.16.cloned.1.call-update) | async-done | bytes 3566608
  1484.3 2181.6 %all-reduce.18.cloned.1.call-done = f32[16,1179648]{1,0:T(8,128)} async-done(((f32[16,1179648]{1,0:T(8,128)}), f32[16,1179648]{1,0:T(8,128)}) %all-reduce.18.cloned.1.call-update) | async-done | bytes 75497488
  3665.9 14.6 fusion.89
  (458 shorter events, 193.5 us)
Async XLA Ops:
  7.2 30.4 copy-start
  34.1 6.9 copy-start.99
  41.0 7.7 copy-start.82
  41.0 10.0 copy-start.106
  41.0 10.3 copy-start.103
  41.0 36.0 all-to-all-start
  48.5 74.0 %reduce-scatter.4.cloned.1.call-start = ((), (), s32[]{:S(2)}) async-start(), calls=%async_computation.7 | async-start | bytes 2949120 | tf_op jit(solution)/shard_map/reduce_scatter | solution.py:179
  51.3 30.3 copy-start.93
  56.0 21.1 copy-start.101
  56.6 29.3 copy-start.39
  57.7 25.1 copy-start.48
  79.8 10.5 copy-start.19
  80.2 98.0 %copy-start.97 = (f32[768]{0:T(1024)}, f32[768]{0:T(1024)S(1)}, u32[]{:S(2)}) copy-start(f32[768]{0:T(1024)S(1)} %add_rsqrt_fusion.1) | copy-start | bytes 9220
  80.9 6.0 copy-start.45
  81.0 6.4 copy-start.62
  90.2 90.9 %all-gather.9.cloned.1.call-start = ((), (), s32[]{:S(2)}) async-start(), calls=%async_computation.8 | async-start | bytes 2949120 | tf_op jit(solution)/shard_map/all_gather | solution.py:181
  124.7 203.1 %all-gather.11.cloned.1.call-start = ((), (), s32[]{:S(2)}) async-start(), calls=%async_computation.9 | async-start | bytes 14155776 | tf_op jit(solution)/shard_map/all_gather | solution.py:211
  125.4 379.3 %all-gather.13.cloned.1.call-start = ((), (), s32[]{:S(2)}) async-start(), calls=%async_computation.10 | async-start | bytes 14155776 | tf_op jit(solution)/shard_map/all_gather | solution.py:212
  126.0 555.6 %all-gather.15.cloned.1.call-start = ((), (), s32[]{:S(2)}) async-start(), calls=%async_computation.11 | async-start | bytes 14155776 | tf_op jit(solution)/shard_map/all_gather | solution.py:213
  130.0 6.0 copy-start.88
  130.0 6.6 copy-start.104
  130.0 18.7 copy-start.105
  130.0 34.3 all-to-all-start.2
  135.7 770.8 %all-reduce.14.cloned.1.call-start = ((), (), s32[]{:S(2)}) async-start(), calls=%async_computation.14 | async-start | bytes 4718592 | tf_op jit(solution)/shard_map/psum | solution.py:301
  136.7 46.6 %copy-start.89 = (f32[768]{0:T(1024)}, f32[768]{0:T(1024)S(1)}, u32[]{:S(2)}) copy-start(f32[768]{0:T(1024)S(1)} %convert_element_type.191) | copy-start | bytes 9220
  184.2 22.0 copy-start.21
  184.2 7.0 copy-start.87
  191.7 9.2 copy-start.64
  695.7 7.2 copy-start.13
  708.7 6.4 copy-start.22
  769.0 187.6 %reduce-scatter.6.cloned.1.call-start = ((), (), s32[]{:S(2)}) async-start(), calls=%async_computation.12 | async-start | bytes 1474560 | tf_op jit(solution)/shard_map/reduce_scatter | solution.py:230
  769.0 25.6 copy-start.12
  808.7 25.5 copy-start.3
  808.7 25.5 copy-start.24
  844.4 25.0 copy-start.23
  879.5 25.1 copy-start.26
  879.5 25.1 copy-start.66
  879.5 25.1 copy-start.68
  906.4 75.6 %reduce-scatter.8.cloned.1.call-start = ((), (), s32[]{:S(2)}) async-start(), calls=%async_computation.15 | async-start | bytes 2949120 | tf_op jit(solution)/shard_map/reduce_scatter | solution.py:358
  910.2 19.6 copy-start.11
  919.6 11.4 copy-start.47
  951.1 397.0 %all-gather.17.cloned.1.call-start = ((), (), s32[]{:S(2)}) async-start(), calls=%async_computation.13 | async-start | bytes 1474560 | tf_op jit(solution)/shard_map/all_gather | solution.py:369
  958.5 31.5 copy-start.102
  958.6 442.9 %all-gather.19.cloned.1.call-start = ((), (), s32[]{:S(2)}) async-start(), calls=%async_computation.16 | async-start | bytes 1474560 | tf_op jit(solution)/shard_map/all_gather | solution.py:372
  992.4 464.6 %all-reduce.16.cloned.1.call-start = ((), (), s32[]{:S(2)}) async-start(), calls=%async_computation.17 | async-start | bytes 7135232
  1283.0 2382.9 %all-reduce.18.cloned.1.call-start = ((), (), s32[]{:S(2)}) async-start(), calls=%async_computation.18 | async-start | bytes 150994944
  1353.5 44.5 %all-to-all-start.1 = ((bf16[8,96,768]{2,1,0:T(8,128)(2,1)}), bf16[8,96,768]{2,1,0:T(8,128)(2,1)S(1)}, u32[]{:S(2)}, u32[]{:S(2)}) async-start(bf16[8,96,768]{2,1,0:T(8,128)(2,1)} %bitcast.33), calls=%async_computation.3 | async-start | bytes 2359296 | tf_op jit(solution)/shard_map/all_to_all | solution.py:384
  1406.8 74.1 %all-to-all-start.3 = ((bf16[8,96,768]{2,1,0:T(8,128)(2,1)}), bf16[8,96,768]{2,1,0:T(8,128)(2,1)S(1)}, u32[]{:S(2)}, u32[]{:S(2)}) async-start(bf16[8,96,768]{2,1,0:T(8,128)(2,1)} %bitcast.69), calls=%async_computation.6 | async-start | bytes 2359296 | tf_op jit(solution)/shard_map/all_to_all | solution.py:391
  (75 other events, 151.8 us)
Sparse Core Ops, SparseCore 0:
  90.4 32.0 reduce-scatter.3
  124.8 24.1 all-gather.8
  151.3 176.3 all-gather.10
  330.1 174.6 all-gather.12
  507.0 174.6 all-gather.14
  769.1 54.0 all-reduce.13
  906.6 23.4 reduce-scatter.5
  951.2 30.8 reduce-scatter.7
  984.3 17.4 all-gather.16
  1003.8 17.4 all-gather.18
  1283.1 173.8 all-reduce.15
  1461.1 2204.7 all-reduce.17
where the time goes:
time: 3700 us; the launch traced here: 3690 us
  waiting for transfers between devices  2790 us (75%)
  local copies, waits for them, and re-layouts  301 us (8%)
  blocking collectives  292 us (8%)
  matrix products  142 us (4%)
  other arithmetic  127 us (3%)
    unnamed x14, waiting for transfers between devices  2230 us
    unnamed x1, blocking collectives  280 us
    all_gather x1, waiting for transfers between devices, body(): lax.all_gather(expert_up, 'expert', axis=0, tiled=True)  169 us
    all_gather x1, waiting for transfers between devices, body(): lax.all_gather(expert_down, 'expert', axis=0, tiled=True)  169 us
    unnamed x241, local copies, waits for them, and re-layouts  121 us
    all_gather x1, waiting for transfers between devices, body(): lax.all_gather(expert_gate, 'expert', axis=0, tiled=True)  102 us
  transfers between devices with their start and end apart: 16, of which 10 were waited for; matrix products, arithmetic and copies ran while one was open for 11% of the time, Pallas kernels for 0%

commit v1 on v0

v1 whole, which is shorter than its diff:
```python
import jax
import jax.numpy as jnp
from jax import lax
from jax.sharding import PartitionSpec as P

HD = 64
EXPERTS = 16
CAP = 120


EPSILON = 1e-05
ROPE_BASE = 10000.0
MASKED = -1e30


def rms_scale(values):
    return lax.rsqrt(jnp.mean(values * values, axis=-1, keepdims=True) + EPSILON)


def matmul(left_side, right_side):
    return jnp.dot(left_side, right_side, preferred_element_type=jnp.float32)


def matmul_bt(left_side, right_side):
    return lax.dot_general(
        left_side, right_side, (((1,), (1,)), ((), ())), preferred_element_type=jnp.float32
    )


def matmul_at(left_side, right_side):
    return lax.dot_general(
        left_side, right_side, (((0,), (0,)), ((), ())), preferred_element_type=jnp.float32
    )


def silu_value(gate_in):
    return gate_in * jax.nn.sigmoid(gate_in)


def silu_slope(gate_in):
    sigma = jax.nn.sigmoid(gate_in)
    return sigma * (1.0 + gate_in * (1.0 - sigma))


def rotate(values, cos_table, sin_table):
    half_size = HD // 2
    shaped = values.reshape(values.shape[0], -1, HD)
    front_half = shaped[..., :half_size]
    back_half = shaped[..., half_size:]
    cos_wide = cos_table[:, None, :]
    sin_wide = sin_table[:, None, :]
    turned = jnp.concatenate(
        [
            front_half * cos_wide - back_half * sin_wide,
            back_half * cos_wide + front_half * sin_wide,
        ],
        axis=-1,
    )
    return turned.reshape(values.shape)


def block_scores(query, key, sequence_segment, block_index, block_rows, score_scale):
    start_row = block_index * block_rows
    end_row = start_row + block_rows
    q_part = query[start_row:end_row].reshape(block_rows, -1, HD)
    k_part = key[:end_row].reshape(end_row, -1, HD)
    scores = (
        jnp.einsum("qhd,khd->hqk", q_part, k_part, preferred_element_type=jnp.float32) * score_scale
    )
    q_rows = jnp.arange(start_row, end_row, dtype=jnp.int32)
    k_rows = jnp.arange(end_row, dtype=jnp.int32)
    allowed = (sequence_segment[start_row:end_row, None] == sequence_segment[None, :end_row]) & (
        q_rows[:, None] >= k_rows[None, :]
    )
    return (jnp.where(allowed[None], scores, MASKED), q_part, k_part)


def core_swap(values):
    return lax.ppermute(values, "tensor", [(i, i ^ 1) for i in range(4)])


def far_swap(values):
    return lax.ppermute(values, "tensor", [(i, i ^ 2) for i in range(4)])


def exchange(values):
    return lax.all_to_all(values, "expert", split_axis=0, concat_axis=0, tiled=True)


def in_order(bit, own, other, axis=0):
    return jnp.where(
        bit == 0,
        jnp.concatenate([own, other], axis=axis),
        jnp.concatenate([other, own], axis=axis),
    )


def gather_four(bit_low, bit_high, own, axis):
    far = far_swap(own)
    near = core_swap(own)
    far_near = core_swap(far)
    here = in_order(bit_low, own, near, axis)
    there = in_order(bit_low, far, far_near, axis)
    return in_order(bit_high, here, there, axis)


def select(onehot, values):
    return jnp.dot(onehot, values, preferred_element_type=jnp.float32).astype(jnp.bfloat16)


def total_over_tensor(values, bit_low):
    half = values.shape[0] // 2
    kept = lax.dynamic_slice_in_dim(values, bit_low * half, half, 0)
    given = lax.dynamic_slice_in_dim(values, (1 - bit_low) * half, half, 0)
    pair = (kept.astype(jnp.float32) + core_swap(given).astype(jnp.float32)).astype(jnp.bfloat16)
    four = (pair.astype(jnp.float32) + far_swap(pair).astype(jnp.float32)).astype(jnp.bfloat16)
    return in_order(bit_low, four, core_swap(four))


def half_over_tensor(values, bit_low):
    half = values.shape[0] // 2
    kept = lax.dynamic_slice_in_dim(values, bit_low * half, half, 0)
    given = lax.dynamic_slice_in_dim(values, (1 - bit_low) * half, half, 0)
    pair = (kept.astype(jnp.float32) + core_swap(given).astype(jnp.float32)).astype(jnp.bfloat16)
    return pair.astype(jnp.float32) + far_swap(pair).astype(jnp.float32)


def body(
    tokens,
    order,
    lengths,
    routes,
    attn_gain,
    w_query,
    w_key,
    w_value,
    w_out,
    ffn_gain,
    w_router,
    shared_gate,
    shared_up,
    shared_down,
    expert_gate,
    expert_up,
    expert_down,
    cotangent,
):
    row_count, feat_width = tokens.shape
    group_count = lax.axis_size("expert")
    share_rows = row_count // group_count
    half_share = share_rows // 2
    half_rows = row_count // 2
    my_group = lax.axis_index("expert")
    my_tensor = lax.axis_index("tensor")
    bit_low = lax.rem(my_tensor, 2)
    bit_high = my_tensor // 2
    slab_dev = expert_gate.shape[0]
    slab_total = slab_dev * group_count
    replicas = max(1, slab_total // EXPERTS)
    half_slots = slab_dev * CAP // 2
    block_rows = 256
    block_count = row_count // block_rows
    score_scale = HD ** (-0.5)
    row_ids = jnp.arange(row_count, dtype=jnp.int32)
    earlier = (row_ids[:, None] < row_ids[None, :]).astype(jnp.bfloat16)

    local_order = lax.dynamic_slice_in_dim(order, my_group * row_count, row_count, 0)
    groups = jnp.arange(group_count, dtype=jnp.int32)
    dest_group = local_order // row_count
    dest_onehot = (groups[:, None] == dest_group[None, :]).astype(jnp.bfloat16)
    dest_before = matmul(dest_onehot, earlier)
    send_rank = jnp.sum(dest_onehot.astype(jnp.float32) * dest_before, axis=0).astype(jnp.int32)
    send_half = send_rank // half_share
    send_slot = send_half * half_rows + dest_group * half_share + send_rank % half_share
    send_pick = send_slot[None, :] == (
        bit_low * half_rows + jnp.arange(half_rows, dtype=jnp.int32)[:, None]
    )
    send_pick = send_pick.astype(jnp.bfloat16)
    in_tokens = exchange(select(send_pick, tokens))
    in_cot = exchange(select(send_pick, cotangent))

    all_order = order.reshape(group_count, row_count)
    mine = all_order // row_count == my_group
    arrive_rank = matmul(mine.astype(jnp.bfloat16), earlier).astype(jnp.int32)
    arrive_rank = jnp.where(mine, arrive_rank, -1)
    landing = all_order - my_group * row_count
    target = jnp.sum(
        jnp.where(
            arrive_rank[:, None, :] == jnp.arange(share_rows, dtype=jnp.int32)[None, :, None],
            landing[:, None, :],
            0,
        ),
        axis=-1,
    )
    target = target.reshape(group_count, 2, half_share).transpose(1, 0, 2).reshape(2, half_rows)
    target_own = lax.dynamic_index_in_dim(target, bit_low, 0, keepdims=False)
    target_other = lax.dynamic_index_in_dim(target, 1 - bit_low, 0, keepdims=False)
    place_own = (row_ids[:, None] == target_own[None, :]).astype(jnp.bfloat16)
    place_other = (row_ids[:, None] == target_other[None, :]).astype(jnp.bfloat16)

    def place(own):
        other = core_swap(own)
        return (matmul(place_own, own) + matmul(place_other, other)).astype(jnp.bfloat16)

    expert_ids = jnp.arange(EXPERTS, dtype=jnp.int32)
    member_one = expert_ids[:, None] == routes[None, :, 0]
    member_two = expert_ids[:, None] == routes[None, :, 1]
    member = member_one | member_two
    slot_rank = matmul(member.astype(jnp.bfloat16), earlier).astype(jnp.int32)
    slot_rank = jnp.where(member, slot_rank, -1)

    def slots_of(half):
        ranks = jnp.repeat(slot_rank, replicas, axis=0).reshape(group_count, slab_dev, row_count)
        ranks = lax.dynamic_index_in_dim(ranks, half * half_slots // CAP, 1, keepdims=False)
        slot = half * half_slots % CAP + jnp.arange(half_slots, dtype=jnp.int32)
        picked = ranks[:, None, :] == slot[None, :, None]
        return picked.reshape(group_count * half_slots, row_count)

    slots_own = slots_of(bit_low)
    slots_one = slots_own.astype(jnp.bfloat16)

    whole_out = gather_four(bit_low, bit_high, w_out, 0)

    seq_lengths = lengths[0]
    seq_ends = jnp.cumsum(seq_lengths)
    passed = row_ids[:, None] >= seq_ends[None, :]
    sequence_segment = jnp.sum(passed.astype(jnp.int32), axis=1)
    position = row_ids - jnp.sum(jnp.where(passed, seq_lengths[None, :], 0), axis=1)
    half_size = HD // 2
    frequency = ROPE_BASE ** (-jnp.arange(half_size, dtype=jnp.float32) / half_size)
    angles = position.astype(jnp.float32)[:, None] * frequency[None, :]
    cos_table = jnp.cos(angles)
    sin_table = jnp.sin(angles)

    grouped = place(in_tokens)
    grouped_cot = place(in_cot)
    cot_rows = exchange(select(slots_one, grouped_cot))

    resid = grouped.astype(jnp.float32)
    scale_one = rms_scale(resid)
    normed_one = resid * scale_one
    gain_one = attn_gain.astype(jnp.float32)
    hidden_one = (normed_one * gain_one).astype(jnp.bfloat16)
    query = rotate(matmul(hidden_one, w_query), cos_table, sin_table).astype(jnp.bfloat16)
    key = rotate(matmul(hidden_one, w_key), cos_table, sin_table).astype(jnp.bfloat16)
    value = matmul(hidden_one, w_value).astype(jnp.bfloat16)
    block_outputs = []
    log_totals = []
    for block_index in range(block_count):
        scores, q_part, k_part = block_scores(
            query, key, sequence_segment, block_index, block_rows, score_scale
        )
        row_max = jnp.max(scores, axis=-1, keepdims=True)
        log_total = row_max + jnp.log(jnp.sum(jnp.exp(scores - row_max), axis=-1, keepdims=True))
        weights = jnp.exp(scores - log_total).astype(jnp.bfloat16)
        end_row = (block_index + 1) * block_rows
        v_part = value[:end_row].reshape(end_row, -1, HD)
        mixture = jnp.einsum("hqk,khd->qhd", weights, v_part, preferred_element_type=jnp.float32)
        block_outputs.append(mixture.reshape(block_rows, -1))
        log_totals.append(log_total)
    attended = jnp.concatenate(block_outputs, axis=0).astype(jnp.bfloat16)
    whole_attended = gather_four(bit_low, bit_high, attended, 1)
    resid_two = resid + matmul(whole_attended, whole_out)
    scale_two = rms_scale(resid_two)
    normed_two = resid_two * scale_two
    gain_two = ffn_gain.astype(jnp.float32)
    hidden_two = (normed_two * gain_two).astype(jnp.bfloat16)

    hidden_rows = exchange(select(slots_one, hidden_two))
    logits = matmul(hidden_two, w_router)
    picked = routes[:, :, None] == expert_ids[None, None, :]
    chosen = jnp.sum(jnp.where(picked, logits[:, None, :], 0.0), axis=-1)
    raised = jnp.exp(chosen - jnp.max(chosen, axis=-1, keepdims=True))
    gate_weights = raised / jnp.sum(raised, axis=-1, keepdims=True)
    dest_slab = jnp.arange(group_count, dtype=jnp.int32) * slab_dev + bit_low * half_slots // CAP
    dest_expert = dest_slab // replicas
    first_here = routes[None, :, 0] == dest_expert[:, None]
    gate_of = jnp.where(first_here, gate_weights[None, :, 0], gate_weights[None, :, 1])
    slots_cube = slots_own.reshape(group_count, half_slots, row_count)
    gate_slots = jnp.sum(jnp.where(slots_cube, gate_of[:, None, :], 0.0), axis=-1)
    gate_rows = exchange(gate_slots).reshape(group_count * half_slots, 1)

    def both(own):
        return in_order(bit_low, own[None], core_swap(own)[None])

    gate_shared = matmul(hidden_two, shared_gate)
    up_shared = matmul(hidden_two, shared_up)
    act_shared = silu_value(gate_shared)
    shared_mid = (act_shared * up_shared).astype(jnp.bfloat16)
    shared_out = matmul(shared_mid, shared_down)
    d_mid_shared = matmul_bt(grouped_cot, shared_down)
    g_shared_down = matmul_at(shared_mid, grouped_cot)
    d_up_shared = (d_mid_shared * act_shared).astype(jnp.bfloat16)
    d_gate_shared = (d_mid_shared * up_shared * silu_slope(gate_shared)).astype(jnp.bfloat16)
    g_shared_gate = matmul_at(hidden_two, d_gate_shared)
    g_shared_up = matmul_at(hidden_two, d_up_shared)
    d_hidden_shared = matmul_bt(d_gate_shared, shared_gate) + matmul_bt(d_up_shared, shared_up)

    rows_h = both(hidden_rows)
    rows_c = both(cot_rows)
    rows_g = both(gate_rows)
    if slab_dev == 2:
        gate_w, up_w, down_w = (expert_gate, expert_up, expert_down)
    else:
        rows_h = rows_h.reshape(1, -1, feat_width)
        rows_c = rows_c.reshape(1, -1, feat_width)
        rows_g = rows_g.reshape(1, -1, 1)
        gate_w, up_w, down_w = (expert_gate, expert_up, expert_down)
    gate_lin = jnp.einsum("kci,kif->kcf", rows_h, gate_w, preferred_element_type=jnp.float32)
    up_lin = jnp.einsum("kci,kif->kcf", rows_h, up_w, preferred_element_type=jnp.float32)
    act = silu_value(gate_lin)
    mid32 = act * up_lin
    mid = mid32.astype(jnp.bfloat16)
    out_rows = jnp.einsum("kcf,kfd->kcd", mid, down_w, preferred_element_type=jnp.float32)
    out_rows = (out_rows * rows_g).astype(jnp.bfloat16)
    d_raw = jnp.einsum("kcd,kfd->kcf", rows_c, down_w, preferred_element_type=jnp.float32)
    d_gate_rows = jnp.sum(d_raw * mid.astype(jnp.float32), axis=-1)
    d_act = d_raw * rows_g
    d_up = (d_act * act).astype(jnp.bfloat16)
    d_gate = (d_act * up_lin * silu_slope(gate_lin)).astype(jnp.bfloat16)
    back_rows = jnp.einsum("kcf,kif->kci", d_gate, gate_w, preferred_element_type=jnp.float32)
    back_rows = back_rows + jnp.einsum(
        "kcf,kif->kci", d_up, up_w, preferred_element_type=jnp.float32
    )
    back_rows = back_rows.astype(jnp.bfloat16)
    mid_g = (mid.astype(jnp.float32) * rows_g).astype(jnp.bfloat16)
    g_expert_gate = jnp.einsum("kci,kcf->kif", rows_h, d_gate, preferred_element_type=jnp.float32)
    g_expert_up = jnp.einsum("kci,kcf->kif", rows_h, d_up, preferred_element_type=jnp.float32)
    g_expert_down = jnp.einsum("kcf,kcd->kfd", mid_g, rows_c, preferred_element_type=jnp.float32)

    def give_back(values, dtype):
        values = values.reshape((2, group_count * half_slots) + values.shape[2:])
        kept = lax.dynamic_index_in_dim(values, bit_low, 0, keepdims=False)
        given = lax.dynamic_index_in_dim(values, 1 - bit_low, 0, keepdims=False)
        total = kept.astype(jnp.float32) + core_swap(given).astype(jnp.float32)
        return exchange(total.astype(dtype))

    back_own = give_back(back_rows, jnp.bfloat16)
    dg_own = give_back(d_gate_rows[..., None].reshape(2, -1, 1), jnp.float32)
    out_own = give_back(out_rows, jnp.bfloat16)

    d_hidden_part = (matmul_at(slots_one, back_own) + d_hidden_shared).astype(jnp.bfloat16)
    d_hidden = total_over_tensor(d_hidden_part, bit_low).astype(jnp.float32)
    dg_cube = dg_own.reshape(group_count, half_slots, 1)
    dg_of = jnp.sum(jnp.where(slots_cube, dg_cube, 0.0), axis=1)
    dg_one = jnp.sum(jnp.where(first_here, dg_of, 0.0), axis=0)
    dg_two = jnp.sum(jnp.where(routes[None, :, 1] == dest_expert[:, None], dg_of, 0.0), axis=0)
    dg_part = jnp.stack([dg_one, dg_two], axis=0)
    dg_part = dg_part + core_swap(dg_part)
    dg_part = dg_part + far_swap(dg_part)
    d_gates = dg_part.T
    d_chosen = gate_weights * (d_gates - jnp.sum(gate_weights * d_gates, axis=-1, keepdims=True))
    d_logits = jnp.sum(jnp.where(picked, d_chosen[:, :, None], 0.0), axis=1).astype(jnp.bfloat16)
    g_router = matmul_at(hidden_two, d_logits)
    d_two = d_hidden + matmul_bt(d_logits, w_router)
    g_ffn_gain = jnp.sum(d_two * normed_two, axis=0)
    e_two = d_two * gain_two
    grad_out = grouped_cot.astype(jnp.float32)
    d_resid = grad_out + scale_two * (
        e_two - normed_two * jnp.mean(e_two * normed_two, axis=-1, keepdims=True)
    )
    d_proj = d_resid.astype(jnp.bfloat16)
    g_out = matmul_at(attended, d_proj)
    d_attended = matmul_bt(d_proj, w_out).astype(jnp.bfloat16)
    query_grads = []
    key_grad = jnp.zeros((row_count, query.shape[1]), jnp.float32)
    value_grad = jnp.zeros((row_count, query.shape[1]), jnp.float32)
    for block_index in range(block_count):
        scores, q_part, k_part = block_scores(
            query, key, sequence_segment, block_index, block_rows, score_scale
        )
        weights = jnp.exp(scores - log_totals[block_index])
        start_row = block_index * block_rows
        end_row = start_row + block_rows
        grad_part = d_attended[start_row:end_row].reshape(block_rows, -1, HD)
        v_part = value[:end_row].reshape(end_row, -1, HD)
        d_weights = jnp.einsum(
            "qhd,khd->hqk", grad_part, v_part, preferred_element_type=jnp.float32
        )
        row_inner = jnp.sum(weights * d_weights, axis=-1, keepdims=True)
        d_scores = (weights * (d_weights - row_inner)).astype(jnp.bfloat16)
        query_grads.append(
            (
                jnp.einsum("hqk,khd->qhd", d_scores, k_part, preferred_element_type=jnp.float32)
                * score_scale
            ).reshape(block_rows, -1)
        )
        key_term = (
            jnp.einsum("hqk,qhd->khd", d_scores, q_part, preferred_element_type=jnp.float32)
            * score_scale
        )
        key_grad = key_grad.at[:end_row].add(key_term.reshape(end_row, -1))
        value_term = jnp.einsum(
            "hqk,qhd->khd",
            weights.astype(jnp.bfloat16),
            grad_part,
            preferred_element_type=jnp.float32,
        )
        value_grad = value_grad.at[:end_row].add(value_term.reshape(end_row, -1))
    d_query = rotate(jnp.concatenate(query_grads, axis=0), cos_table, -sin_table).astype(
        jnp.bfloat16
    )
    d_key = rotate(key_grad, cos_table, -sin_table).astype(jnp.bfloat16)
    d_value = value_grad.astype(jnp.bfloat16)
    g_query = matmul_at(hidden_one, d_query)
    g_key = matmul_at(hidden_one, d_key)
    g_value = matmul_at(hidden_one, d_value)
    d_one = matmul_bt(d_query, w_query) + matmul_bt(d_key, w_key) + matmul_bt(d_value, w_value)
    d_one = total_over_tensor(d_one.astype(jnp.bfloat16), bit_low).astype(jnp.float32)
    g_attn_gain = jnp.sum(d_one * normed_one, axis=0)
    e_one = d_one * gain_one
    d_group = (
        d_resid
        + scale_one * (e_one - normed_one * jnp.mean(e_one * normed_one, axis=-1, keepdims=True))
    ).astype(jnp.bfloat16)

    ffn_part = (matmul_at(slots_one, out_own) + shared_out).astype(jnp.bfloat16)
    ffn_sum = total_over_tensor(ffn_part, bit_low).astype(jnp.float32)
    output_group = (resid_two + ffn_sum).astype(jnp.bfloat16)
    unsend = (
        send_slot[:, None] == jnp.arange(row_count, dtype=jnp.int32)[None, :]
    ).astype(jnp.bfloat16)

    def give_rows(values):
        own = exchange(matmul_at(place_own, values).astype(jnp.bfloat16))
        return select(unsend, in_order(bit_low, own, core_swap(own)))

    output = give_rows(output_group)
    d_tokens = give_rows(d_group)

    def total_over_groups(members):
        wide = jnp.concatenate([m.astype(jnp.bfloat16) for m in members], axis=0)
        return lax.psum(wide, "expert").astype(jnp.float32)

    hidden_s = shared_gate.shape[1]
    early = total_over_groups([g_shared_gate, g_shared_up])
    g_shared_gate, g_shared_up = early[:feat_width], early[feat_width:]
    gains = jnp.stack([g_ffn_gain, g_attn_gain], axis=0)
    late_down = total_over_groups([g_shared_down, g_out, g_router.T, gains])
    g_shared_down = late_down[:hidden_s]
    head_rows = w_out.shape[0]
    g_out = late_down[hidden_s : hidden_s + head_rows]
    at = hidden_s + head_rows
    g_router = late_down[at : at + EXPERTS].T
    g_ffn_gain = late_down[at + EXPERTS]
    g_attn_gain = late_down[at + EXPERTS + 1]
    late = total_over_groups([g_query, g_key, g_value])
    g_query = late[:feat_width]
    g_key = late[feat_width : 2 * feat_width]
    g_value = late[2 * feat_width :]
    return (
        output,
        d_tokens,
        g_attn_gain,
        g_query,
        g_key,
        g_value,
        g_out,
        g_ffn_gain,
        g_router,
        g_shared_gate,
        g_shared_up,
        g_shared_down,
        g_expert_gate,
        g_expert_up,
        g_expert_down,
    )


def solution(mesh):
    return jax.shard_map(
        body,
        mesh=mesh,
        in_specs=(
            P("expert", None),
            P(),
            P("expert", None),
            P("expert", None),
            P(),
            P(None, "tensor"),
            P(None, "tensor"),
            P(None, "tensor"),
            P("tensor", None),
            P(),
            P(),
            P(None, "tensor"),
            P(None, "tensor"),
            P("tensor", None),
            P("expert", None, "tensor"),
            P("expert", None, "tensor"),
            P("expert", "tensor", None),
            P("expert", None),
        ),
        out_specs=(
            P("expert", None),
            P("expert", None),
            P(),
            P(None, "tensor"),
            P(None, "tensor"),
            P(None, "tensor"),
            P("tensor", None),
            P(),
            P(),
            P(None, "tensor"),
            P(None, "tensor"),
            P("tensor", None),
            P("expert", None, "tensor"),
            P("expert", None, "tensor"),
            P("expert", "tensor", None),
        ),
        check_vma=False,
    )
```

time: 3700 us -> 564 us (0.15)
  waiting for transfers between devices: 2790 us -> 254 us
  blocking collectives: 292 us -> 9.94 us
  local copies, waits for them, and re-layouts: 301 us -> 43.5 us
  other arithmetic: 127 us -> 51.5 us
    unnamed x14 -> x1, waiting for transfers between devices: 2230 us -> 0.02 us
    all_gather x6 -> x0, waiting for transfers between devices: 439 us -> none  [the longest x1 169 us: body(): lax.all_gather(expert_up, 'expert', axis=0, tiled=True)]
    unnamed x1 -> x0, blocking collectives: 280 us -> none
    unnamed x241 -> x225, local copies, waits for them, and re-layouts: 121 us -> 12.8 us
    psum x1, waiting for transfers between devices: 0.02 us -> 80.6 us  [total_over_groups(): return lax.psum(wide, 'expert').astype(jnp.float32)]
    all_to_all x4 -> x9, waiting for transfers between devices: 72.5 us -> 151 us  [exchange(): lax.all_to_all(values, 'expert', split_axis=0, concat_axis=0, tiled=True)]
    gather x15 -> x0, local copies, waits for them, and re-layouts: 70.5 us -> none  [the longest x1 9.53 us: body(): back_pad[index_of_slot].reshape(row_count, 2, feat_width)]
    concatenate x2 -> x3, other arithmetic: 64.4 us -> 4.15 us  [the longest x2 2.32 us: total_over_groups(): wide = jnp.concatenate([m.astype(jnp.bfloat16) for m in members], axis=0)]
  transfers between devices with their start and end apart: 16 -> 37, of which waited for: 10 -> 17; matrix products, arithmetic and copies ran while one was open for 11% -> 31% of each run, Pallas kernels for 0% -> 0%
where the time goes in v1:
time: 564 us; the launch traced here: 558 us
  waiting for transfers between devices  254 us (45%)
  matrix products  130 us (23%)
  starting transfers between devices  52.6 us (9%)
  other arithmetic  51.5 us (9%)
  local copies, waits for them, and re-layouts  43.5 us (8%)
  between operations  16.4 us (3%)
  blocking collectives  9.94 us (2%)
    all_to_all x9, waiting for transfers between devices, exchange(): lax.all_to_all(values, 'expert', split_axis=0, concat_axis=0, tiled=True)  151 us
    psum x1, waiting for transfers between devices, total_over_groups(): return lax.psum(wide, 'expert').astype(jnp.float32)  80.6 us
    all_to_all x9, starting transfers between devices, exchange(): lax.all_to_all(values, 'expert', split_axis=0, concat_axis=0, tiled=True)  40.9 us
    dot_general x12, matrix products, matmul_at(): lax.dot_general(left_side, right_side, (((0,), (0,)), ((), ())), preferre...  27.5 us
    dot_general x15, matrix products, matmul(): return jnp.dot(left_side, right_side, preferred_element_type=jnp.float32)  18.6 us
    dot_general x6, matrix products, select(): jnp.dot(onehot, values, preferred_element_type=jnp.float32)  17.8 us
    ppermute x6, waiting for transfers between devices, far_swap(): return lax.ppermute(values, 'tensor', [(i, i ^ 2) for i in range(4)])  17.1 us
    unnamed x225, local copies, waits for them, and re-layouts  12.8 us
  transfers between devices with their start and end apart: 37, of which 17 were waited for; matrix products, arithmetic and copies ran while one was open for 31% of the time, Pallas kernels for 0%

profile of v1, /device:TPU:0, one launch (start us, length us, event | category | flops | bytes accessed | tf_op | source)
XLA Modules:
  0.0 558.1 jit_solution(2995853752026167544)
XLA Ops:
  7.2 3.0 collective-permute-start.5
  12.1 2.8 fusion.49
  14.9 5.8 %all-to-all-start = ((bf16[8,48,768]{2,1,0:T(8,128)(2,1)}), bf16[8,48,768]{2,1,0:T(8,128)(2,1)S(1)}, u32[]{:S(2)}, u32[]{:S(2)}) async-start(bf16[8,48,768]{2,1,0:T(8,128)(2,1)} %bitcast.1), calls=%async_computation | async-start | bytes 1179648 | tf_op jit(solution)/shard_map/all_to_all | solution.py:87
  25.1 2.8 fusion.52
  27.8 9.4 %all-to-all-done = bf16[8,48,768]{2,1,0:T(8,128)(2,1)S(1)} async-done(((bf16[8,48,768]{2,1,0:T(8,128)(2,1)}), bf16[8,48,768]{2,1,0:T(8,128)(2,1)S(1)}, u32[]{:S(2)}, u32[]{:S(2)}) %all-to-all-start) | async-done | bytes 589856 | tf_op jit(solution)/shard_map/all_to_all | solution.py:87
  37.2 4.4 all-to-all-start.5
  70.8 3.6 collective-permute-done.2
  80.7 2.8 multiply_reduce_fusion.3
  83.5 2.9 multiply_convert_fusion.5
  86.4 3.9 convolution_convert_fusion.1
  90.3 5.9 %all-to-all-start.1 = ((bf16[8,120,768]{2,1,0:T(8,128)(2,1)}), bf16[8,120,768]{2,1,0:T(8,128)(2,1)}, u32[]{:S(2)}, u32[]{:S(2)}) async-start(bf16[8,120,768]{2,1,0:T(8,128)(2,1)} %bitcast.207), calls=%async_computation.1 | async-start | bytes 2949120 | tf_op jit(solution)/shard_map/all_to_all | solution.py:87
  102.9 29.0 %all-to-all-done.1 = bf16[8,120,768]{2,1,0:T(8,128)(2,1)} async-done(((bf16[8,120,768]{2,1,0:T(8,128)(2,1)}), bf16[8,120,768]{2,1,0:T(8,128)(2,1)}, u32[]{:S(2)}, u32[]{:S(2)}) %all-to-all-start.1) | async-done | bytes 1474592 | tf_op jit(solution)/shard_map/all_to_all | solution.py:87
  131.9 4.3 all-to-all-start.6
  139.2 31.7 %all-to-all-done.6 = bf16[8,120,768]{2,1,0:T(8,128)(2,1)} async-done(((bf16[8,120,768]{2,1,0:T(8,128)(2,1)}), bf16[8,120,768]{2,1,0:T(8,128)(2,1)}, u32[]{:S(2)}, u32[]{:S(2)}) %all-to-all-start.6) | async-done | bytes 1474592 | tf_op jit(solution)/shard_map/all_to_all | solution.py:87
  171.6 4.7 fusion.198
  176.4 5.1 fusion.197
  181.6 8.8 %fusion.4 = (f32[2,960]{1,0:T(2,128)S(1)}, bf16[2,960,512]{2,1,0:T(8,128)(2,1)}, f32[2,960,512]{2,1,0:T(8,128)}) fusion(f32[2,960,512]{2,1,0:T(8,128)S(1)} %fusion.197, f32[2,960,512]{2,1,0:T(8,128)S(1)} %fusion.198, bf16[2,512,768]{2,1,0:T(8,128)(2,1)S(1)} %copy-done, bf16[1,960,768]{2,1,0:T(8,128)(2,1)S(1)} %bitcast.240, ...), kind=kOutput, calls=%fused_computation.10 | convolution fusion | flops 1523218560 | bytes 18292224 | tf_op jit(solution)/shard_map/kcd,kfd->kcf/dot_general | solution.py:316
  193.7 3.9 all-to-all-start.8
  199.1 5.0 all-to-all-done.8
  206.2 9.9 %all_to_all.108 = f32[8,1,120]{2,1,0:T(1,128)} all-to-all(f32[8,1,120]{2,1,0:T(1,128)S(1)} %bitcast.236), channel_id=1, replica_groups=mesh['expert'=8,'tensor'=4] {'expert'}, dimensions={0} | all-to-all | bytes 7680 | tf_op jit(solution)/shard_map/all_to_all | solution.py:87
  222.1 5.6 multiply_convert_fusion.1
  230.3 3.3 add_convert_fusion
  236.7 3.2 collective-permute-done.16
  239.9 3.3 fusion.13
  243.2 4.3 all-to-all-start.7
  254.9 2.6 multiply_convert_fusion.7
  257.5 3.0 convolution_convert_fusion.2
  264.3 18.9 %all-to-all-done.7 = bf16[8,120,768]{2,1,0:T(8,128)(2,1)} async-done(((bf16[8,120,768]{2,1,0:T(8,128)(2,1)}), bf16[8,120,768]{2,1,0:T(8,128)(2,1)}, u32[]{:S(2)}, u32[]{:S(2)}) %all-to-all-start.7) | async-done | bytes 1474592 | tf_op jit(solution)/shard_map/all_to_all | solution.py:87
  283.2 4.3 all-to-all-start.3
  287.8 3.0 convolution_convert_fusion.4
  294.7 3.0 fusion.23
  298.4 2.9 convolution_convert_fusion.3
  305.1 17.3 %all-to-all-done.3 = bf16[8,120,768]{2,1,0:T(8,128)(2,1)} async-done(((bf16[8,120,768]{2,1,0:T(8,128)(2,1)}), bf16[8,120,768]{2,1,0:T(8,128)(2,1)}, u32[]{:S(2)}, u32[]{:S(2)}) %all-to-all-start.3) | async-done | bytes 1474592 | tf_op jit(solution)/shard_map/all_to_all | solution.py:87
  322.4 3.7 fusion.24
  329.9 2.7 multiply_reduce_fusion
  357.4 12.8 %collective-permute-done.24 = bf16[384,768]{0,1:T(8,128)(2,1)S(1)} collective-permute-done((bf16[384,768]{0,1:T(8,128)(2,1)S(1)}, bf16[384,768]{0,1:T(8,128)(2,1)S(1)}, u32[]{:S(2)}, u32[]{:S(2)}) %collective-permute-start.24) | collective-permute-done | bytes 589856 | tf_op jit(solution)/shard_map/ppermute | solution.py:83
  373.4 4.6 concatenate.181
  378.8 4.0 convolution_convert_fusion.6
  382.7 4.2 all-to-all-start.4
  387.0 3.7 convolution_convert_fusion.5
  390.7 29.3 %all-to-all-done.4 = bf16[8,48,768]{2,1,0:T(8,128)(2,1)} async-done(((bf16[8,48,768]{2,1,0:T(8,128)(2,1)}), bf16[8,48,768]{2,1,0:T(8,128)(2,1)}, u32[]{:S(2)}, u32[]{:S(2)}) %all-to-all-start.4) | async-done | bytes 589856 | tf_op jit(solution)/shard_map/all_to_all | solution.py:87
  420.0 3.8 all-to-all-start.9
  423.8 7.1 %fusion.195 = f32[2,768,512]{2,1,0:T(8,128)} fusion(bf16[2,960,512]{2,1,0:T(8,128)(2,1)} %copy-done.11, bf16[1,960,768]{2,1,0:T(8,128)(2,1)} %bitcast.21, bf16[1,960,768]{2,1,0:T(8,128)(2,1)} %bitcast.19, pred[]{:T(512)S(6)} %eq.140), kind=kOutput, calls=%fused_computation.353 | convolution fusion | flops 1514373120 | bytes 8060929 | tf_op jit(solution)/shard_map/kci,kcf->kif/dot_general | solution.py:328
  430.9 5.6 fusion.30
  438.1 10.8 %all-to-all-done.9 = bf16[8,48,768]{2,1,0:T(8,128)(2,1)S(1)} async-done(((bf16[8,48,768]{2,1,0:T(8,128)(2,1)}), bf16[8,48,768]{2,1,0:T(8,128)(2,1)S(1)}, u32[]{:S(2)}, u32[]{:S(2)}) %all-to-all-start.9) | async-done | bytes 589856 | tf_op jit(solution)/shard_map/all_to_all | solution.py:87
  450.0 6.3 %fusion.196 = f32[2,768,512]{2,1,0:T(8,128)} fusion(bf16[2,960,512]{2,1,0:T(8,128)(2,1)S(1)} %copy-done.10, bf16[1,960,768]{2,1,0:T(8,128)(2,1)} %bitcast.21, bf16[1,960,768]{2,1,0:T(8,128)(2,1)} %bitcast.19, pred[]{:T(512)S(6)} %eq.140), kind=kOutput, calls=%fused_computation.354 | convolution fusion | flops 1514373120 | bytes 8060929 | tf_op jit(solution)/shard_map/kci,kcf->kif/dot_general | solution.py:327
  456.3 3.6 fusion.39
  462.2 80.6 %all-reduce.5.cloned.1.call-done = (bf16[722,768]{1,0:T(8,128)(2,1)}, bf16[2304,192]{0,1:T(8,128)(2,1)}, bf16[1536,512]{1,0:T(8,128)(2,1)}) async-done(((bf16[722,768]{1,0:T(8,128)(2,1)}, bf16[2304,192]{0,1:T(8,128)(2,1)}, bf16[1536,512]{1,0:T(8,128)(2,1)}), (bf16[722,768]{1,0:T(8,128)(2,1)}, bf16[2304,192]{0,1:T(8,128)(2,1)}, bf16[1536,512]{1,0:T(8,128)(2,1)})) %all-reduce.5.cloned.1.call-update) | async-done | bytes 3566608 | tf_op jit(solution)/shard_map/psum | solution.py:433
  (446 shorter events, 134.4 us)
Async XLA Ops:
  7.2 174.4 %copy-start = (bf16[2,512,768]{2,1,0:T(8,128)(2,1)S(1)}, bf16[2,512,768]{2,1,0:T(8,128)(2,1)}, u32[]{:S(2)}) copy-start(bf16[2,512,768]{2,1,0:T(8,128)(2,1)} %param.50) | copy-start | bytes 4718596
  7.2 58.2 %collective-permute-start.5 = (bf16[192,768]{1,0:T(8,128)(2,1)}, bf16[192,768]{1,0:T(8,128)(2,1)}, u32[]{:S(2)}, u32[]{:S(2)}) collective-permute-start(bf16[192,768]{1,0:T(8,128)(2,1)} %param.42), channel_id=1, source_target_pairs={{0,2},{1,3},{2,0},{3,1},{4,6},{5,7},{6,4},{7,5},{8,10},{9,11},{10,... | collective-permute-start | bytes 884744 | tf_op jit(solution)/shard_map/ppermute | solution.py:83
  10.2 64.2 %collective-permute-start.4 = (bf16[192,768]{1,0:T(8,128)(2,1)}, bf16[192,768]{1,0:T(8,128)(2,1)}, u32[]{:S(2)}, u32[]{:S(2)}) collective-permute-start(bf16[192,768]{1,0:T(8,128)(2,1)} %param.42), channel_id=1, source_target_pairs={{0,1},{1,0},{2,3},{3,2},{4,5},{5,4},{6,7},{7,6},{8,9},{9,8},{10,11... | collective-permute-start | bytes 884744 | tf_op jit(solution)/shard_map/ppermute | solution.py:79
  14.9 22.4 %all-to-all-start = ((bf16[8,48,768]{2,1,0:T(8,128)(2,1)}), bf16[8,48,768]{2,1,0:T(8,128)(2,1)S(1)}, u32[]{:S(2)}, u32[]{:S(2)}) async-start(bf16[8,48,768]{2,1,0:T(8,128)(2,1)} %bitcast.1), calls=%async_computation | async-start | bytes 1179648 | tf_op jit(solution)/shard_map/all_to_all | solution.py:87
  21.8 24.7 %copy-start.95 = (f32[768]{0:T(1024)}, f32[768]{0:T(1024)S(1)}, u32[]{:S(2)}) copy-start(f32[768]{0:T(1024)S(1)} %convert_element_type.307) | copy-start | bytes 9220
  22.5 40.6 %copy-start.82 = (s32[768]{0:T(1024)}, s32[768]{0:T(1024)S(1)}, u32[]{:S(2)}) copy-start(s32[768]{0:T(1024)S(1)} %get-tuple-element.115) | copy-start | bytes 9220
  22.5 20.3 %copy-start.92 = (s32[384]{0:T(512)}, s32[384]{0:T(512)S(1)}, u32[]{:S(2)}) copy-start(s32[384]{0:T(512)S(1)} %get-tuple-element.118) | copy-start | bytes 4612
  22.5 21.2 %copy-start.90 = (s32[384]{0:T(512)}, s32[384]{0:T(512)S(1)}, u32[]{:S(2)}) copy-start(s32[384]{0:T(512)S(1)} %get-tuple-element.117) | copy-start | bytes 4612
  37.2 53.1 %all-to-all-start.5 = ((bf16[8,48,768]{2,1,0:T(8,128)(2,1)}), bf16[8,48,768]{2,1,0:T(8,128)(2,1)}, u32[]{:S(2)}, u32[]{:S(2)}) async-start(bf16[8,48,768]{2,1,0:T(8,128)(2,1)} %bitcast.30), calls=%async_computation.5 | async-start | bytes 1179648 | tf_op jit(solution)/shard_map/all_to_all | solution.py:87
  41.6 2.1 collective-permute-start
  62.6 11.8 %collective-permute-start.2 = (bf16[768,192]{1,0:T(8,128)(2,1)}, bf16[768,192]{1,0:T(8,128)(2,1)}, u32[]{:S(2)}, u32[]{:S(2)}) collective-permute-start(bf16[768,192]{1,0:T(8,128)(2,1)} %pad_maximum_fusion.3), channel_id=1, source_target_pairs={{0,2},{1,3},{2,0},{3,1},{4,6},{5,7},{6,4},{7,5},{8,10},{9,11},{10,... | collective-permute-start | bytes 884744 | tf_op jit(solution)/shard_map/ppermute | solution.py:83
  65.4 10.4 %collective-permute-start.6 = (bf16[192,768]{1,0:T(8,128)(2,1)}, bf16[192,768]{1,0:T(8,128)(2,1)}, u32[]{:S(2)}, u32[]{:S(2)}) collective-permute-start(bf16[192,768]{1,0:T(8,128)(2,1)} %collective-permute-done.5), channel_id=1, source_target_pairs={{0,1},{1,0},{2,3},{3,2},{4,5},{5,4},{6,7},{7,6},{8,9},{9,8},{10,11... | collective-permute-start | bytes 884744 | tf_op jit(solution)/shard_map/ppermute | solution.py:79
  67.1 10.3 %collective-permute-start.1 = (bf16[768,192]{1,0:T(8,128)(2,1)}, bf16[768,192]{1,0:T(8,128)(2,1)}, u32[]{:S(2)}, u32[]{:S(2)}) collective-permute-start(bf16[768,192]{1,0:T(8,128)(2,1)} %pad_maximum_fusion.3), channel_id=1, source_target_pairs={{0,1},{1,0},{2,3},{3,2},{4,5},{5,4},{6,7},{7,6},{8,9},{9,8},{10,11... | collective-permute-start | bytes 884744 | tf_op jit(solution)/shard_map/ppermute | solution.py:79
  68.1 15.4 %copy-start.78 = (f32[768]{0:T(1024)}, f32[768]{0:T(1024)S(1)}, u32[]{:S(2)}) copy-start(f32[768]{0:T(1024)S(1)} %convert_element_type.317) | copy-start | bytes 9220
  70.8 15.6 %copy-start.57 = (pred[960,768]{1,0:T(32,128)(4,1)}, pred[960,768]{1,0:T(32,128)(4,1)S(1)}, u32[]{:S(2)}) copy-start(pred[960,768]{1,0:T(32,128)(4,1)S(1)} %bitcast_compare_fusion) | copy-start | bytes 2211844
  74.4 4.6 collective-permute-start.3
  90.3 41.6 %all-to-all-start.1 = ((bf16[8,120,768]{2,1,0:T(8,128)(2,1)}), bf16[8,120,768]{2,1,0:T(8,128)(2,1)}, u32[]{:S(2)}, u32[]{:S(2)}) async-start(bf16[8,120,768]{2,1,0:T(8,128)(2,1)} %bitcast.207), calls=%async_computation.1 | async-start | bytes 2949120 | tf_op jit(solution)/shard_map/all_to_all | solution.py:87
  96.3 2.3 collective-permute-start.14
  131.9 39.0 %all-to-all-start.6 = ((bf16[8,120,768]{2,1,0:T(8,128)(2,1)}), bf16[8,120,768]{2,1,0:T(8,128)(2,1)}, u32[]{:S(2)}, u32[]{:S(2)}) async-start(bf16[8,120,768]{2,1,0:T(8,128)(2,1)} %bitcast.208), calls=%async_computation.6 | async-start | bytes 2949120 | tf_op jit(solution)/shard_map/all_to_all | solution.py:87
  136.2 34.8 %collective-permute-start.7 = (bf16[960,768]{1,0:T(8,128)(2,1)}, bf16[960,768]{1,0:T(8,128)(2,1)}, u32[]{:S(2)}, u32[]{:S(2)}) collective-permute-start(bf16[960,768]{1,0:T(8,128)(2,1)} %bitcast.20), channel_id=1, source_target_pairs={{0,1},{1,0},{2,3},{3,2},{4,5},{5,4},{6,7},{7,6},{8,9},{9,8},{10,11... | collective-permute-start | bytes 4423688 | tf_op jit(solution)/shard_map/ppermute | solution.py:79
  171.0 10.5 %collective-permute-start.15 = (bf16[960,768]{1,0:T(8,128)(2,1)}, bf16[960,768]{1,0:T(8,128)(2,1)S(1)}, u32[]{:S(2)}, u32[]{:S(2)}) collective-permute-start(bf16[960,768]{1,0:T(8,128)(2,1)} %bitcast.34), channel_id=1, source_target_pairs={{0,1},{1,0},{2,3},{3,2},{4,5},{5,4},{6,7},{7,6},{8,9},{9,8},{10,11... | collective-permute-start | bytes 4423688 | tf_op jit(solution)/shard_map/ppermute | solution.py:79
  190.4 1.4 collective-permute-start.20
  193.7 10.3 %all-to-all-start.8 = ((f32[8,120,1]{1,2,0:T(1,128)}), f32[8,120,1]{1,2,0:T(1,128)}, u32[]{:S(2)}, u32[]{:S(2)}) async-start(f32[8,120,1]{1,2,0:T(1,128)} %all_to_all.93), calls=%async_computation.8 | async-start | bytes 8192 | tf_op jit(solution)/shard_map/all_to_all | solution.py:87
  217.5 3.8 collective-permute-start.8
  236.2 3.7 collective-permute-start.16
  243.2 40.0 %all-to-all-start.7 = ((bf16[8,120,768]{2,1,0:T(8,128)(2,1)}), bf16[8,120,768]{2,1,0:T(8,128)(2,1)}, u32[]{:S(2)}, u32[]{:S(2)}) async-start(bf16[8,120,768]{2,1,0:T(8,128)(2,1)} %bitcast.196), calls=%async_computation.7 | async-start | bytes 2949120 | tf_op jit(solution)/shard_map/all_to_all | solution.py:87
  251.8 10.9 %collective-permute-start.9 = (bf16[960,768]{1,0:T(8,128)(2,1)S(1)}, bf16[960,768]{1,0:T(8,128)(2,1)S(1)}, u32[]{:S(2)}, u32[]{:S(2)}) collective-permute-start(bf16[960,768]{1,0:T(8,128)(2,1)S(1)} %dynamic-slice_bitcast_fusion.1), channel_id=1, source_target_pairs={{0,1},{1,0},{2,3},{3,2},{4,5},{5,4},{6,7},{7,6},{8,9},{9,8},{10,11... | collective-permute-start | bytes 4423688 | tf_op jit(solution)/shard_map/ppermute | solution.py:79
  283.2 39.2 %all-to-all-start.3 = ((bf16[8,120,768]{2,1,0:T(8,128)(2,1)}), bf16[8,120,768]{2,1,0:T(8,128)(2,1)}, u32[]{:S(2)}, u32[]{:S(2)}) async-start(bf16[8,120,768]{2,1,0:T(8,128)(2,1)} %bitcast.26), calls=%async_computation.3 | async-start | bytes 2949120 | tf_op jit(solution)/shard_map/all_to_all | solution.py:87
  287.5 255.2 %all-reduce.5.cloned.1.call-start = ((), (), s32[]{:S(2)}) async-start(), calls=%async_computation.10 | async-start | bytes 7151616 | tf_op jit(solution)/shard_map/psum | solution.py:433
  297.8 4.2 collective-permute-start.17
  297.9 3.5 collective-permute-start.21
  301.4 3.7 collective-permute-start.22
  302.9 23.4 %collective-permute-start.18 = (bf16[384,768]{0,1:T(8,128)(2,1)}, bf16[384,768]{0,1:T(8,128)(2,1)}, u32[]{:S(2)}, u32[]{:S(2)}) collective-permute-start(bf16[384,768]{0,1:T(8,128)(2,1)} %add_convert_fusion.9), channel_id=1, source_target_pairs={{0,2},{1,3},{2,0},{3,1},{4,6},{5,7},{6,4},{7,5},{8,10},{9,11},{10,... | collective-permute-start | bytes 1769480 | tf_op jit(solution)/shard_map/ppermute | solution.py:83
  326.2 2.1 collective-permute-start.10
  327.7 2.2 collective-permute-start.19
  328.5 24.8 %collective-permute-start.11 = (bf16[384,768]{0,1:T(8,128)(2,1)S(1)}, bf16[384,768]{0,1:T(8,128)(2,1)S(1)}, u32[]{:S(2)}, u32[]{:S(2)}) collective-permute-start(bf16[384,768]{0,1:T(8,128)(2,1)S(1)} %add_convert_fusion.11), channel_id=1, source_target_pairs={{0,2},{1,3},{2,0},{3,1},{4,6},{5,7},{6,4},{7,5},{8,10},{9,11},{10,... | collective-permute-start | bytes 1769480 | tf_op jit(solution)/shard_map/ppermute | solution.py:83
  335.0 36.6 %copy-start.6 = (f32[768,768]{0,1:T(8,128)}, f32[768,768]{0,1:T(8,128)S(1)}, u32[]{:S(2)}) copy-start(f32[768,768]{0,1:T(8,128)S(1)} %multiply_add_fusion) | copy-start | bytes 7077892
  349.6 5.1 collective-permute-start.23
  354.2 23.9 %collective-permute-start.12 = (bf16[384,768]{0,1:T(8,128)(2,1)}, bf16[384,768]{0,1:T(8,128)(2,1)}, u32[]{:S(2)}, u32[]{:S(2)}) collective-permute-start(bf16[384,768]{0,1:T(8,128)(2,1)} %add_convert_fusion.10), channel_id=1, source_target_pairs={{0,1},{1,0},{2,3},{3,2},{4,5},{5,4},{6,7},{7,6},{8,9},{9,8},{10,11... | collective-permute-start | bytes 1769480 | tf_op jit(solution)/shard_map/ppermute | solution.py:79
  354.8 15.4 %collective-permute-start.24 = (bf16[384,768]{0,1:T(8,128)(2,1)S(1)}, bf16[384,768]{0,1:T(8,128)(2,1)S(1)}, u32[]{:S(2)}, u32[]{:S(2)}) collective-permute-start(bf16[384,768]{0,1:T(8,128)(2,1)S(1)} %add_convert_fusion.7), channel_id=1, source_target_pairs={{0,2},{1,3},{2,0},{3,1},{4,6},{5,7},{6,4},{7,5},{8,10},{9,11},{10,... | collective-permute-start | bytes 1769480 | tf_op jit(solution)/shard_map/ppermute | solution.py:83
  357.4 14.2 %copy-start.31 = (bf16[256,192]{1,0:T(8,128)(2,1)S(1)}, bf16[256,192]{1,0:T(8,128)(2,1)}, u32[]{:S(2)}) copy-start(bf16[256,192]{1,0:T(8,128)(2,1)} %copy.140) | copy-start | bytes 294916
  357.4 14.2 %copy-start.33 = (bf16[256,192]{1,0:T(8,128)(2,1)S(1)}, bf16[256,192]{1,0:T(8,128)(2,1)}, u32[]{:S(2)}) copy-start(bf16[256,192]{1,0:T(8,128)(2,1)} %copy.141) | copy-start | bytes 294916
  357.4 14.2 %copy-start.35 = (bf16[256,192]{1,0:T(8,128)(2,1)S(1)}, bf16[256,192]{1,0:T(8,128)(2,1)}, u32[]{:S(2)}) copy-start(bf16[256,192]{1,0:T(8,128)(2,1)} %copy.142) | copy-start | bytes 294916
  370.4 2.1 collective-permute-start.25
  382.7 37.3 %all-to-all-start.4 = ((bf16[8,48,768]{2,1,0:T(8,128)(2,1)}), bf16[8,48,768]{2,1,0:T(8,128)(2,1)}, u32[]{:S(2)}, u32[]{:S(2)}) async-start(bf16[8,48,768]{2,1,0:T(8,128)(2,1)} %bitcast.222), calls=%async_computation.4 | async-start | bytes 1179648 | tf_op jit(solution)/shard_map/all_to_all | solution.py:87
  420.0 28.9 %all-to-all-start.9 = ((bf16[8,48,768]{2,1,0:T(8,128)(2,1)}), bf16[8,48,768]{2,1,0:T(8,128)(2,1)S(1)}, u32[]{:S(2)}, u32[]{:S(2)}) async-start(bf16[8,48,768]{2,1,0:T(8,128)(2,1)} %bitcast.221), calls=%async_computation.9 | async-start | bytes 1179648 | tf_op jit(solution)/shard_map/all_to_all | solution.py:87
  438.0 18.2 %collective-permute-start.13 = (bf16[384,768]{0,1:T(8,128)(2,1)S(1)}, bf16[384,768]{0,1:T(8,128)(2,1)}, u32[]{:S(2)}, u32[]{:S(2)}) collective-permute-start(bf16[384,768]{0,1:T(8,128)(2,1)S(1)} %copy.146), channel_id=1, source_target_pairs={{0,1},{1,0},{2,3},{3,2},{4,5},{5,4},{6,7},{7,6},{8,9},{9,8},{10,11... | collective-permute-start | bytes 1769480 | tf_op jit(solution)/shard_map/ppermute | solution.py:79
  450.0 9.9 %collective-permute-start.26 = (bf16[384,768]{0,1:T(8,128)(2,1)}, bf16[384,768]{0,1:T(8,128)(2,1)S(1)}, u32[]{:S(2)}, u32[]{:S(2)}) collective-permute-start(bf16[384,768]{0,1:T(8,128)(2,1)} %copy.161), channel_id=1, source_target_pairs={{0,1},{1,0},{2,3},{3,2},{4,5},{5,4},{6,7},{7,6},{8,9},{9,8},{10,11... | collective-permute-start | bytes 1769480 | tf_op jit(solution)/shard_map/ppermute | solution.py:79
  (101 other events, 345.6 us)
Sparse Core Ops, SparseCore 0:
  378.2 164.4 all-reduce.4

commit v2 on v1

v2 whole, which is shorter than its diff:
```python
import functools

import jax
import jax.numpy as jnp
from jax import lax
from jax.experimental import pallas as pl
from jax.experimental.pallas import tpu as pltpu
from jax.sharding import PartitionSpec as P

HD = 64
EXPERTS = 16
CAP = 120


EPSILON = 1e-05
ROPE_BASE = 10000.0
MASKED = -1e30


def rms_scale(values):
    return lax.rsqrt(jnp.mean(values * values, axis=-1, keepdims=True) + EPSILON)


def matmul(left_side, right_side):
    return jnp.dot(left_side, right_side, preferred_element_type=jnp.float32)


def matmul_bt(left_side, right_side):
    return lax.dot_general(
        left_side, right_side, (((1,), (1,)), ((), ())), preferred_element_type=jnp.float32
    )


def matmul_at(left_side, right_side):
    return lax.dot_general(
        left_side, right_side, (((0,), (0,)), ((), ())), preferred_element_type=jnp.float32
    )


def silu_value(gate_in):
    return gate_in * jax.nn.sigmoid(gate_in)


def silu_slope(gate_in):
    sigma = jax.nn.sigmoid(gate_in)
    return sigma * (1.0 + gate_in * (1.0 - sigma))


def tie(*values):
    return lax.optimization_barrier(values)


def core_swap(values):
    return lax.ppermute(values, "tensor", [(i, i ^ 1) for i in range(4)])


def far_swap(values):
    return lax.ppermute(values, "tensor", [(i, i ^ 2) for i in range(4)])


def exchange(values):
    return lax.all_to_all(values, "expert", split_axis=0, concat_axis=0, tiled=True)


def in_order(bit, own, other, axis=0):
    return jnp.where(
        bit == 0,
        jnp.concatenate([own, other], axis=axis),
        jnp.concatenate([other, own], axis=axis),
    )


def gather_four(bit_low, bit_high, own, axis):
    far = far_swap(own)
    near = core_swap(own)
    far_near = core_swap(far)
    here = in_order(bit_low, own, near, axis)
    there = in_order(bit_low, far, far_near, axis)
    return in_order(bit_high, here, there, axis)


def select(onehot, values):
    return jnp.dot(onehot, values, preferred_element_type=jnp.float32).astype(jnp.bfloat16)


def pair_of_halves(kept, given, meanwhile=lambda pair: None):
    pair = (kept.astype(jnp.float32) + core_swap(given).astype(jnp.float32)).astype(jnp.bfloat16)
    far = far_swap(pair)
    meanwhile(pair)
    return pair.astype(jnp.float32) + far.astype(jnp.float32)


def after(values, *anchors):
    return lax.optimization_barrier((values, *anchors))[0]


def group_swap(values, step):
    size = lax.axis_size("expert")
    return lax.ppermute(values, "expert", [(i, i ^ (1 << step)) for i in range(size)])


class GroupSum:
    def __init__(self, values):
        self.steps = lax.axis_size("expert").bit_length() - 1
        self.me = lax.axis_index("expert")
        self.shape = values.shape
        self.part = values.astype(jnp.bfloat16).reshape(1 << self.steps, -1, values.shape[1])
        self.stage = 0
        self.split()

    def split(self):
        bit = (self.me >> self.stage) & 1
        pairs = self.part.reshape((-1, 2) + self.part.shape[1:])
        self.kept = lax.dynamic_index_in_dim(pairs, bit, 1, keepdims=False)
        self.given = lax.dynamic_index_in_dim(pairs, 1 - bit, 1, keepdims=False)

    def start(self, *anchors):
        if self.stage < self.steps:
            self.came = group_swap(after(self.given, *anchors), self.stage)
        else:
            step = 2 * self.steps - 1 - self.stage
            self.came = group_swap(after(self.part, *anchors), step)

    def end(self, *anchors):
        came = after(self.came, *anchors)
        if self.stage < self.steps:
            total = self.kept.astype(jnp.float32) + came.astype(jnp.float32)
            self.part = total.astype(jnp.bfloat16)
            self.stage += 1
            if self.stage < self.steps:
                self.split()
        else:
            bit = (self.me >> (2 * self.steps - 1 - self.stage)) & 1
            both = in_order(bit, self.part[:, None], came[:, None], 1)
            self.part = both.reshape((-1,) + self.part.shape[1:])
            self.stage += 1

    def advance(self, *anchors):
        self.end(*anchors)
        self.start()

    def finish(self, *anchors):
        while self.stage < 2 * self.steps:
            self.end(*anchors)
            if self.stage < 2 * self.steps:
                self.start()
        return self.part.reshape(self.shape)


def three_parts(values):
    high = lax.reduce_precision(values, 8, 7)
    rest = values - high
    middle = lax.reduce_precision(rest, 8, 7)
    return [part.astype(jnp.bfloat16) for part in (high, middle, rest - middle)]


def expert_kernel(
    half_slots,
    block,
    which_ref,
    rows_ref,
    cot_ref,
    gate_ref,
    up_ref,
    down_ref,
    back_ref,
    out_ref,
    mid_ref,
    d_gate_ref,
    d_up_ref,
):
    rows = rows_ref[...]
    count = rows.shape[0]
    gate_w, up_w, down_w = (gate_ref[0], up_ref[0], down_ref[0])
    gate_lin = matmul(rows, gate_w)
    up_lin = matmul(rows, up_w)
    raw = matmul_bt(cot_ref[...], down_w)
    sigma = 1.0 / (1.0 + jnp.exp(-gate_lin))
    act = gate_lin * sigma
    mid = act * up_lin
    scalar = jnp.sum(raw * mid, axis=1, keepdims=True)
    lanes = lax.broadcasted_iota(jnp.int32, (block, 128), 1)
    subs = lax.broadcasted_iota(jnp.int32, (block, 128), 0)
    diagonal = (lanes == subs) & (lanes < half_slots)
    last = 16
    at = half_slots - (block - last)
    sub_last = lax.broadcasted_iota(jnp.int32, (last, 128), 0)
    gates = []
    for b in range(count // block):
        tail = rows_ref[(b + 1) * block - last : (b + 1) * block, 0:384].astype(jnp.float32)
        total = tail[:, 0:128] + tail[:, 128:256] + tail[:, 256:384]
        line = jnp.sum(jnp.where(sub_last == at, total, 0.0), axis=0, keepdims=True)
        gates.append(jnp.sum(jnp.where(diagonal, line, 0.0), axis=1, keepdims=True))
    gate = jnp.concatenate(gates, axis=0) if len(gates) > 1 else gates[0]
    d_act = raw * gate
    d_up = (d_act * act).astype(jnp.bfloat16)
    d_gate = (d_act * up_lin * (sigma * (1.0 + gate_lin * (1.0 - sigma)))).astype(jnp.bfloat16)
    mid_g = (mid * gate).astype(jnp.bfloat16)
    mid_ref[...] = mid_g
    d_gate_ref[...] = d_gate
    d_up_ref[...] = d_up
    back = matmul_bt(d_gate, gate_w) + matmul_bt(d_up, up_w)
    back_ref[...] = back.astype(jnp.bfloat16)
    for b in range(count // block):
        part = jnp.where(diagonal, scalar[b * block : (b + 1) * block], 0.0)
        line = jnp.sum(part, axis=0, keepdims=True)
        high = line.astype(jnp.bfloat16).astype(jnp.float32)
        rest = line - high
        middle = rest.astype(jnp.bfloat16).astype(jnp.float32)
        for i, piece in enumerate((high, middle, rest - middle)):
            old = back[(b + 1) * block - last : (b + 1) * block, i * 128 : (i + 1) * 128]
            back_ref[(b + 1) * block - last : (b + 1) * block, i * 128 : (i + 1) * 128] = jnp.where(
                sub_last == at, piece, old
            ).astype(jnp.bfloat16)
    out_ref[...] = matmul(mid_g, down_w).astype(jnp.bfloat16)


def run_expert(which, rows, cots, gate_w, up_w, down_w, half_slots, block):
    count, feat = rows.shape
    hidden = gate_w.shape[2]
    step_rows = min(256, count)
    row_spec = pl.BlockSpec((step_rows, feat), lambda i, w: (i, 0))
    mid_spec = pl.BlockSpec((step_rows, hidden), lambda i, w: (i, 0))
    return pl.pallas_call(
        functools.partial(expert_kernel, half_slots, block),
        grid_spec=pltpu.PrefetchScalarGridSpec(
            num_scalar_prefetch=1,
            grid=(count // step_rows,),
            in_specs=[
                row_spec,
                row_spec,
                pl.BlockSpec((1, feat, hidden), lambda i, w: (w[0], 0, 0)),
                pl.BlockSpec((1, feat, hidden), lambda i, w: (w[0], 0, 0)),
                pl.BlockSpec((1, hidden, feat), lambda i, w: (w[0], 0, 0)),
            ],
            out_specs=[row_spec, row_spec, mid_spec, mid_spec, mid_spec],
        ),
        out_shape=[jax.ShapeDtypeStruct((count, feat), jnp.bfloat16)] * 2
        + [jax.ShapeDtypeStruct((count, hidden), jnp.bfloat16)] * 3,
        compiler_params=pltpu.CompilerParams(vmem_limit_bytes=50 << 20),
        cost_estimate=pl.CostEstimate(
            flops=12 * count * feat * hidden,
            bytes_accessed=8 * count * feat + 6 * feat * hidden + 6 * count * hidden,
            transcendentals=count * hidden,
        ),
        name="expert_rows",
    )(which, rows, cots, gate_w, up_w, down_w)


def weight_kernel(
    which_ref,
    rows_own,
    rows_other,
    cot_own,
    cot_other,
    mid_own,
    mid_other,
    dg_own,
    dg_other,
    du_own,
    du_other,
    g_gate_ref,
    g_up_ref,
    g_down_ref,
):
    def fill(rows, cots, mid, d_gate, d_up):
        turned = rows[...].T
        g_gate_ref[0] = matmul(turned, d_gate[...])
        g_up_ref[0] = matmul(turned, d_up[...])
        g_down_ref[0] = matmul_at(mid[...], cots[...])

    @pl.when(pl.program_id(0) == 0)
    def _():
        fill(rows_own, cot_own, mid_own, dg_own, du_own)

    @pl.when(pl.program_id(0) == 1)
    def _():
        fill(rows_other, cot_other, mid_other, dg_other, du_other)


def run_weights(bit_low, own, other):
    count, feat = own[0].shape
    hidden = own[2].shape[1]
    width = min(256, hidden)
    whole = pl.BlockSpec((count, feat), lambda s, j, w: (0, 0))
    first = pl.BlockSpec((count, width), lambda s, j, w: (0, jnp.where(s == 0, j, 0)))
    second = pl.BlockSpec((count, width), lambda s, j, w: (0, jnp.where(s == 1, j, 0)))

    def slab(s, w):
        return jnp.where(s == 0, w[0], 1 - w[0])

    wide = pl.BlockSpec((1, feat, width), lambda s, j, w: (slab(s, w), 0, j))
    tall = pl.BlockSpec((1, width, feat), lambda s, j, w: (slab(s, w), j, 0))
    return pl.pallas_call(
        weight_kernel,
        grid_spec=pltpu.PrefetchScalarGridSpec(
            num_scalar_prefetch=1,
            grid=(2, hidden // width),
            in_specs=[whole, whole, whole, whole, first, second, first, second, first, second],
            out_specs=[wide, wide, tall],
        ),
        out_shape=[
            jax.ShapeDtypeStruct((2, feat, hidden), jnp.float32),
            jax.ShapeDtypeStruct((2, feat, hidden), jnp.float32),
            jax.ShapeDtypeStruct((2, hidden, feat), jnp.float32),
        ],
        compiler_params=pltpu.CompilerParams(vmem_limit_bytes=56 << 20),
        cost_estimate=pl.CostEstimate(
            flops=12 * count * feat * hidden,
            bytes_accessed=8 * count * feat + 12 * count * hidden + 24 * feat * hidden,
            transcendentals=0,
        ),
        name="expert_weights",
    )(
        bit_low.reshape(1),
        own[0],
        other[0],
        own[1],
        other[1],
        own[2],
        other[2],
        own[3],
        other[3],
        own[4],
        other[4],
    )


def swap_halves(values):
    lanes = lax.broadcasted_iota(jnp.int32, values.shape, 1)
    return jnp.where(lanes % HD < HD // 2, pltpu.roll(values, 96, 1), pltpu.roll(values, 32, 1))


def fill_bias(bias_ref, start_ref):
    rows = bias_ref.shape[0]
    row_at = lax.broadcasted_iota(jnp.int32, (rows, 128), 0)
    lane_at = lax.broadcasted_iota(jnp.int32, (rows, 128), 1)
    start = start_ref[...]
    for part in range(rows // 128):
        key_at = lane_at + part * 128
        allowed = (key_at >= start) & (key_at <= row_at)
        bias_ref[:, part * 128 : part * 128 + 128] = jnp.where(allowed, 0.0, MASKED)


def fixed(shape):
    return pl.BlockSpec(shape, lambda *_: tuple(0 for _ in shape))


def pad_rows(piece, rows):
    return jnp.concatenate([piece, jnp.zeros((rows - piece.shape[0], piece.shape[1]), piece.dtype)], 0)


def heads_of(piece_rows, pair):
    return min(2, (piece_rows - pair * 128) // HD)


def attend_piece(hidden, weights, cos, sin, bias_ref, outs):
    q_ref, k_ref, v_ref, mixed_ref, lse_ref = outs
    rows = hidden.shape[0]
    width = q_ref.shape[1]
    span = 256
    lane_ids = lax.broadcasted_iota(jnp.int32, (rows, 128), 1)
    lse_ref[...] = jnp.zeros_like(lse_ref)
    linear = matmul_bt(
        hidden, jnp.concatenate([pad_rows(weight[...], width) for weight in weights], axis=0)
    )
    for pair in range(width // 128):
        at = slice(pair * 128, pair * 128 + 128)
        q_lin = linear[:, pair * 128 : pair * 128 + 128]
        k_lin = linear[:, width + pair * 128 : width + pair * 128 + 128]
        v_pair = linear[:, 2 * width + pair * 128 : 2 * width + pair * 128 + 128]
        v_pair = v_pair.astype(jnp.bfloat16)
        q_pair = (q_lin * cos + swap_halves(q_lin) * sin).astype(jnp.bfloat16)
        k_pair = (k_lin * cos + swap_halves(k_lin) * sin).astype(jnp.bfloat16)
        q_ref[:, at] = q_pair
        k_ref[:, at] = k_pair
        v_ref[:, at] = v_pair
        q_scaled = q_pair * jnp.bfloat16(HD ** (-0.5))
        zero = jnp.zeros_like(q_scaled)
        q_heads = [jnp.where(lane_ids < HD, q_scaled, zero), jnp.where(lane_ids < HD, zero, q_scaled)]
        q_heads = q_heads[: heads_of(weights[0].shape[0], pair)]
        for start in range(0, rows, span):
            end = start + span
            ids = lane_ids[start:end]
            mixed = None
            for head, q_head in enumerate(q_heads):
                scores = matmul_bt(q_head[start:end], k_pair[:end]) + bias_ref[start:end, :end]
                top = jnp.max(scores, axis=-1, keepdims=True)
                raised = jnp.exp(scores - top)
                total = jnp.sum(raised, axis=-1, keepdims=True)
                out = matmul(raised.astype(jnp.bfloat16), v_pair[:end]) / total
                mixed = out if mixed is None else jnp.where(ids < HD, mixed, out)
                lse = top + jnp.log(total)
                lse_ref[start:end, :] = jnp.where(
                    ids == pair * 2 + head, lse, lse_ref[start:end, :]
                )
            mixed_ref[start:end, at] = mixed.astype(jnp.bfloat16)


def attention_near_kernel(
    own_ref,
    other_ref,
    place_own_ref,
    place_other_ref,
    gain_ref,
    wq_ref,
    wk_ref,
    wv_ref,
    cos_ref,
    sin_ref,
    start_ref,
    grouped_ref,
    hidden_ref,
    q_ref,
    k_ref,
    v_ref,
    mixed_ref,
    lse_ref,
    bias_ref,
):
    fill_bias(bias_ref, start_ref)
    placed = matmul(place_own_ref[...], own_ref[...])
    placed = placed + matmul(place_other_ref[...], other_ref[...])
    grouped_ref[...] = placed.astype(jnp.bfloat16)
    hidden_ref[...] = (placed * rms_scale(placed) * gain_ref[...]).astype(jnp.bfloat16)
    attend_piece(
        hidden_ref[...],
        (wq_ref, wk_ref, wv_ref),
        cos_ref[...],
        sin_ref[...],
        bias_ref,
        (q_ref, k_ref, v_ref, mixed_ref, lse_ref),
    )


def attention_far_kernel(
    hidden_ref,
    wq_ref,
    wk_ref,
    wv_ref,
    cos_ref,
    sin_ref,
    start_ref,
    q_ref,
    k_ref,
    v_ref,
    mixed_ref,
    lse_ref,
    bias_ref,
):
    fill_bias(bias_ref, start_ref)
    attend_piece(
        hidden_ref[...],
        (wq_ref, wk_ref, wv_ref),
        cos_ref[...],
        sin_ref[...],
        bias_ref,
        (q_ref, k_ref, v_ref, mixed_ref, lse_ref),
    )


def call_whole(kernel, name, ins, outs, scratch, flops, transcendentals=0, prefetch=()):
    moved = sum(array.size * array.dtype.itemsize for array in (*ins, *outs))
    return pl.pallas_call(
        kernel,
        grid_spec=pltpu.PrefetchScalarGridSpec(
            num_scalar_prefetch=len(prefetch),
            grid=(1,),
            in_specs=[fixed(array.shape) for array in ins],
            out_specs=[fixed(out.shape) for out in outs],
            scratch_shapes=scratch,
        ),
        out_shape=list(outs),
        compiler_params=pltpu.CompilerParams(vmem_limit_bytes=56 << 20),
        cost_estimate=pl.CostEstimate(
            flops=flops, bytes_accessed=moved, transcendentals=transcendentals
        ),
        name=name,
    )(*prefetch, *ins)


def padded(piece_rows):
    return -(-piece_rows // 128) * 128


def run_attention(near, ins):
    rows = ins[-1].shape[0]
    feat = ins[0].shape[1]
    piece = ins[-4].shape[0]
    width = padded(piece)
    outs = [jax.ShapeDtypeStruct((rows, feat), jnp.bfloat16)] * (2 if near else 0)
    outs = outs + [jax.ShapeDtypeStruct((rows, width), jnp.bfloat16)] * 4
    outs = outs + [jax.ShapeDtypeStruct((rows, 128), jnp.float32)]
    return call_whole(
        attention_near_kernel if near else attention_far_kernel,
        "attention_near" if near else "attention_far",
        ins,
        outs,
        [pltpu.VMEM((rows, rows), jnp.float32)],
        6 * rows * feat * width + 4 * rows * rows * width + (2 * rows * rows * feat if near else 0),
        rows * rows * piece // HD,
    )


def middle_kernel(
    half_slots,
    block,
    turn_ref,
    m0_ref,
    m1_ref,
    m2_ref,
    m3_ref,
    grouped_ref,
    o0_ref,
    o1_ref,
    o2_ref,
    o3_ref,
    gain_ref,
    router_ref,
    slots_ref,
    one_ref,
    two_ref,
    first_ref,
    second_ref,
    resid_ref,
    hidden_ref,
    sent_ref,
    weight_ref,
    mixed_ref,
    whole_ref,
):
    mixed = (m0_ref, m1_ref, m2_ref, m3_ref)
    parts = (o0_ref, o1_ref, o2_ref, o3_ref)
    width = m0_ref.shape[1]
    for turn in range(4):

        @pl.when(turn_ref[0] == turn)
        def _():
            for i in range(4):
                mixed_ref[:, i * width : (i + 1) * width] = mixed[i ^ turn][...]
                whole_ref[i * width : (i + 1) * width, :] = pad_rows(parts[i ^ turn][...], width)

    resid = grouped_ref[...].astype(jnp.float32) + matmul(mixed_ref[...], whole_ref[...])
    resid_ref[...] = resid
    hidden = (resid * rms_scale(resid) * gain_ref[...]).astype(jnp.bfloat16)
    hidden_ref[...] = hidden
    logits = matmul_bt(router_ref[...], hidden)
    chosen_one = jnp.sum(one_ref[...] * logits, axis=0, keepdims=True)
    chosen_two = jnp.sum(two_ref[...] * logits, axis=0, keepdims=True)
    top = jnp.maximum(chosen_one, chosen_two)
    raised_one = jnp.exp(chosen_one - top)
    raised_two = jnp.exp(chosen_two - top)
    weight_one = raised_one / (raised_one + raised_two)
    weight_two = raised_two / (raised_one + raised_two)
    weight_ref[0:1, :] = weight_one
    weight_ref[1:2, :] = weight_two
    gate_of = first_ref[...] * weight_one + second_ref[...] * weight_two
    high = gate_of.astype(jnp.bfloat16).astype(jnp.float32)
    rest = gate_of - high
    middle = rest.astype(jnp.bfloat16).astype(jnp.float32)
    three = jnp.concatenate([high, middle, rest - middle], axis=0).astype(jnp.bfloat16)
    lines = matmul_bt(three, slots_ref[...])
    dests = first_ref.shape[0]
    last = 16
    at = half_slots - (block - last)
    sub_last = lax.broadcasted_iota(jnp.int32, (last, block), 0)
    chunk = 256
    for base in range(0, slots_ref.shape[0], chunk):
        rows = matmul(slots_ref[base : base + chunk, :], hidden)
        sent_ref[base : base + chunk, :] = rows.astype(jnp.bfloat16)
        for inner in range(block, chunk + 1, block):
            dest = (base + inner) // block - 1
            for i in range(3):
                line = lines[i * dests + dest : i * dests + dest + 1, dest * block : (dest + 1) * block]
                old = rows[inner - last : inner, i * 128 : i * 128 + block]
                sent_ref[base + inner - last : base + inner, i * 128 : i * 128 + block] = jnp.where(
                    sub_last == at, line, old
                ).astype(jnp.bfloat16)


def run_middle(half_slots, block, turn, *ins):
    rows, width = ins[0].shape
    feat = ins[4].shape[1]
    slots = ins[11]
    outs = [
        jax.ShapeDtypeStruct((rows, feat), jnp.float32),
        jax.ShapeDtypeStruct((rows, feat), jnp.bfloat16),
        jax.ShapeDtypeStruct((slots.shape[0], feat), jnp.bfloat16),
        jax.ShapeDtypeStruct((8, rows), jnp.float32),
    ]
    return call_whole(
        functools.partial(middle_kernel, half_slots, block),
        "middle",
        ins,
        outs,
        [pltpu.VMEM((rows, 4 * width), jnp.bfloat16), pltpu.VMEM((4 * width, feat), jnp.bfloat16)],
        2 * rows * feat * (4 * width + slots.shape[0]),
        4 * rows,
        (turn,),
    )


def piece_gradients(d_proj, w_out, q_ref, k_ref, v_ref, lse_ref, bias_ref, cos, sin, all_ref):
    rows, width = q_ref.shape
    span = 256
    scale = HD ** (-0.5)
    lane_ids = lax.broadcasted_iota(jnp.int32, (rows, 128), 1)
    d_all = matmul_bt(d_proj, pad_rows(w_out, width)).astype(jnp.bfloat16)
    blocks = rows // span

    def unturn(values):
        return (values * cos - swap_halves(values) * sin).astype(jnp.bfloat16)

    for pair in range(width // 128):
        at = slice(pair * 128, pair * 128 + 128)
        k = k_ref[:, at]
        v = v_ref[:, at]
        q_scaled = q_ref[:, at] * jnp.bfloat16(scale)
        d_mixed = d_all[:, at]
        zero = jnp.zeros_like(q_scaled)
        d_q = [jnp.zeros((span, 128), jnp.float32) for _ in range(blocks)]
        d_k = [jnp.zeros((span, 128), jnp.float32) for _ in range(blocks)]
        d_v = [jnp.zeros((span, 128), jnp.float32) for _ in range(blocks)]
        for head in range(heads_of(w_out.shape[0], pair)):
            mask = (lane_ids < HD) if head == 0 else (lane_ids >= HD)
            q_head = jnp.where(mask, q_scaled, zero)
            k_head = jnp.where(mask, k, zero)
            d_head = jnp.where(mask, d_mixed, zero)
            which = pair * 2 + head
            for block in range(blocks):
                start, end = block * span, block * span + span
                lse = jnp.sum(
                    jnp.where(lane_ids[start:end] == which, lse_ref[start:end, :], 0.0),
                    axis=-1,
                    keepdims=True,
                )
                scores = matmul_bt(q_head[start:end], k[:end]) + bias_ref[start:end, :end]
                probs = jnp.exp(scores - lse)
                d_probs = matmul_bt(d_head[start:end], v[:end])
                inner = jnp.sum(probs * d_probs, axis=-1, keepdims=True)
                d_scores = (probs * (d_probs - inner)).astype(jnp.bfloat16)
                probs = probs.astype(jnp.bfloat16)
                d_q[block] = d_q[block] + matmul(d_scores, k_head[:end])
                key_term = matmul_at(d_scores, q_head[start:end])
                value_term = matmul_at(probs, d_head[start:end])
                for other in range(block + 1):
                    part = slice(other * span, other * span + span)
                    d_k[other] = d_k[other] + key_term[part]
                    d_v[other] = d_v[other] + value_term[part]
        at_k = slice(width + pair * 128, width + pair * 128 + 128)
        at_v = slice(2 * width + pair * 128, 2 * width + pair * 128 + 128)
        all_ref[:, at] = unturn(jnp.concatenate(d_q, axis=0) * scale)
        all_ref[:, at_k] = unturn(jnp.concatenate(d_k, axis=0))
        all_ref[:, at_v] = jnp.concatenate(d_v, axis=0).astype(jnp.bfloat16)


def back_near_kernel(
    turn_ref,
    dh_own_ref,
    dh_other_ref,
    dg_ref,
    weight_ref,
    one_ref,
    two_ref,
    router_ref,
    resid_ref,
    hidden_two_ref,
    cot_ref,
    gain_ref,
    hidden_ref,
    mixed_ref,
    start_ref,
    cos_ref,
    sin_ref,
    lse_ref,
    w_out_ref,
    q_ref,
    k_ref,
    v_ref,
    wq_ref,
    wk_ref,
    wv_ref,
    d_resid_ref,
    d_proj_ref,
    g_ffn_ref,
    g_router_ref,
    late_ref,
    term_ref,
    bias_ref,
    all_ref,
    dh_ref,
):
    half = dh_own_ref.shape[0]

    @pl.when(turn_ref[0] % 2 == 0)
    def _():
        dh_ref[:half, :] = dh_own_ref[...]
        dh_ref[half:, :] = dh_other_ref[...]

    @pl.when(turn_ref[0] % 2 == 1)
    def _():
        dh_ref[:half, :] = dh_other_ref[...]
        dh_ref[half:, :] = dh_own_ref[...]

    fill_bias(bias_ref, start_ref)
    weight_one, weight_two = (weight_ref[0:1, :], weight_ref[1:2, :])
    d_one, d_two = (dg_ref[0:1, :], dg_ref[1:2, :])
    inner = weight_one * d_one + weight_two * d_two
    d_logits = one_ref[...] * (weight_one * (d_one - inner))
    d_logits = d_logits + two_ref[...] * (weight_two * (d_two - inner))
    d_logits = d_logits.astype(jnp.bfloat16)
    g_router_ref[...] = matmul(d_logits, hidden_two_ref[...])
    d_rows = dh_ref[...].astype(jnp.float32) + matmul_at(d_logits, router_ref[...])
    resid = resid_ref[...]
    scale = rms_scale(resid)
    normed = resid * scale
    g_ffn_ref[...] = jnp.sum(d_rows * normed, axis=0, keepdims=True)
    grown = d_rows * gain_ref[...]
    shift = jnp.mean(grown * normed, axis=-1, keepdims=True)
    d_resid = cot_ref[...].astype(jnp.float32) + scale * (grown - normed * shift)
    d_resid_ref[...] = d_resid
    d_proj_ref[...] = d_resid.astype(jnp.bfloat16)
    piece_gradients(
        d_proj_ref[...],
        w_out_ref[...],
        q_ref,
        k_ref,
        v_ref,
        lse_ref,
        bias_ref,
        cos_ref[...],
        sin_ref[...],
        all_ref,
    )
    piece, width = (w_out_ref.shape[0], q_ref.shape[1])
    grads = matmul_at(all_ref[...], hidden_ref[...]).astype(jnp.bfloat16)
    for i in range(3):
        late_ref[i * piece : (i + 1) * piece, :] = grads[i * width : i * width + piece, :]
    g_out = matmul_at(mixed_ref[...], d_proj_ref[...]).astype(jnp.bfloat16)
    late_ref[3 * piece : 4 * piece, :] = g_out[:piece, :]
    whole = jnp.concatenate([pad_rows(w[...], width) for w in (wq_ref, wk_ref, wv_ref)], axis=0)
    term_ref[...] = matmul(all_ref[...], whole)


def run_back_near(turn, *ins):
    rows, feat = ins[7].shape
    piece = ins[17].shape[0]
    width = padded(piece)
    outs = [
        jax.ShapeDtypeStruct((rows, feat), jnp.float32),
        jax.ShapeDtypeStruct((rows, feat), jnp.bfloat16),
        jax.ShapeDtypeStruct((1, feat), jnp.float32),
        jax.ShapeDtypeStruct((EXPERTS, feat), jnp.float32),
        jax.ShapeDtypeStruct((4 * piece, feat), jnp.bfloat16),
        jax.ShapeDtypeStruct((rows, feat), jnp.float32),
    ]
    return call_whole(
        back_near_kernel,
        "back_near",
        ins,
        outs,
        [
            pltpu.VMEM((rows, rows), jnp.float32),
            pltpu.VMEM((rows, 3 * width), jnp.bfloat16),
            pltpu.VMEM((rows, feat), jnp.bfloat16),
        ],
        rows * width * (16 * feat + 10 * rows),
        rows * rows * piece // HD,
        (turn,),
    )


def back_far_kernel(
    d_proj_ref,
    start_ref,
    cos_ref,
    sin_ref,
    lse_ref,
    w_out_ref,
    q_ref,
    k_ref,
    v_ref,
    all_ref,
    bias_ref,
):
    fill_bias(bias_ref, start_ref)
    piece_gradients(
        d_proj_ref[...],
        w_out_ref[...],
        q_ref,
        k_ref,
        v_ref,
        lse_ref,
        bias_ref,
        cos_ref[...],
        sin_ref[...],
        all_ref,
    )


def run_back_far(*ins):
    rows, feat = ins[0].shape
    piece = ins[5].shape[0]
    width = padded(piece)
    return call_whole(
        back_far_kernel,
        "back_far",
        ins,
        [jax.ShapeDtypeStruct((rows, 3 * width), jnp.bfloat16)],
        [pltpu.VMEM((rows, rows), jnp.float32)],
        rows * width * (2 * feat + 10 * rows),
        rows * rows * piece // HD,
    )[0]


def back_rows_kernel(
    all_ref,
    d_resid_ref,
    term_ref,
    place_own_ref,
    place_other_ref,
    wq_ref,
    wk_ref,
    wv_ref,
    give_ref,
    keep_ref,
    d_half_ref,
    sum_ref,
):
    width = all_ref.shape[1] // 3
    whole = jnp.concatenate([pad_rows(w[...], width) for w in (wq_ref, wk_ref, wv_ref)], axis=0)
    sum_ref[...] = matmul(all_ref[...], whole)
    total = (term_ref[...] + sum_ref[...]).astype(jnp.bfloat16)
    give_ref[...] = matmul_at(place_other_ref[...], total).astype(jnp.bfloat16)
    keep_ref[...] = matmul_at(place_own_ref[...], total).astype(jnp.bfloat16)
    d_resid = d_resid_ref[...]
    high = d_resid.astype(jnp.bfloat16)
    low = (d_resid - high.astype(jnp.float32)).astype(jnp.bfloat16)
    d_half_ref[...] = matmul_at(place_own_ref[...], high) + matmul_at(place_own_ref[...], low)


def run_back_rows(*ins):
    rows, width = ins[0].shape
    feat = ins[1].shape[1]
    half = ins[3].shape[1]
    outs = [
        jax.ShapeDtypeStruct((half, feat), jnp.bfloat16),
        jax.ShapeDtypeStruct((half, feat), jnp.bfloat16),
        jax.ShapeDtypeStruct((half, feat), jnp.float32),
    ]
    return call_whole(
        back_rows_kernel,
        "back_rows",
        ins,
        outs,
        [pltpu.VMEM((rows, feat), jnp.float32)],
        2 * rows * width * feat + 8 * rows * half * feat,
    )


def body(
    tokens,
    order,
    lengths,
    routes,
    attn_gain,
    w_query,
    w_key,
    w_value,
    w_out,
    ffn_gain,
    w_router,
    shared_gate,
    shared_up,
    shared_down,
    expert_gate,
    expert_up,
    expert_down,
    cotangent,
):
    row_count, feat_width = tokens.shape
    group_count = lax.axis_size("expert")
    share_rows = row_count // group_count
    half_share = share_rows // 2
    half_rows = row_count // 2
    my_group = lax.axis_index("expert")
    my_tensor = lax.axis_index("tensor")
    bit_low = lax.rem(my_tensor, 2)
    bit_high = my_tensor // 2
    slab_dev = expert_gate.shape[0]
    slab_total = slab_dev * group_count
    replicas = max(1, slab_total // EXPERTS)
    half_slots = slab_dev * CAP // 2
    row_ids = jnp.arange(row_count, dtype=jnp.int32)
    earlier = (row_ids[:, None] < row_ids[None, :]).astype(jnp.bfloat16)

    local_order = lax.dynamic_slice_in_dim(order, my_group * row_count, row_count, 0)
    groups = jnp.arange(group_count, dtype=jnp.int32)
    dest_group = local_order // row_count
    dest_onehot = (groups[:, None] == dest_group[None, :]).astype(jnp.bfloat16)
    dest_before = matmul(dest_onehot, earlier)
    send_rank = jnp.sum(dest_onehot.astype(jnp.float32) * dest_before, axis=0).astype(jnp.int32)
    send_half = send_rank // half_share
    send_slot = send_half * half_rows + dest_group * half_share + send_rank % half_share
    send_pick = send_slot[None, :] == (
        bit_low * half_rows + jnp.arange(half_rows, dtype=jnp.int32)[:, None]
    )
    send_pick = send_pick.astype(jnp.bfloat16)
    in_tokens = exchange(select(send_pick, tokens))
    cot_send, in_tokens = tie(select(send_pick, cotangent), in_tokens)
    in_cot = exchange(cot_send)

    near_weights = (w_query.T, w_key.T, w_value.T)
    far_weights = tuple(far_swap(weight) for weight in near_weights)
    out_far = far_swap(after(w_out, far_weights[1]))
    tokens_other = core_swap(in_tokens)
    turn = my_tensor.reshape(1)

    all_order = order.reshape(group_count, row_count)
    mine = all_order // row_count == my_group
    arrive_rank = matmul(mine.astype(jnp.bfloat16), earlier).astype(jnp.int32)
    arrive_rank = jnp.where(mine, arrive_rank, -1)
    landing = all_order - my_group * row_count
    target = jnp.sum(
        jnp.where(
            arrive_rank[:, None, :] == jnp.arange(share_rows, dtype=jnp.int32)[None, :, None],
            landing[:, None, :],
            0,
        ),
        axis=-1,
    )
    target = target.reshape(group_count, 2, half_share).transpose(1, 0, 2).reshape(2, half_rows)
    target_own = lax.dynamic_index_in_dim(target, bit_low, 0, keepdims=False)
    target_other = lax.dynamic_index_in_dim(target, 1 - bit_low, 0, keepdims=False)
    place_own = (row_ids[:, None] == target_own[None, :]).astype(jnp.bfloat16)
    place_other = (row_ids[:, None] == target_other[None, :]).astype(jnp.bfloat16)

    expert_ids = jnp.arange(EXPERTS, dtype=jnp.int32)
    member_one = expert_ids[:, None] == routes[None, :, 0]
    member_two = expert_ids[:, None] == routes[None, :, 1]
    member = member_one | member_two
    slot_rank = matmul(member.astype(jnp.bfloat16), earlier).astype(jnp.int32)
    slot_rank = jnp.where(member, slot_rank, -1)

    block = (half_slots + 16) // 16 * 16
    ranks = jnp.repeat(slot_rank, replicas, axis=0).reshape(group_count, slab_dev, row_count)
    ranks = lax.dynamic_index_in_dim(ranks, bit_low * half_slots // CAP, 1, keepdims=False)
    slot_ids = jnp.arange(block, dtype=jnp.int32)
    slots = bit_low * half_slots % CAP + slot_ids
    slots = jnp.where(slot_ids < half_slots, slots, -2)
    slots_cube = (ranks[:, None, :] == slots[None, :, None]).astype(jnp.bfloat16)
    slots_one = slots_cube.reshape(group_count * block, row_count)

    quarter = block // 2
    slots_part = lax.dynamic_slice_in_dim(slots_cube, bit_high * quarter, quarter, 1)
    slots_part = slots_part.reshape(-1, row_count)
    cot_pick_own = select(slots_part, place_own)
    cot_pick_other = select(slots_part, place_other)

    seq_lengths = lengths[0]
    seq_ends = jnp.cumsum(seq_lengths)
    passed = row_ids[:, None] >= seq_ends[None, :]
    sequence_segment = jnp.sum(passed.astype(jnp.int32), axis=1)
    position = row_ids - jnp.sum(jnp.where(passed, seq_lengths[None, :], 0), axis=1)
    half_size = HD // 2
    lanes = jnp.arange(128, dtype=jnp.int32)
    frequency = ROPE_BASE ** (-(lanes % half_size).astype(jnp.float32) / half_size)
    angles = position.astype(jnp.float32)[:, None] * frequency[None, :]
    cos_table = jnp.cos(angles)
    sin_table = jnp.where(lanes % HD < half_size, -1.0, 1.0) * jnp.sin(angles)
    seq_start = jnp.broadcast_to((row_ids - position)[:, None], (row_count, 128))
    gain_one = attn_gain.astype(jnp.float32)[None, :]
    gain_two = ffn_gain.astype(jnp.float32)[None, :]
    tables = (cos_table, sin_table, seq_start)
    grouped, hidden_one, *near_heads, near_mixed, near_lse = run_attention(
        True,
        (in_tokens, tokens_other, place_own, place_other, gain_one, *near_weights, *tables),
    )
    near_swapped = core_swap(near_mixed)
    far_weights = after(far_weights, near_mixed)
    *far_heads, far_mixed, far_lse = run_attention(False, (hidden_one, *far_weights, *tables))
    far_swapped = core_swap(far_mixed)
    out_pieces = (w_out, core_swap(w_out), out_far, core_swap(out_far))
    in_cot = after(in_cot, far_mixed)
    cot_half = core_swap(in_cot)
    cot_part = matmul(cot_pick_own, in_cot) + matmul(cot_pick_other, cot_half)
    cot_part = cot_part.astype(jnp.bfloat16)
    far_swapped = after(far_swapped, cot_part)
    cot_part = exchange(cot_part)

    dest_slab = jnp.arange(group_count, dtype=jnp.int32) * slab_dev + bit_low * half_slots // CAP
    dest_expert = dest_slab // replicas
    first_here = (routes[None, :, 0] == dest_expert[:, None]).astype(jnp.float32)
    second_here = (routes[None, :, 1] == dest_expert[:, None]).astype(jnp.float32)
    one_of = member_one.astype(jnp.float32)
    two_of = member_two.astype(jnp.float32)
    router_rows = w_router.T
    resid_two, hidden_two, sent, gate_weights = run_middle(
        half_slots,
        block,
        turn,
        near_mixed,
        near_swapped,
        far_mixed,
        far_swapped,
        grouped,
        *out_pieces,
        gain_two,
        router_rows,
        slots_one,
        one_of,
        two_of,
        first_here,
        second_here,
    )
    hidden_rows = exchange(after(sent, cot_part))
    cot_part = cot_part.reshape(group_count, quarter, feat_width)
    cot_own = in_order(bit_high, cot_part, far_swap(cot_part), 1).reshape(-1, feat_width)
    cot_other = core_swap(cot_own)
    grouped_cot = matmul(place_own, after(in_cot, sent)) + matmul(place_other, cot_half)
    grouped_cot = grouped_cot.astype(jnp.bfloat16)
    hidden_late = hidden_two

    gate_shared = matmul(hidden_late, shared_gate)
    up_shared = matmul(hidden_late, shared_up)
    act_shared = silu_value(gate_shared)
    shared_mid = (act_shared * up_shared).astype(jnp.bfloat16)
    shared_out = matmul(shared_mid, shared_down)
    d_mid_shared = matmul_bt(grouped_cot, shared_down)
    d_up_shared = (d_mid_shared * act_shared).astype(jnp.bfloat16)
    d_gate_shared = (d_mid_shared * up_shared * silu_slope(gate_shared)).astype(jnp.bfloat16)
    d_hidden_shared = matmul_bt(d_gate_shared, shared_gate) + matmul_bt(d_up_shared, shared_up)
    d_both = jnp.concatenate([d_gate_shared, d_up_shared], axis=1)
    early = GroupSum(
        jnp.concatenate([matmul_at(d_both, hidden_late), matmul_at(shared_mid, grouped_cot)], axis=0)
    )
    shared_send = shared_out.astype(jnp.bfloat16)
    shared_own = matmul_at(place_own, shared_send)
    shared_other = matmul_at(place_other, shared_send)
    resid_high, resid_low = three_parts(resid_two)[:2]
    resid_half = matmul_at(place_own, resid_high) + matmul_at(place_own, resid_low)
    hidden_rows = after(hidden_rows, early.given, shared_own, shared_other, resid_half)
    early.start()

    rows_other = core_swap(hidden_rows)
    which_own = (bit_low * half_slots // CAP).reshape(1)
    which_other = ((1 - bit_low) * half_slots // CAP).reshape(1)
    weights_here = (expert_gate, expert_up, expert_down, half_slots, block)
    back_kept, out_kept, mid_own, dg_own, du_own = run_expert(
        which_own, hidden_rows, cot_own, *weights_here
    )
    back_given, out_given, mid_other, dg_other, du_other = run_expert(
        which_other, rows_other, cot_other, *weights_here
    )
    early.advance(back_given)
    stack_own = (hidden_rows, cot_own, mid_own, dg_own, du_own)
    stack_other = (rows_other, cot_other, mid_other, dg_other, du_other)

    def pair_sum(kept, given):
        return kept.astype(jnp.float32) + core_swap(given).astype(jnp.float32)

    back_sum = pair_sum(back_kept, back_given).reshape(group_count, block, feat_width)
    lines = back_sum[:, half_slots, :384].reshape(group_count, 3, 128)
    lines = jnp.stack(three_parts(jnp.sum(lines, axis=1)), axis=1).astype(jnp.float32)
    lines = jnp.pad(lines.reshape(group_count, 1, 384), ((0, 0), (0, 0), (0, feat_width - 384)))
    back_sum = jnp.where(slot_ids[None, :, None] == half_slots, lines, back_sum)
    back_send = back_sum.astype(jnp.bfloat16).reshape(-1, feat_width)
    back_own = exchange(back_send)
    early.end(back_send)
    out_sum = pair_sum(out_kept, after(out_given, back_send)).astype(jnp.bfloat16)
    out_sum = out_sum.reshape(group_count, block, feat_width)
    out_kept = lax.dynamic_slice_in_dim(out_sum, bit_high * quarter, quarter, 1)
    out_given = lax.dynamic_slice_in_dim(out_sum, (1 - bit_high) * quarter, quarter, 1)
    out_send = out_kept.astype(jnp.float32) + far_swap(out_given).astype(jnp.float32)
    out_send = out_send.astype(jnp.bfloat16).reshape(-1, feat_width)
    if slab_dev == 2:
        own_late = after(stack_own[0], out_given)
        stack_own = (own_late,) + stack_own[1:]
        g_expert_gate, g_expert_up, g_expert_down = run_weights(bit_low, stack_own, stack_other)
    else:
        wide = [jnp.concatenate(pair, axis=0) for pair in zip(stack_own, stack_other)]
        g_expert_gate = matmul_at(wide[0], wide[3])[None]
        g_expert_up = matmul_at(wide[0], wide[4])[None]
        g_expert_down = matmul_at(wide[2], wide[1])[None]


    back_own = after(back_own, g_expert_gate, out_send)
    d_hidden_part = (matmul_at(slots_one, back_own) + d_hidden_shared).astype(jnp.bfloat16)
    out_own = exchange(after(out_send, d_hidden_part))
    early.start(d_hidden_part)
    kept = lax.dynamic_slice_in_dim(d_hidden_part, bit_low * half_rows, half_rows, 0)
    given = lax.dynamic_slice_in_dim(d_hidden_part, (1 - bit_low) * half_rows, half_rows, 0)
    d_hidden_half = pair_of_halves(kept, given).astype(jnp.bfloat16)
    d_hidden_other = core_swap(d_hidden_half)
    dg_lines = back_own.reshape(group_count, block, feat_width)[:, half_slots, :384]
    dg_lines = dg_lines.reshape(group_count, 3, 128)[:, :, :block]
    dg_of = jnp.einsum("dps,dsr->dpr", dg_lines, slots_cube, preferred_element_type=jnp.float32)
    dg_of = jnp.sum(dg_of, axis=1)
    dg_part = jnp.stack(
        [jnp.sum(first_here * dg_of, axis=0), jnp.sum(second_here * dg_of, axis=0)], axis=0
    )
    dg_part = jnp.pad(dg_part, ((0, 6), (0, 0)))
    dg_part = dg_part + core_swap(dg_part)
    dg_part = dg_part + far_swap(dg_part)
    early.end(d_hidden_half, dg_part)
    early.start()

    d_resid, d_proj, g_ffn_gain, g_router, late, term = run_back_near(
        turn,
        d_hidden_half,
        d_hidden_other,
        dg_part,
        gate_weights,
        one_of,
        two_of,
        router_rows,
        resid_two,
        hidden_two,
        grouped_cot,
        gain_two,
        hidden_one,
        near_mixed,
        seq_start,
        cos_table,
        sin_table,
        near_lse,
        w_out,
        *near_heads,
        *near_weights,
    )
    late = GroupSum(late)
    late.start()
    early.advance(d_proj)
    ffn_rows = after(out_own, d_proj)
    ffn_given = (matmul_at(cot_pick_other, ffn_rows) + shared_other).astype(jnp.bfloat16)
    ffn_kept = (matmul_at(cot_pick_own, ffn_rows) + shared_own).astype(jnp.bfloat16)
    ffn_half = pair_of_halves(ffn_kept, ffn_given)
    output_send = (resid_half + ffn_half).astype(jnp.bfloat16)
    far_all = run_back_far(
        after(d_proj, ffn_given, ffn_kept),
        seq_start,
        cos_table,
        sin_table,
        far_lse,
        out_far,
        *far_heads,
    )
    late.advance(far_all)
    d_one_given, d_one_kept, d_resid_half = run_back_rows(
        after(far_all, output_send, late.part), d_resid, term, place_own, place_other, *far_weights
    )
    late.advance(d_one_given)
    early.advance(d_one_given)
    d_one = d_one_kept.astype(jnp.float32) + core_swap(d_one_given).astype(jnp.float32)
    resid = in_tokens.astype(jnp.float32)
    scale_one = rms_scale(resid)
    normed_one = resid * scale_one
    e_one = d_one * gain_one
    shift_one = jnp.mean(e_one * normed_one, axis=-1, keepdims=True)
    d_tokens_send = (d_resid_half + scale_one * (e_one - normed_one * shift_one)).astype(jnp.bfloat16)
    g_attn_gain = jnp.sum(d_one * normed_one, axis=0, keepdims=True)
    both_send = jnp.concatenate(
        [
            d_tokens_send.reshape(group_count, half_share, feat_width),
            output_send.reshape(group_count, half_share, feat_width),
        ],
        axis=1,
    )
    both_own = exchange(both_send)
    both_other = core_swap(both_own)

    unsend = (send_slot[:, None] == row_ids[None, :]).astype(jnp.bfloat16)

    def arrive_back(part):
        own = both_own[:, part].reshape(half_rows, feat_width)
        other = both_other[:, part].reshape(half_rows, feat_width)
        return select(unsend, in_order(bit_low, own, other))

    g_attn_gain = g_attn_gain + core_swap(g_attn_gain)
    small = jnp.concatenate([g_router, g_ffn_gain, g_attn_gain], axis=0)
    small = jnp.pad(small, ((0, -small.shape[0] % 8), (0, 0)))
    for step in range(group_count.bit_length() - 1):
        small = small + group_swap(small, step)
    g_router = small[:EXPERTS].T
    g_ffn_gain = small[EXPERTS]
    g_attn_gain = small[EXPERTS + 1]
    late = late.finish(both_send).astype(jnp.float32)
    shared = early.finish(both_send).astype(jnp.float32)
    hidden_s = shared_gate.shape[1]
    g_shared_gate = shared[:hidden_s].T
    g_shared_up = shared[hidden_s : 2 * hidden_s].T
    g_shared_down = shared[2 * hidden_s :]
    head_rows = w_out.shape[0]
    g_query = late[:head_rows].T
    g_key = late[head_rows : 2 * head_rows].T
    g_value = late[2 * head_rows : 3 * head_rows].T
    g_out = late[3 * head_rows :]
    d_tokens = arrive_back(slice(0, half_share))
    output = arrive_back(slice(half_share, 2 * half_share))
    return (
        output,
        d_tokens,
        g_attn_gain,
        g_query,
        g_key,
        g_value,
        g_out,
        g_ffn_gain,
        g_router,
        g_shared_gate,
        g_shared_up,
        g_shared_down,
        g_expert_gate,
        g_expert_up,
        g_expert_down,
    )


def solution(mesh):
    return jax.shard_map(
        body,
        mesh=mesh,
        in_specs=(
            P("expert", None),
            P(),
            P("expert", None),
            P("expert", None),
            P(),
            P(None, "tensor"),
            P(None, "tensor"),
            P(None, "tensor"),
            P("tensor", None),
            P(),
            P(),
            P(None, "tensor"),
            P(None, "tensor"),
            P("tensor", None),
            P("expert", None, "tensor"),
            P("expert", None, "tensor"),
            P("expert", "tensor", None),
            P("expert", None),
        ),
        out_specs=(
            P("expert", None),
            P("expert", None),
            P(),
            P(None, "tensor"),
            P(None, "tensor"),
            P(None, "tensor"),
            P("tensor", None),
            P(),
            P(),
            P(None, "tensor"),
            P(None, "tensor"),
            P("tensor", None),
            P("expert", None, "tensor"),
            P("expert", None, "tensor"),
            P("expert", "tensor", None),
        ),
        check_vma=False,
    )
```

time: 564 us -> 406 us (0.72)
  waiting for transfers between devices: 254 us -> 140 us
  Pallas kernels: 0 us -> 88.4 us
  matrix products: 130 us -> 42.5 us
  other arithmetic: 51.5 us -> 35 us
  between operations: 16.4 us -> 2.05 us
  local copies, waits for them, and re-layouts: 43.5 us -> 29.6 us
  starting transfers between devices: 52.6 us -> 63.8 us
  blocking collectives: 9.94 us -> 0 us
    all_to_all x9 -> x7, waiting for transfers between devices: 151 us -> 28.3 us  [exchange(): lax.all_to_all(values, 'expert', split_axis=0, concat_axis=0, tiled=True)]
    pallas_call x0 -> x9, Pallas kernels: none -> 88.4 us  [the longest x6 58.4 us: call_whole(): pl.pallas_call(kernel, grid_spec=pltpu.PrefetchScalarGridSpec(num_scalar_...]
    psum x1 -> x0, waiting for transfers between devices: 80.6 us -> none  [total_over_groups(): return lax.psum(wide, 'expert').astype(jnp.float32)]
    ppermute x0 -> x15, waiting for transfers between devices: none -> 79.1 us  [group_swap(): lax.ppermute(values, 'expert', [(i, i ^ 1 << step) for i in range(size)])]
    dot_general x27 -> x1, matrix products: 56.1 us -> 0.5 us  [body(): jnp.einsum('dps,dsr->dpr', dg_lines, slots_cube, preferred_element_type=j...]
    ppermute x0 -> x15, starting transfers between devices: none -> 16.7 us  [group_swap(): lax.ppermute(values, 'expert', [(i, i ^ 1 << step) for i in range(size)])]
    dot_general x12 -> x9, matrix products: 27.5 us -> 16.1 us  [matmul_at(): lax.dot_general(left_side, right_side, (((0,), (0,)), ((), ())), preferre...]
    all_to_all x1 -> x0, blocking collectives: 9.94 us -> none  [exchange(): lax.all_to_all(values, 'expert', split_axis=0, concat_axis=0, tiled=True)]
  transfers between devices with their start and end apart: 37 -> 48, of which waited for: 17 -> 22; matrix products, arithmetic and copies ran while one was open for 31% -> 20% of each run, Pallas kernels for 0% -> 20%
where the time goes in v2:
time: 406 us; the launch traced here: 401 us
  waiting for transfers between devices  140 us (34%)
  Pallas kernels  88.4 us (22%)
  starting transfers between devices  63.8 us (16%)
  matrix products  42.5 us (10%)
  other arithmetic  35 us (9%)
  local copies, waits for them, and re-layouts  29.6 us (7%)
    ppermute x15, waiting for transfers between devices, group_swap(): lax.ppermute(values, 'expert', [(i, i ^ 1 << step) for i in range(size)])  79.1 us
    pallas_call x6, Pallas kernels, call_whole(): pl.pallas_call(kernel, grid_spec=pltpu.PrefetchScalarGridSpec(num_scalar_...  58.4 us
    all_to_all x7, starting transfers between devices, exchange(): lax.all_to_all(values, 'expert', split_axis=0, concat_axis=0, tiled=True)  35.7 us
    all_to_all x7, waiting for transfers between devices, exchange(): lax.all_to_all(values, 'expert', split_axis=0, concat_axis=0, tiled=True)  28.3 us
    ppermute x9, waiting for transfers between devices, far_swap(): return lax.ppermute(values, 'tensor', [(i, i ^ 2) for i in range(4)])  23.5 us
    pallas_call x2, Pallas kernels, run_expert(): pl.pallas_call(functools.partial(expert_kernel, half_slots, block), grid_...  17.9 us
    ppermute x15, starting transfers between devices, group_swap(): lax.ppermute(values, 'expert', [(i, i ^ 1 << step) for i in range(size)])  16.7 us
    dot_general x9, matrix products, matmul_at(): lax.dot_general(left_side, right_side, (((0,), (0,)), ((), ())), preferre...  16.1 us
  transfers between devices with their start and end apart: 48, of which 22 were waited for; matrix products, arithmetic and copies ran while one was open for 20% of the time, Pallas kernels for 20%

profile of v2, /device:TPU:0, one launch (start us, length us, event | category | flops | bytes accessed | tf_op | source)
XLA Modules:
  0.0 400.8 jit_solution(15598746925055579373)
XLA Ops:
  4.1 7.4 %all-to-all-start = ((bf16[8,48,768]{2,1,0:T(8,128)(2,1)}), bf16[8,48,768]{2,1,0:T(8,128)(2,1)S(1)}, u32[]{:S(2)}, u32[]{:S(2)}) async-start(bf16[8,48,768]{2,1,0:T(8,128)(2,1)} %bitcast.5), calls=%async_computation | async-start | bytes 1179648 | tf_op jit(solution)/shard_map/all_to_all | solution.py:62
  17.9 2.5 fusion.81
  22.0 5.5 %all-to-all-done = bf16[8,48,768]{2,1,0:T(8,128)(2,1)S(1)} async-done(((bf16[8,48,768]{2,1,0:T(8,128)(2,1)}), bf16[8,48,768]{2,1,0:T(8,128)(2,1)S(1)}, u32[]{:S(2)}, u32[]{:S(2)}) %all-to-all-start) | async-done | bytes 589856 | tf_op jit(solution)/shard_map/all_to_all | solution.py:62
  27.4 3.8 all-to-all-start.1
  37.0 9.8 %attention_near.1 = (bf16[768,768]{1,0:T(8,128)(2,1)}, bf16[768,768]{1,0:T(8,128)(2,1)}, bf16[768,256]{1,0:T(8,128)(2,1)}, bf16[768,256]{1,0:T(8,128)(2,1)}, bf1...) custom-call(bf16[384,768]{1,0:T(8,128)(2,1)} %bitcast.159, bf16[384,768]{1,0:T(8,128)(2,1)} %copy-done.49, ...), custom_call_target="tpu_custom_call" | custom-call | flops 2415919104 | bytes 8752128 | tf_op jit(solution)/shard_map/attention_near/pallas_call | solution.py:464
  46.8 7.4 %attention_far.1 = (bf16[768,256]{1,0:T(8,128)(2,1)}, bf16[768,256]{1,0:T(8,128)(2,1)}, bf16[768,256]{1,0:T(8,128)(2,1)}, bf16[768,256]{1,0:T(8,128)(2,1)}, f32[768,128]{1,0:T(8,128)}) custom-call(bf16[768,768]{1,0:T(8,128)(2,1)} %get-tuple-element.85.hidden_ref, bf16[192,768]{1,0:T(8,128)(2,1)} %collective-permute-done.2.wq_ref, ...), custom_call_target="tpu_custom_call" | custom-call | flops 1509949440 | bytes 5210112 | tf_op jit(solution)/shard_map/attention_far/pallas_call | solution.py:464
  54.4 2.1 bitcast_compare_fusion
  61.6 6.0 %all-to-all-start.3 = ((bf16[8,64,768]{2,1,0:T(8,128)(2,1)}), bf16[8,64,768]{2,1,0:T(8,128)(2,1)S(1)}, u32[]{:S(2)}, u32[]{:S(2)}) async-start(bf16[8,64,768]{2,1,0:T(8,128)(2,1)} %bitcast.22), calls=%async_computation.3 | async-start | bytes 1572864 | tf_op jit(solution)/shard_map/all_to_all | solution.py:62
  67.6 8.1 %middle.1 = (f32[768,768]{1,0:T(8,128)}, bf16[768,768]{1,0:T(8,128)(2,1)}, bf16[1024,768]{1,0:T(8,128)(2,1)}, f32[8,768]{1,0:T(8,128)}) custom-call(s32[1]{0:T(128)} %bitcast.turn_ref, bf16[768,256]{1,0:T(8,128)(2,1)} %get-tuple-element.84.m0_ref.mixed_ref, bf16[768,256]{1,0:T(8,128)(2,1)} %collective-permute-done.1.m1_ref, ...), custom_call_target="tpu_custom_call" | custom-call | flops 2415919104 | bytes 10816512 | tf_op jit(solution)/shard_map/middle/pallas_call | solution.py:464
  82.0 6.1 %all-to-all-done.3 = bf16[8,64,768]{2,1,0:T(8,128)(2,1)S(1)} async-done(((bf16[8,64,768]{2,1,0:T(8,128)(2,1)}), bf16[8,64,768]{2,1,0:T(8,128)(2,1)S(1)}, u32[]{:S(2)}, u32[]{:S(2)}) %all-to-all-start.3) | async-done | bytes 786464 | tf_op jit(solution)/shard_map/all_to_all | solution.py:62
  88.1 4.8 %all-to-all-start.2 = ((bf16[8,128,768]{2,1,0:T(8,128)(2,1)}), bf16[8,128,768]{2,1,0:T(8,128)(2,1)}, u32[]{:S(2)}, u32[]{:S(2)}) async-start(bf16[8,128,768]{2,1,0:T(8,128)(2,1)} %bitcast.182), calls=%async_computation.2 | async-start | bytes 3145728 | tf_op jit(solution)/shard_map/all_to_all | solution.py:62
  93.0 3.7 multiply_convert_fusion.2
  109.5 13.2 %collective-permute-done.10 = bf16[8,64,768]{2,1,0:T(8,128)(2,1)S(1)} collective-permute-done((bf16[8,64,768]{2,1,0:T(8,128)(2,1)S(1)}, bf16[8,64,768]{2,1,0:T(8,128)(2,1)S(1)}, u32[]{:S(2)}, u32[]{:S(2)}) %collective-permute-start.10) | collective-permute-done | bytes 786464 | tf_op jit(solution)/shard_map/ppermute | solution.py:58
  124.5 5.1 %all-to-all-done.2 = bf16[8,128,768]{2,1,0:T(8,128)(2,1)} async-done(((bf16[8,128,768]{2,1,0:T(8,128)(2,1)}), bf16[8,128,768]{2,1,0:T(8,128)(2,1)}, u32[]{:S(2)}, u32[]{:S(2)}) %all-to-all-start.2) | async-done | bytes 1572896 | tf_op jit(solution)/shard_map/all_to_all | solution.py:62
  129.6 3.7 collective-permute-done.11.rows_ref.rows_other
  133.3 9.0 %expert_rows.3 = (bf16[1024,768]{1,0:T(8,128)(2,1)}, bf16[1024,768]{1,0:T(8,128)(2,1)}, bf16[1024,512]{1,0:T(8,128)(2,1)S(1)}, bf16[1024,512]{1,0:T(8,128)(2,1)S(1)}, bf16[1024,512]{1,0:T(8,128)(2,1)S(1)}) custom-call(s32[1]{0:T(128)} %bitcast.24.which_ref, bf16[1024,768]{1,0:T(8,128)(2,1)} %collective-permute-done.11.rows_ref.rows_other, ...), custom_call_target="tpu_custom_call" | custom-call | flops 4831838208 | bytes 11796480 | tf_op jit(solution)/shard_map/expert_rows/pallas_call | solution.py:224
  145.4 9.0 %expert_rows.2 = (bf16[1024,768]{1,0:T(8,128)(2,1)}, bf16[1024,768]{1,0:T(8,128)(2,1)}, bf16[1024,512]{1,0:T(8,128)(2,1)S(1)}, bf16[1024,512]{1,0:T(8,128)(2,1)S(1)}, bf16[1024,512]{1,0:T(8,128)(2,1)S(1)}) custom-call(s32[1]{0:T(128)} %bitcast.4.which_ref, bf16[1024,768]{1,0:T(8,128)(2,1)} %bitcast.19.rows_ref.rows_own, ...), custom_call_target="tpu_custom_call" | custom-call | flops 4831838208 | bytes 11796480 | tf_op jit(solution)/shard_map/expert_rows/pallas_call | solution.py:224
  154.5 3.0 convert_add_fusion
  159.7 4.6 %all-to-all-start.4 = ((bf16[8,128,768]{2,1,0:T(8,128)(2,1)}), bf16[8,128,768]{2,1,0:T(8,128)(2,1)}, u32[]{:S(2)}, u32[]{:S(2)}) async-start(bf16[8,128,768]{2,1,0:T(8,128)(2,1)} %bitcast.31), calls=%async_computation.4 | async-start | bytes 3145728 | tf_op jit(solution)/shard_map/all_to_all | solution.py:62
  170.7 2.2 fusion.129
  172.9 12.0 %expert_weights.1 = (f32[2,768,512]{2,1,0:T(8,128)}, f32[2,768,512]{2,1,0:T(8,128)}, f32[2,512,768]{2,1,0:T(8,128)}) custom-call(s32[1]{0:T(128)} %bitcast.33.which_ref, bf16[1024,768]{1,0:T(8,128)(2,1)} %bitcast.19.rows_ref.rows_own, bf16[1024,768]{1,0:T(8,128)(2,1)} %collective-permute-done.11.rows_ref.rows_other, ...), custom_call_target="tpu_custom_call" | custom-call | flops 4831838208 | bytes 22020096 | tf_op jit(solution)/shard_map/expert_weights/pallas_call | solution.py:294
  185.0 3.1 collective-permute-done.15
  188.1 2.2 add_convert_fusion.3
  190.3 11.6 %all-to-all-done.4 = bf16[8,128,768]{2,1,0:T(8,128)(2,1)} async-done(((bf16[8,128,768]{2,1,0:T(8,128)(2,1)}), bf16[8,128,768]{2,1,0:T(8,128)(2,1)}, u32[]{:S(2)}, u32[]{:S(2)}) %all-to-all-start.4) | async-done | bytes 1572896 | tf_op jit(solution)/shard_map/all_to_all | solution.py:62
  201.9 3.5 fusion.128
  207.4 2.1 constant_dynamic-slice_fusion.2
  209.4 2.3 collective-permute-done.16
  211.8 2.2 add_convert_fusion.8
  218.0 4.2 %all-to-all-start.5 = ((bf16[8,64,768]{2,1,0:T(8,128)(2,1)}), bf16[8,64,768]{2,1,0:T(8,128)(2,1)S(1)}, u32[]{:S(2)}, u32[]{:S(2)}) async-start(bf16[8,64,768]{2,1,0:T(8,128)(2,1)} %add_convert_fusion.3), calls=%async_computation.5 | async-start | bytes 1572864 | tf_op jit(solution)/shard_map/all_to_all | solution.py:62
  222.9 6.8 %collective-permute-done.17 = bf16[384,768]{1,0:T(8,128)(2,1)} collective-permute-done((bf16[384,768]{1,0:T(8,128)(2,1)}, bf16[384,768]{1,0:T(8,128)(2,1)}, u32[]{:S(2)}, u32[]{:S(2)}) %collective-permute-start.17) | collective-permute-done | bytes 589856 | tf_op jit(solution)/shard_map/ppermute | solution.py:58
  233.8 7.9 %collective-permute-done.36 = bf16[2,192,768]{2,1,0:T(8,128)(2,1)} collective-permute-done((bf16[2,192,768]{2,1,0:T(8,128)(2,1)S(1)}, bf16[2,192,768]{2,1,0:T(8,128)(2,1)}, u32[]{:S(2)}, u32[]{:S(2)}) %collective-permute-start.36) | collective-permute-done | bytes 589856 | tf_op jit(solution)/shard_map/ppermute | solution.py:99
  243.1 16.0 %back_near.1 = (f32[768,768]{1,0:T(8,128)}, bf16[768,768]{1,0:T(8,128)(2,1)}, f32[1,768]{1,0:T(1,128)}, f32[16,768]{1,0:T(8,128)}, bf16[768,768]{1,0:T(8,128)(2,1)}, /*index=5*/f32[768,768]{1,0:T(8,128)}) custom-call(s32[1]{0:T(128)} %bitcast.turn_ref, bf16[384,768]{1,0:T(8,128)(2,1)} %copy-done.34, bf16[384,768]{1,0:T(8,128)(2,1)} %copy-done.48, ...), custom_call_target="tpu_custom_call" | custom-call | flops 3925868544 | bytes 18708480 | tf_op jit(solution)/shard_map/back_near/pallas_call | solution.py:464
  259.2 2.7 fusion.22
  264.6 16.1 %collective-permute-done.37 = bf16[1,192,768]{2,1,0:T(8,128)(2,1)} collective-permute-done((bf16[1,192,768]{2,1,0:T(8,128)(2,1)}, bf16[1,192,768]{2,1,0:T(8,128)(2,1)}, u32[]{:S(2)}, u32[]{:S(2)}) %collective-permute-start.37) | collective-permute-done | bytes 294944 | tf_op jit(solution)/shard_map/ppermute | solution.py:99
  286.2 10.0 %back_far.1.all_ref = bf16[768,768]{1,0:T(8,128)(2,1)} custom-call(bf16[768,768]{1,0:T(8,128)(2,1)} %get-tuple-element.122.d_proj_ref, s32[768,128]{1,0:T(8,128)} %broadcast_in_dim.146.start_ref, f32[768,128]{1,0:T(8,128)} %get-tuple-element.240.cos_ref, f32[768,128]{1,0:T(8,128)} %get-tuple-element.239.sin_ref, f32[768,128]{1,0:T(8,128)} %get-tuple-element.123.lse_ref, ...), custom_call_target="tpu_custom_call" | custom-call | flops 1811939328 | bytes 5406720 | tf_op jit(solution)/shard_map/back_far/pallas_call | solution.py:464
  299.1 7.1 %back_rows.1 = (bf16[384,768]{1,0:T(8,128)(2,1)}, bf16[384,768]{1,0:T(8,128)(2,1)}, f32[384,768]{1,0:T(8,128)}) custom-call(bf16[768,768]{1,0:T(8,128)(2,1)} %back_far.1.all_ref, f32[768,768]{1,0:T(8,128)} %get-tuple-element.130.d_resid_ref, f32[768,768]{1,0:T(8,128)} %get-tuple-element.131.term_ref, bf16[768,384]{1,0:T(8,128)(2,1)} %get-tuple-element.251.place_own_ref, ...), custom_call_target="tpu_custom_call" | custom-call | flops 2717908992 | bytes 10321920 | tf_op jit(solution)/shard_map/back_rows/pallas_call | solution.py:464
  310.5 4.9 %all-to-all-start.6 = ((bf16[8,96,768]{2,1,0:T(8,128)(2,1)}), bf16[8,96,768]{2,1,0:T(8,128)(2,1)}, u32[]{:S(2)}, u32[]{:S(2)}) async-start(bf16[8,96,768]{2,1,0:T(8,128)(2,1)} %pad_maximum_fusion.1), calls=%async_computation.6 | async-start | bytes 2359296 | tf_op jit(solution)/shard_map/all_to_all | solution.py:62
  315.4 3.0 collective-permute-start.31
  318.5 4.0 %collective-permute-done.39 = bf16[2,192,768]{2,1,0:T(8,128)(2,1)S(1)} collective-permute-done((bf16[2,192,768]{2,1,0:T(8,128)(2,1)S(1)}, bf16[2,192,768]{2,1,0:T(8,128)(2,1)S(1)}, u32[]{:S(2)}, u32[]{:S(2)}) %collective-permute-start.39) | collective-permute-done | bytes 589856 | tf_op jit(solution)/shard_map/ppermute | solution.py:99
  322.8 4.9 %collective-permute-start.40 = (bf16[4,192,768]{2,1,0:T(8,128)(2,1)S(1)}, bf16[4,192,768]{2,1,0:T(8,128)(2,1)S(1)}, u32[]{:S(2)}, u32[]{:S(2)}) collective-permute-start(bf16[4,192,768]{2,1,0:T(8,128)(2,1)S(1)} %bitcast.172), channel_id=1, source_target_pairs={{0,4},{4,0},{8,12},{12,8},{16,20},{20,16},{24,28},{28,24},{1,5},{5... | collective-permute-start | bytes 3538952 | tf_op jit(solution)/shard_map/ppermute | solution.py:99
  327.8 22.7 %collective-permute-done.31 = bf16[1,96,768]{2,1,0:T(8,128)(2,1)S(1)} collective-permute-done((bf16[1,96,768]{2,1,0:T(8,128)(2,1)S(1)}, bf16[1,96,768]{2,1,0:T(8,128)(2,1)S(1)}, u32[]{:S(2)}, u32[]{:S(2)}) %collective-permute-start.31) | collective-permute-done | bytes 147488 | tf_op jit(solution)/shard_map/ppermute | solution.py:99
  352.2 10.1 %collective-permute-done.27 = f32[24,768]{1,0:T(8,128)S(1)} collective-permute-done((f32[24,768]{1,0:T(8,128)S(1)}, f32[24,768]{1,0:T(8,128)S(1)}, u32[]{:S(2)}, u32[]{:S(2)}) %collective-permute-start.27) | collective-permute-done | bytes 73760 | tf_op jit(solution)/shard_map/ppermute | solution.py:99
  362.5 2.1 collective-permute-start.33
  364.5 3.0 collective-permute-done.28
  368.2 5.4 %collective-permute-done.29 = f32[24,768]{1,0:T(8,128)S(1)} collective-permute-done((f32[24,768]{1,0:T(8,128)S(1)}, f32[24,768]{1,0:T(8,128)S(1)}, u32[]{:S(2)}, u32[]{:S(2)}) %collective-permute-start.29) | collective-permute-done | bytes 73760 | tf_op jit(solution)/shard_map/ppermute | solution.py:99
  381.4 8.6 %collective-permute-done.34 = bf16[4,96,768]{2,1,0:T(8,128)(2,1)} collective-permute-done((bf16[4,96,768]{2,1,0:T(8,128)(2,1)}, bf16[4,96,768]{2,1,0:T(8,128)(2,1)}, u32[]{:S(2)}, u32[]{:S(2)}) %collective-permute-start.34) | collective-permute-done | bytes 589856 | tf_op jit(solution)/shard_map/ppermute | solution.py:99
  396.0 2.3 fusion.14
  398.3 2.3 fusion.13
  (302 shorter events, 98.6 us)
Async XLA Ops:
  4.1 23.3 %all-to-all-start = ((bf16[8,48,768]{2,1,0:T(8,128)(2,1)}), bf16[8,48,768]{2,1,0:T(8,128)(2,1)S(1)}, u32[]{:S(2)}, u32[]{:S(2)}) async-start(bf16[8,48,768]{2,1,0:T(8,128)(2,1)} %bitcast.5), calls=%async_computation | async-start | bytes 1179648 | tf_op jit(solution)/shard_map/all_to_all | solution.py:62
  11.5 23.0 %collective-permute-start.3 = (bf16[192,768]{1,0:T(8,128)(2,1)S(1)}, bf16[192,768]{1,0:T(8,128)(2,1)}, u32[]{:S(2)}, u32[]{:S(2)}) collective-permute-start(bf16[192,768]{1,0:T(8,128)(2,1)S(1)} %bitcast.213), channel_id=1, source_target_pairs={{0,2},{1,3},{2,0},{3,1},{4,6},{5,7},{6,4},{7,5},{8,10},{9,11},{10,... | collective-permute-start | bytes 884744 | tf_op jit(solution)/shard_map/ppermute | solution.py:58
  13.1 33.7 %collective-permute-start.2 = (bf16[192,768]{1,0:T(8,128)(2,1)S(1)}, bf16[192,768]{1,0:T(8,128)(2,1)}, u32[]{:S(2)}, u32[]{:S(2)}) collective-permute-start(bf16[192,768]{1,0:T(8,128)(2,1)S(1)} %bitcast.210), channel_id=1, source_target_pairs={{0,2},{1,3},{2,0},{3,1},{4,6},{5,7},{6,4},{7,5},{8,10},{9,11},{10,... | collective-permute-start | bytes 884744 | tf_op jit(solution)/shard_map/ppermute | solution.py:58
  13.6 33.1 %collective-permute-start.4 = (bf16[192,768]{1,0:T(8,128)(2,1)}, bf16[192,768]{1,0:T(8,128)(2,1)}, u32[]{:S(2)}, u32[]{:S(2)}) collective-permute-start(bf16[192,768]{1,0:T(8,128)(2,1)} %bitcast.10.wv_ref), channel_id=1, source_target_pairs={{0,2},{1,3},{2,0},{3,1},{4,6},{5,7},{6,4},{7,5},{8,10},{9,11},{10,... | collective-permute-start | bytes 884744 | tf_op jit(solution)/shard_map/ppermute | solution.py:58
  15.1 52.5 %collective-permute-start.7 = (bf16[192,768]{1,0:T(8,128)(2,1)}, bf16[192,768]{1,0:T(8,128)(2,1)}, u32[]{:S(2)}, u32[]{:S(2)}) collective-permute-start(bf16[192,768]{1,0:T(8,128)(2,1)} %w_out_ref.1), channel_id=1, source_target_pairs={{0,1},{1,0},{2,3},{3,2},{4,5},{5,4},{6,7},{7,6},{8,9},{9,8},{10,11... | collective-permute-start | bytes 884744 | tf_op jit(solution)/shard_map/ppermute | solution.py:54
  27.4 26.7 %all-to-all-start.1 = ((bf16[8,48,768]{2,1,0:T(8,128)(2,1)}), bf16[8,48,768]{2,1,0:T(8,128)(2,1)S(1)}, u32[]{:S(2)}, u32[]{:S(2)}) async-start(bf16[8,48,768]{2,1,0:T(8,128)(2,1)} %bitcast.15), calls=%async_computation.1 | async-start | bytes 1179648 | tf_op jit(solution)/shard_map/all_to_all | solution.py:62
  31.9 4.1 %collective-permute-start = (bf16[384,768]{1,0:T(8,128)(2,1)S(1)}, bf16[384,768]{1,0:T(8,128)(2,1)S(1)}, u32[]{:S(2)}, u32[]{:S(2)}) collective-permute-start(bf16[384,768]{1,0:T(8,128)(2,1)S(1)} %bitcast.158), channel_id=1, source_target_pairs={{0,1},{1,0},{2,3},{3,2},{4,5},{5,4},{6,7},{7,6},{8,9},{9,8},{10,11... | collective-permute-start | bytes 1769480 | tf_op jit(solution)/shard_map/ppermute | solution.py:54
  34.5 23.2 %collective-permute-start.8 = (bf16[192,768]{1,0:T(8,128)(2,1)}, bf16[192,768]{1,0:T(8,128)(2,1)S(1)}, u32[]{:S(2)}, u32[]{:S(2)}) collective-permute-start(bf16[192,768]{1,0:T(8,128)(2,1)} %w_out_ref.1), channel_id=1, source_target_pairs={{0,2},{1,3},{2,0},{3,1},{4,6},{5,7},{6,4},{7,5},{8,10},{9,11},{10,... | collective-permute-start | bytes 884744 | tf_op jit(solution)/shard_map/ppermute | solution.py:58
  54.2 5.2 %collective-permute-start.6 = (bf16[384,768]{1,0:T(8,128)(2,1)S(1)}, bf16[384,768]{1,0:T(8,128)(2,1)S(1)}, u32[]{:S(2)}, u32[]{:S(2)}) collective-permute-start(bf16[384,768]{1,0:T(8,128)(2,1)S(1)} %bitcast.169), channel_id=1, source_target_pairs={{0,1},{1,0},{2,3},{3,2},{4,5},{5,4},{6,7},{7,6},{8,9},{9,8},{10,11... | collective-permute-start | bytes 1769480 | tf_op jit(solution)/shard_map/ppermute | solution.py:54
  57.7 9.9 %collective-permute-start.9 = (bf16[192,768]{1,0:T(8,128)(2,1)S(1)}, bf16[192,768]{1,0:T(8,128)(2,1)}, u32[]{:S(2)}, u32[]{:S(2)}) collective-permute-start(bf16[192,768]{1,0:T(8,128)(2,1)S(1)} %collective-permute-done.8.o2_ref.w_out_ref), channel_id=1, source_target_pairs={{0,1},{1,0},{2,3},{3,2},{4,5},{5,4},{6,7},{7,6},{8,9},{9,8},{10,11... | collective-permute-start | bytes 884744 | tf_op jit(solution)/shard_map/ppermute | solution.py:54
  58.1 2.8 collective-permute-start.5
  58.3 9.3 %collective-permute-start.1 = (bf16[768,256]{1,0:T(8,128)(2,1)}, bf16[768,256]{1,0:T(8,128)(2,1)}, u32[]{:S(2)}, u32[]{:S(2)}) collective-permute-start(bf16[768,256]{1,0:T(8,128)(2,1)} %get-tuple-element.84.m0_ref.mixed_ref), channel_id=1, source_target_pairs={{0,1},{1,0},{2,3},{3,2},{4,5},{5,4},{6,7},{7,6},{8,9},{9,8},{10,11... | collective-permute-start | bytes 1179656 | tf_op jit(solution)/shard_map/ppermute | solution.py:54
  61.6 26.5 %all-to-all-start.3 = ((bf16[8,64,768]{2,1,0:T(8,128)(2,1)}), bf16[8,64,768]{2,1,0:T(8,128)(2,1)S(1)}, u32[]{:S(2)}, u32[]{:S(2)}) async-start(bf16[8,64,768]{2,1,0:T(8,128)(2,1)} %bitcast.22), calls=%async_computation.3 | async-start | bytes 1572864 | tf_op jit(solution)/shard_map/all_to_all | solution.py:62
  88.1 41.5 %all-to-all-start.2 = ((bf16[8,128,768]{2,1,0:T(8,128)(2,1)}), bf16[8,128,768]{2,1,0:T(8,128)(2,1)}, u32[]{:S(2)}, u32[]{:S(2)}) async-start(bf16[8,128,768]{2,1,0:T(8,128)(2,1)} %bitcast.182), calls=%async_computation.2 | async-start | bytes 3145728 | tf_op jit(solution)/shard_map/all_to_all | solution.py:62
  104.0 18.6 %collective-permute-start.10 = (bf16[8,64,768]{2,1,0:T(8,128)(2,1)S(1)}, bf16[8,64,768]{2,1,0:T(8,128)(2,1)S(1)}, u32[]{:S(2)}, u32[]{:S(2)}) collective-permute-start(bf16[8,64,768]{2,1,0:T(8,128)(2,1)S(1)} %all-to-all-done.3), channel_id=1, source_target_pairs={{0,2},{1,3},{2,0},{3,1},{4,6},{5,7},{6,4},{7,5},{8,10},{9,11},{10,... | collective-permute-start | bytes 2359304 | tf_op jit(solution)/shard_map/ppermute | solution.py:58
  124.5 5.1 %collective-permute-start.12 = (bf16[1024,768]{1,0:T(8,128)(2,1)}, bf16[1024,768]{1,0:T(8,128)(2,1)S(1)}, u32[]{:S(2)}, u32[]{:S(2)}) collective-permute-start(bf16[1024,768]{1,0:T(8,128)(2,1)} %bitcast.23.cot_ref.cot_own), channel_id=1, source_target_pairs={{0,1},{1,0},{2,3},{3,2},{4,5},{5,4},{6,7},{7,6},{8,9},{9,8},{10,11... | collective-permute-start | bytes 4718600 | tf_op jit(solution)/shard_map/ppermute | solution.py:54
  129.6 3.8 collective-permute-start.11
  145.3 9.1 %collective-permute-start.13 = (bf16[1024,768]{1,0:T(8,128)(2,1)}, bf16[1024,768]{1,0:T(8,128)(2,1)S(1)}, u32[]{:S(2)}, u32[]{:S(2)}) collective-permute-start(bf16[1024,768]{1,0:T(8,128)(2,1)} %get-tuple-element.101), channel_id=1, source_target_pairs={{0,1},{1,0},{2,3},{3,2},{4,5},{5,4},{6,7},{7,6},{8,9},{9,8},{10,11... | collective-permute-start | bytes 4718600 | tf_op jit(solution)/shard_map/ppermute | solution.py:54
  159.3 5.0 %collective-permute-start.14 = (bf16[1024,768]{1,0:T(8,128)(2,1)}, bf16[1024,768]{1,0:T(8,128)(2,1)}, u32[]{:S(2)}, u32[]{:S(2)}) collective-permute-start(bf16[1024,768]{1,0:T(8,128)(2,1)} %get-tuple-element.104), channel_id=1, source_target_pairs={{0,1},{1,0},{2,3},{3,2},{4,5},{5,4},{6,7},{7,6},{8,9},{9,8},{10,11... | collective-permute-start | bytes 4718600 | tf_op jit(solution)/shard_map/ppermute | solution.py:54
  159.7 42.2 %all-to-all-start.4 = ((bf16[8,128,768]{2,1,0:T(8,128)(2,1)}), bf16[8,128,768]{2,1,0:T(8,128)(2,1)}, u32[]{:S(2)}, u32[]{:S(2)}) async-start(bf16[8,128,768]{2,1,0:T(8,128)(2,1)} %bitcast.31), calls=%async_computation.4 | async-start | bytes 3145728 | tf_op jit(solution)/shard_map/all_to_all | solution.py:62
  168.2 19.9 %collective-permute-start.15 = (bf16[8,64,768]{2,1,0:T(8,128)(2,1)}, bf16[8,64,768]{2,1,0:T(8,128)(2,1)}, u32[]{:S(2)}, u32[]{:S(2)}) collective-permute-start(bf16[8,64,768]{2,1,0:T(8,128)(2,1)} %constant_dynamic-slice_fusion.3), channel_id=1, source_target_pairs={{0,2},{1,3},{2,0},{3,1},{4,6},{5,7},{6,4},{7,5},{8,10},{9,11},{10,... | collective-permute-start | bytes 2359304 | tf_op jit(solution)/shard_map/ppermute | solution.py:58
  168.8 40.7 %collective-permute-start.35 = (bf16[4,192,768]{2,1,0:T(8,128)(2,1)}, bf16[4,192,768]{2,1,0:T(8,128)(2,1)}, u32[]{:S(2)}, u32[]{:S(2)}) collective-permute-start(bf16[4,192,768]{2,1,0:T(8,128)(2,1)} %dynamic-slice_bitcast_fusion), channel_id=1, source_target_pairs={{0,4},{4,0},{8,12},{12,8},{16,20},{20,16},{24,28},{28,24},{1,5},{5... | collective-permute-start | bytes 3538952 | tf_op jit(solution)/shard_map/ppermute | solution.py:99
  209.4 2.3 collective-permute-start.16
  214.0 15.7 %collective-permute-start.17 = (bf16[384,768]{1,0:T(8,128)(2,1)}, bf16[384,768]{1,0:T(8,128)(2,1)}, u32[]{:S(2)}, u32[]{:S(2)}) collective-permute-start(bf16[384,768]{1,0:T(8,128)(2,1)} %add_convert_fusion.8), channel_id=1, source_target_pairs={{0,2},{1,3},{2,0},{3,1},{4,6},{5,7},{6,4},{7,5},{8,10},{9,11},{10,... | collective-permute-start | bytes 1769480 | tf_op jit(solution)/shard_map/ppermute | solution.py:58
  217.1 24.6 %collective-permute-start.36 = (bf16[2,192,768]{2,1,0:T(8,128)(2,1)S(1)}, bf16[2,192,768]{2,1,0:T(8,128)(2,1)}, u32[]{:S(2)}, u32[]{:S(2)}) collective-permute-start(bf16[2,192,768]{2,1,0:T(8,128)(2,1)S(1)} %dynamic-slice_bitcast_fusion.1), channel_id=1, source_target_pairs={{0,8},{4,12},{8,0},{12,4},{16,24},{20,28},{24,16},{28,20},{1,9},{5... | collective-permute-start | bytes 1769480 | tf_op jit(solution)/shard_map/ppermute | solution.py:99
  218.0 41.2 %all-to-all-start.5 = ((bf16[8,64,768]{2,1,0:T(8,128)(2,1)}), bf16[8,64,768]{2,1,0:T(8,128)(2,1)S(1)}, u32[]{:S(2)}, u32[]{:S(2)}) async-start(bf16[8,64,768]{2,1,0:T(8,128)(2,1)} %add_convert_fusion.3), calls=%async_computation.5 | async-start | bytes 1572864 | tf_op jit(solution)/shard_map/all_to_all | solution.py:62
  231.0 11.3 %collective-permute-start.18 = (bf16[384,768]{1,0:T(8,128)(2,1)S(1)}, bf16[384,768]{1,0:T(8,128)(2,1)S(1)}, u32[]{:S(2)}, u32[]{:S(2)}) collective-permute-start(bf16[384,768]{1,0:T(8,128)(2,1)S(1)} %add_convert_fusion.7.dh_own_ref), channel_id=1, source_target_pairs={{0,1},{1,0},{2,3},{3,2},{4,5},{5,4},{6,7},{7,6},{8,9},{9,8},{10,11... | collective-permute-start | bytes 1769480 | tf_op jit(solution)/shard_map/ppermute | solution.py:54
  231.1 2.0 collective-permute-start.19
  233.2 8.5 %collective-permute-start.20 = (f32[8,768]{1,0:T(8,128)S(1)}, f32[8,768]{1,0:T(8,128)S(1)}, u32[]{:S(2)}, u32[]{:S(2)}) collective-permute-start(f32[8,768]{1,0:T(8,128)S(1)} %fusion.114), channel_id=1, source_target_pairs={{0,2},{1,3},{2,0},{3,1},{4,6},{5,7},{6,4},{7,5},{8,10},{9,11},{10,... | collective-permute-start | bytes 73736 | tf_op jit(solution)/shard_map/ppermute | solution.py:58
  261.9 20.0 %collective-permute-start.21 = (bf16[384,768]{1,0:T(8,128)(2,1)}, bf16[384,768]{1,0:T(8,128)(2,1)}, u32[]{:S(2)}, u32[]{:S(2)}) collective-permute-start(bf16[384,768]{1,0:T(8,128)(2,1)} %fusion.22), channel_id=1, source_target_pairs={{0,1},{1,0},{2,3},{3,2},{4,5},{5,4},{6,7},{7,6},{8,9},{9,8},{10,11... | collective-permute-start | bytes 1769480 | tf_op jit(solution)/shard_map/ppermute | solution.py:54
  263.9 16.8 %collective-permute-start.37 = (bf16[1,192,768]{2,1,0:T(8,128)(2,1)}, bf16[1,192,768]{2,1,0:T(8,128)(2,1)}, u32[]{:S(2)}, u32[]{:S(2)}) collective-permute-start(bf16[1,192,768]{2,1,0:T(8,128)(2,1)} %constant_dynamic-slice_fusion), channel_id=1, source_target_pairs={{0,16},{4,20},{8,24},{12,28},{16,0},{20,4},{24,8},{28,12},{1,17},{... | collective-permute-start | bytes 884744 | tf_op jit(solution)/shard_map/ppermute | solution.py:99
  281.8 15.4 %collective-permute-start.23 = (bf16[4,96,768]{2,1,0:T(8,128)(2,1)S(1)}, bf16[4,96,768]{2,1,0:T(8,128)(2,1)S(1)}, u32[]{:S(2)}, u32[]{:S(2)}) collective-permute-start(bf16[4,96,768]{2,1,0:T(8,128)(2,1)S(1)} %dynamic-slice_bitcast_fusion.2), channel_id=1, source_target_pairs={{0,4},{4,0},{8,12},{12,8},{16,20},{20,16},{24,28},{28,24},{1,5},{5... | collective-permute-start | bytes 1769480 | tf_op jit(solution)/shard_map/ppermute | solution.py:99
  283.5 15.4 %collective-permute-start.22 = (bf16[384,768]{1,0:T(8,128)(2,1)S(1)}, bf16[384,768]{1,0:T(8,128)(2,1)S(1)}, u32[]{:S(2)}, u32[]{:S(2)}) collective-permute-start(bf16[384,768]{1,0:T(8,128)(2,1)S(1)} %add_convert_fusion.6), channel_id=1, source_target_pairs={{0,2},{1,3},{2,0},{3,1},{4,6},{5,7},{6,4},{7,5},{8,10},{9,11},{10,... | collective-permute-start | bytes 1769480 | tf_op jit(solution)/shard_map/ppermute | solution.py:58
  286.1 20.2 %collective-permute-start.38 = (bf16[1,192,768]{2,1,0:T(8,128)(2,1)S(1)}, bf16[1,192,768]{2,1,0:T(8,128)(2,1)S(1)}, u32[]{:S(2)}, u32[]{:S(2)}) collective-permute-start(bf16[1,192,768]{2,1,0:T(8,128)(2,1)S(1)} %add_convert_fusion.9), channel_id=1, source_target_pairs={{0,16},{4,20},{8,24},{12,28},{16,0},{20,4},{24,8},{28,12},{1,17},{... | collective-permute-start | bytes 884744 | tf_op jit(solution)/shard_map/ppermute | solution.py:99
  297.4 9.9 %collective-permute-start.30 = (bf16[2,96,768]{2,1,0:T(8,128)(2,1)S(1)}, bf16[2,96,768]{2,1,0:T(8,128)(2,1)S(1)}, u32[]{:S(2)}, u32[]{:S(2)}) collective-permute-start(bf16[2,96,768]{2,1,0:T(8,128)(2,1)S(1)} %dynamic-slice_bitcast_fusion.3), channel_id=1, source_target_pairs={{0,8},{4,12},{8,0},{12,4},{16,24},{20,28},{24,16},{28,20},{1,9},{5... | collective-permute-start | bytes 884744 | tf_op jit(solution)/shard_map/ppermute | solution.py:99
  306.2 2.2 collective-permute-start.24
  306.3 16.2 %collective-permute-start.39 = (bf16[2,192,768]{2,1,0:T(8,128)(2,1)S(1)}, bf16[2,192,768]{2,1,0:T(8,128)(2,1)S(1)}, u32[]{:S(2)}, u32[]{:S(2)}) collective-permute-start(bf16[2,192,768]{2,1,0:T(8,128)(2,1)S(1)} %maximum_select_fusion.10), channel_id=1, source_target_pairs={{0,8},{4,12},{8,0},{12,4},{16,24},{20,28},{24,16},{28,20},{1,9},{5... | collective-permute-start | bytes 1769480 | tf_op jit(solution)/shard_map/ppermute | solution.py:99
  310.5 65.6 %all-to-all-start.6 = ((bf16[8,96,768]{2,1,0:T(8,128)(2,1)}), bf16[8,96,768]{2,1,0:T(8,128)(2,1)}, u32[]{:S(2)}, u32[]{:S(2)}) async-start(bf16[8,96,768]{2,1,0:T(8,128)(2,1)} %pad_maximum_fusion.1), calls=%async_computation.6 | async-start | bytes 2359296 | tf_op jit(solution)/shard_map/all_to_all | solution.py:62
  315.4 35.1 %collective-permute-start.31 = (bf16[1,96,768]{2,1,0:T(8,128)(2,1)S(1)}, bf16[1,96,768]{2,1,0:T(8,128)(2,1)S(1)}, u32[]{:S(2)}, u32[]{:S(2)}) collective-permute-start(bf16[1,96,768]{2,1,0:T(8,128)(2,1)S(1)} %constant_dynamic-slice_fusion.1), channel_id=1, source_target_pairs={{0,16},{4,20},{8,24},{12,28},{16,0},{20,4},{24,8},{28,12},{1,17},{... | collective-permute-start | bytes 442376 | tf_op jit(solution)/shard_map/ppermute | solution.py:99
  322.5 28.0 %collective-permute-start.26 = (f32[1,768]{1,0:T(1,128)S(1)}, f32[1,768]{1,0:T(1,128)S(1)}, u32[]{:S(2)}, u32[]{:S(2)}) collective-permute-start(f32[1,768]{1,0:T(1,128)S(1)} %broadcast_in_dim.153), channel_id=1, source_target_pairs={{0,1},{1,0},{2,3},{3,2},{4,5},{5,4},{6,7},{7,6},{8,9},{9,8},{10,11... | collective-permute-start | bytes 9224 | tf_op jit(solution)/shard_map/ppermute | solution.py:54
  322.8 53.0 %collective-permute-start.40 = (bf16[4,192,768]{2,1,0:T(8,128)(2,1)S(1)}, bf16[4,192,768]{2,1,0:T(8,128)(2,1)S(1)}, u32[]{:S(2)}, u32[]{:S(2)}) collective-permute-start(bf16[4,192,768]{2,1,0:T(8,128)(2,1)S(1)} %bitcast.172), channel_id=1, source_target_pairs={{0,4},{4,0},{8,12},{12,8},{16,20},{20,16},{24,28},{28,24},{1,5},{5... | collective-permute-start | bytes 3538952 | tf_op jit(solution)/shard_map/ppermute | solution.py:99
  350.6 11.8 %collective-permute-start.27 = (f32[24,768]{1,0:T(8,128)S(1)}, f32[24,768]{1,0:T(8,128)S(1)}, u32[]{:S(2)}, u32[]{:S(2)}) collective-permute-start(f32[24,768]{1,0:T(8,128)S(1)} %select_maximum_fusion), channel_id=1, source_target_pairs={{0,4},{4,0},{8,12},{12,8},{16,20},{20,16},{24,28},{28,24},{1,5},{5... | collective-permute-start | bytes 221192 | tf_op jit(solution)/shard_map/ppermute | solution.py:99
  352.2 10.3 %collective-permute-start.32 = (bf16[1,96,768]{2,1,0:T(8,128)(2,1)S(1)}, bf16[1,96,768]{2,1,0:T(8,128)(2,1)S(1)}, u32[]{:S(2)}, u32[]{:S(2)}) collective-permute-start(bf16[1,96,768]{2,1,0:T(8,128)(2,1)S(1)} %add_convert_fusion.10), channel_id=1, source_target_pairs={{0,16},{4,20},{8,24},{12,28},{16,0},{20,4},{24,8},{28,12},{1,17},{... | collective-permute-start | bytes 442376 | tf_op jit(solution)/shard_map/ppermute | solution.py:99
  362.3 5.2 %collective-permute-start.28 = (f32[24,768]{1,0:T(8,128)S(1)}, f32[24,768]{1,0:T(8,128)S(1)}, u32[]{:S(2)}, u32[]{:S(2)}) collective-permute-start(f32[24,768]{1,0:T(8,128)S(1)} %fusion.119), channel_id=1, source_target_pairs={{0,8},{4,12},{8,0},{12,4},{16,24},{20,28},{24,16},{28,20},{1,9},{5... | collective-permute-start | bytes 221192 | tf_op jit(solution)/shard_map/ppermute | solution.py:99
  362.5 12.4 %collective-permute-start.33 = (bf16[2,96,768]{2,1,0:T(8,128)(2,1)S(1)}, bf16[2,96,768]{2,1,0:T(8,128)(2,1)S(1)}, u32[]{:S(2)}, u32[]{:S(2)}) collective-permute-start(bf16[2,96,768]{2,1,0:T(8,128)(2,1)S(1)} %maximum_select_fusion.12), channel_id=1, source_target_pairs={{0,8},{4,12},{8,0},{12,4},{16,24},{20,28},{24,16},{28,20},{1,9},{5... | collective-permute-start | bytes 884744 | tf_op jit(solution)/shard_map/ppermute | solution.py:99
  367.6 6.0 %collective-permute-start.29 = (f32[24,768]{1,0:T(8,128)S(1)}, f32[24,768]{1,0:T(8,128)S(1)}, u32[]{:S(2)}, u32[]{:S(2)}) collective-permute-start(f32[24,768]{1,0:T(8,128)S(1)} %add.293), channel_id=1, source_target_pairs={{0,16},{4,20},{8,24},{12,28},{16,0},{20,4},{24,8},{28,12},{1,17},{... | collective-permute-start | bytes 221192 | tf_op jit(solution)/shard_map/ppermute | solution.py:99
  375.8 14.3 %collective-permute-start.34 = (bf16[4,96,768]{2,1,0:T(8,128)(2,1)}, bf16[4,96,768]{2,1,0:T(8,128)(2,1)}, u32[]{:S(2)}, u32[]{:S(2)}) collective-permute-start(bf16[4,96,768]{2,1,0:T(8,128)(2,1)} %bitcast.56), channel_id=1, source_target_pairs={{0,4},{4,0},{8,12},{12,8},{16,20},{20,16},{24,28},{28,24},{1,5},{5... | collective-permute-start | bytes 1769480 | tf_op jit(solution)/shard_map/ppermute | solution.py:99
  376.2 18.5 %collective-permute-start.25 = (bf16[8,96,768]{2,1,0:T(8,128)(2,1)}, bf16[8,96,768]{2,1,0:T(8,128)(2,1)}, u32[]{:S(2)}, u32[]{:S(2)}) collective-permute-start(bf16[8,96,768]{2,1,0:T(8,128)(2,1)} %all-to-all-done.6), channel_id=1, source_target_pairs={{0,1},{1,0},{2,3},{3,2},{4,5},{5,4},{6,7},{7,6},{8,9},{9,8},{10,11... | collective-permute-start | bytes 3538952 | tf_op jit(solution)/shard_map/ppermute | solution.py:54
  (56 other events, 332.2 us)

commit v3 on v2

--- a/solution.py
+++ b/solution.py
@@ -83,11 +83,8 @@
     return jnp.dot(onehot, values, preferred_element_type=jnp.float32).astype(jnp.bfloat16)
 
 
-def pair_of_halves(kept, given, meanwhile=lambda pair: None):
-    pair = (kept.astype(jnp.float32) + core_swap(given).astype(jnp.float32)).astype(jnp.bfloat16)
-    far = far_swap(pair)
-    meanwhile(pair)
-    return pair.astype(jnp.float32) + far.astype(jnp.float32)
+def pair_sum(kept, given):
+    return (kept.astype(jnp.float32) + core_swap(given).astype(jnp.float32)).astype(jnp.bfloat16)
 
 
 def after(values, *anchors):
@@ -100,50 +97,68 @@
 
 
 class GroupSum:
-    def __init__(self, values):
-        self.steps = lax.axis_size("expert").bit_length() - 1
+    def __init__(self, values, whole_last=False):
+        self.bits = lax.axis_size("expert").bit_length() - 1
+        self.steps = list(range(self.bits)) + list(reversed(range(self.bits)))
+        if whole_last:
+            self.steps[self.bits - 1 : self.bits + 1] = [self.bits - 1]
+        self.halvings = self.bits - 1 if whole_last else self.bits
+        self.whole_last = whole_last
         self.me = lax.axis_index("expert")
         self.shape = values.shape
-        self.part = values.astype(jnp.bfloat16).reshape(1 << self.steps, -1, values.shape[1])
+        pieces = 1 << self.halvings
+        self.part = values.astype(jnp.bfloat16).reshape(pieces, -1, values.shape[1])
         self.stage = 0
-        self.split()
-
-    def split(self):
-        bit = (self.me >> self.stage) & 1
-        pairs = self.part.reshape((-1, 2) + self.part.shape[1:])
-        self.kept = lax.dynamic_index_in_dim(pairs, bit, 1, keepdims=False)
-        self.given = lax.dynamic_index_in_dim(pairs, 1 - bit, 1, keepdims=False)
+        self.pending = False
+        self.prepare()
+
+    def prepare(self):
+        if self.stage < self.halvings:
+            bit = (self.me >> self.stage) & 1
+            pairs = self.part.reshape((-1, 2) + self.part.shape[1:])
+            self.kept = lax.dynamic_index_in_dim(pairs, bit, 1, keepdims=False)
+            self.given = lax.dynamic_index_in_dim(pairs, 1 - bit, 1, keepdims=False)
+        else:
+            self.kept = self.given = self.part
+
+    def start_first(self, share):
+        self.cut = self.given.shape[1] // share
+        self.first = group_swap(self.given[:, : self.cut], self.steps[self.stage])
+
+    def start_second(self, *anchors):
+        self.first, second = tie(self.first, self.given[:, self.cut :], *anchors)[:2]
+        self.second = group_swap(second, self.steps[self.stage])
+
+    def end_second(self, *anchors):
+        self.came = jnp.concatenate([self.first, after(self.second, *anchors)], axis=1)
+        self.end()
+
+    def done(self):
+        return self.stage == len(self.steps)
 
     def start(self, *anchors):
-        if self.stage < self.steps:
-            self.came = group_swap(after(self.given, *anchors), self.stage)
-        else:
-            step = 2 * self.steps - 1 - self.stage
-            self.came = group_swap(after(self.part, *anchors), step)
+        self.pending = True
+        self.came = group_swap(after(self.given, *anchors), self.steps[self.stage])
 
     def end(self, *anchors):
         came = after(self.came, *anchors)
-        if self.stage < self.steps:
+        self.pending = False
+        if self.stage < self.bits:
             total = self.kept.astype(jnp.float32) + came.astype(jnp.float32)
             self.part = total.astype(jnp.bfloat16)
-            self.stage += 1
-            if self.stage < self.steps:
-                self.split()
         else:
-            bit = (self.me >> (2 * self.steps - 1 - self.stage)) & 1
+            bit = (self.me >> self.steps[self.stage]) & 1
             both = in_order(bit, self.part[:, None], came[:, None], 1)
             self.part = both.reshape((-1,) + self.part.shape[1:])
-            self.stage += 1
-
-    def advance(self, *anchors):
-        self.end(*anchors)
-        self.start()
+        self.stage += 1
+        if not self.done():
+            self.prepare()
 
     def finish(self, *anchors):
-        while self.stage < 2 * self.steps:
+        while not self.done():
+            if not self.pending:
+                self.start()
             self.end(*anchors)
-            if self.stage < 2 * self.steps:
-                self.start()
         return self.part.reshape(self.shape)
 
 
@@ -1019,9 +1034,9 @@
     cot_other = core_swap(cot_own)
     grouped_cot = matmul(place_own, after(in_cot, sent)) + matmul(place_other, cot_half)
     grouped_cot = grouped_cot.astype(jnp.bfloat16)
-    hidden_late = hidden_two
-
-    gate_shared = matmul(hidden_late, shared_gate)
+    hidden_late = after(hidden_two, cot_part)
+
+    gate_shared = matmul(hidden_two, shared_gate)
     up_shared = matmul(hidden_late, shared_up)
     act_shared = silu_value(gate_shared)
     shared_mid = (act_shared * up_shared).astype(jnp.bfloat16)
@@ -1029,37 +1044,46 @@
     d_mid_shared = matmul_bt(grouped_cot, shared_down)
     d_up_shared = (d_mid_shared * act_shared).astype(jnp.bfloat16)
     d_gate_shared = (d_mid_shared * up_shared * silu_slope(gate_shared)).astype(jnp.bfloat16)
-    d_hidden_shared = matmul_bt(d_gate_shared, shared_gate) + matmul_bt(d_up_shared, shared_up)
     d_both = jnp.concatenate([d_gate_shared, d_up_shared], axis=1)
     early = GroupSum(
         jnp.concatenate([matmul_at(d_both, hidden_late), matmul_at(shared_mid, grouped_cot)], axis=0)
     )
+    early.start()
+    d_gate_shared, d_up_shared, shared_out, resid_late, _ = tie(
+        d_gate_shared, d_up_shared, shared_out, resid_two, early.given
+    )
+    d_hidden_shared = matmul_bt(d_gate_shared, shared_gate) + matmul_bt(d_up_shared, shared_up)
     shared_send = shared_out.astype(jnp.bfloat16)
     shared_own = matmul_at(place_own, shared_send)
     shared_other = matmul_at(place_other, shared_send)
-    resid_high, resid_low = three_parts(resid_two)[:2]
+    resid_high, resid_low = three_parts(resid_late)[:2]
     resid_half = matmul_at(place_own, resid_high) + matmul_at(place_own, resid_low)
-    hidden_rows = after(hidden_rows, early.given, shared_own, shared_other, resid_half)
+    hidden_rows = after(
+        hidden_rows, cot_other, d_hidden_shared, shared_own, shared_other, resid_half
+    )
+    rows_other = core_swap(hidden_rows)
+    early.end(d_hidden_shared, shared_own, shared_other, resid_half)
     early.start()
-
-    rows_other = core_swap(hidden_rows)
+    rows_other = after(rows_other, early.given)
+
     which_own = (bit_low * half_slots // CAP).reshape(1)
     which_other = ((1 - bit_low) * half_slots // CAP).reshape(1)
     weights_here = (expert_gate, expert_up, expert_down, half_slots, block)
+    back_given, out_given, mid_other, dg_other, du_other = run_expert(
+        which_other, rows_other, cot_other, *weights_here
+    )
+    early.end(back_given)
+    early.start()
+    back_given = after(back_given, early.given)
+    hidden_rows = after(hidden_rows, back_given)
     back_kept, out_kept, mid_own, dg_own, du_own = run_expert(
         which_own, hidden_rows, cot_own, *weights_here
     )
-    back_given, out_given, mid_other, dg_other, du_other = run_expert(
-        which_other, rows_other, cot_other, *weights_here
-    )
-    early.advance(back_given)
     stack_own = (hidden_rows, cot_own, mid_own, dg_own, du_own)
     stack_other = (rows_other, cot_other, mid_other, dg_other, du_other)
 
-    def pair_sum(kept, given):
-        return kept.astype(jnp.float32) + core_swap(given).astype(jnp.float32)
-
-    back_sum = pair_sum(back_kept, back_given).reshape(group_count, block, feat_width)
+    back_sum = back_kept.astype(jnp.float32) + core_swap(back_given).astype(jnp.float32)
+    back_sum = back_sum.reshape(group_count, block, feat_width)
     lines = back_sum[:, half_slots, :384].reshape(group_count, 3, 128)
     lines = jnp.stack(three_parts(jnp.sum(lines, axis=1)), axis=1).astype(jnp.float32)
     lines = jnp.pad(lines.reshape(group_count, 1, 384), ((0, 0), (0, 0), (0, feat_width - 384)))
@@ -1067,7 +1091,10 @@
     back_send = back_sum.astype(jnp.bfloat16).reshape(-1, feat_width)
     back_own = exchange(back_send)
     early.end(back_send)
-    out_sum = pair_sum(out_kept, after(out_given, back_send)).astype(jnp.bfloat16)
+    while early.stage < early.bits:
+        early.start()
+        early.end()
+    out_sum = pair_sum(out_kept, after(out_given, back_send, early.part))
     out_sum = out_sum.reshape(group_count, block, feat_width)
     out_kept = lax.dynamic_slice_in_dim(out_sum, bit_high * quarter, quarter, 1)
     out_given = lax.dynamic_slice_in_dim(out_sum, (1 - bit_high) * quarter, quarter, 1)
@@ -1086,12 +1113,8 @@
 
     back_own = after(back_own, g_expert_gate, out_send)
     d_hidden_part = (matmul_at(slots_one, back_own) + d_hidden_shared).astype(jnp.bfloat16)
-    out_own = exchange(after(out_send, d_hidden_part))
-    early.start(d_hidden_part)
     kept = lax.dynamic_slice_in_dim(d_hidden_part, bit_low * half_rows, half_rows, 0)
     given = lax.dynamic_slice_in_dim(d_hidden_part, (1 - bit_low) * half_rows, half_rows, 0)
-    d_hidden_half = pair_of_halves(kept, given).astype(jnp.bfloat16)
-    d_hidden_other = core_swap(d_hidden_half)
     dg_lines = back_own.reshape(group_count, block, feat_width)[:, half_slots, :384]
     dg_lines = dg_lines.reshape(group_count, 3, 128)[:, :, :block]
     dg_of = jnp.einsum("dps,dsr->dpr", dg_lines, slots_cube, preferred_element_type=jnp.float32)
@@ -1101,10 +1124,14 @@
     )
     dg_part = jnp.pad(dg_part, ((0, 6), (0, 0)))
     dg_part = dg_part + core_swap(dg_part)
-    dg_part = dg_part + far_swap(dg_part)
-    early.end(d_hidden_half, dg_part)
-    early.start()
-
+    pair = pair_sum(kept, given)
+    early.start(pair)
+    far, early.came, dg_far = tie(far_swap(pair), early.came, far_swap(dg_part))
+    d_hidden_half = (pair.astype(jnp.float32) + far.astype(jnp.float32)).astype(jnp.bfloat16)
+    early.end(d_hidden_half)
+    out_own = exchange(after(out_send, d_hidden_half))
+    d_hidden_other = core_swap(d_hidden_half)
+    dg_part = dg_part + dg_far
     d_resid, d_proj, g_ffn_gain, g_router, late, term = run_back_near(
         turn,
         d_hidden_half,
@@ -1128,16 +1155,17 @@
         *near_heads,
         *near_weights,
     )
-    late = GroupSum(late)
+    early.start(d_proj)
+    late = GroupSum(late, True)
     late.start()
-    early.advance(d_proj)
-    ffn_rows = after(out_own, d_proj)
+    ffn_rows = after(out_own, late.given)
     ffn_given = (matmul_at(cot_pick_other, ffn_rows) + shared_other).astype(jnp.bfloat16)
     ffn_kept = (matmul_at(cot_pick_own, ffn_rows) + shared_own).astype(jnp.bfloat16)
-    ffn_half = pair_of_halves(ffn_kept, ffn_given)
+    ffn_pair = pair_sum(ffn_kept, ffn_given)
+    ffn_half = ffn_pair.astype(jnp.float32) + far_swap(ffn_pair).astype(jnp.float32)
     output_send = (resid_half + ffn_half).astype(jnp.bfloat16)
     far_all = run_back_far(
-        after(d_proj, ffn_given, ffn_kept),
+        after(d_proj, ffn_pair),
         seq_start,
         cos_table,
         sin_table,
@@ -1145,12 +1173,22 @@
         out_far,
         *far_heads,
     )
-    late.advance(far_all)
+    late.end(far_all)
+    late.start()
+    early.end(far_all)
+    early.start_first(4)
     d_one_given, d_one_kept, d_resid_half = run_back_rows(
-        after(far_all, output_send, late.part), d_resid, term, place_own, place_other, *far_weights
-    )
-    late.advance(d_one_given)
-    early.advance(d_one_given)
+        after(far_all, output_send, late.given),
+        d_resid,
+        term,
+        place_own,
+        place_other,
+        *far_weights,
+    )
+    late.end(d_one_given)
+    late.start()
+    early.first, d_one_given = tie(early.first, d_one_given)
+    early.start_second()
     d_one = d_one_kept.astype(jnp.float32) + core_swap(d_one_given).astype(jnp.float32)
     resid = in_tokens.astype(jnp.float32)
     scale_one = rms_scale(resid)
@@ -1166,26 +1204,24 @@
         ],
         axis=1,
     )
-    both_own = exchange(both_send)
-    both_other = core_swap(both_own)
-
-    unsend = (send_slot[:, None] == row_ids[None, :]).astype(jnp.bfloat16)
-
-    def arrive_back(part):
-        own = both_own[:, part].reshape(half_rows, feat_width)
-        other = both_other[:, part].reshape(half_rows, feat_width)
-        return select(unsend, in_order(bit_low, own, other))
-
-    g_attn_gain = g_attn_gain + core_swap(g_attn_gain)
-    small = jnp.concatenate([g_router, g_ffn_gain, g_attn_gain], axis=0)
+    small = jnp.concatenate([g_router, g_ffn_gain, g_attn_gain + core_swap(g_attn_gain)], axis=0)
     small = jnp.pad(small, ((0, -small.shape[0] % 8), (0, 0)))
-    for step in range(group_count.bit_length() - 1):
+    late.end(both_send)
+    late.start()
+    late.end()
+    both_own = exchange(after(both_send, late.part))
+    small = after(small, late.part)
+    small = small + group_swap(small, 0)
+    late.start(small)
+    early.end_second(late.part)
+
+    for step in range(1, group_count.bit_length() - 1):
         small = small + group_swap(small, step)
     g_router = small[:EXPERTS].T
     g_ffn_gain = small[EXPERTS]
     g_attn_gain = small[EXPERTS + 1]
-    late = late.finish(both_send).astype(jnp.float32)
-    shared = early.finish(both_send).astype(jnp.float32)
+    late = late.finish().astype(jnp.float32)
+    shared = early.finish(late).astype(jnp.float32)
     hidden_s = shared_gate.shape[1]
     g_shared_gate = shared[:hidden_s].T
     g_shared_up = shared[hidden_s : 2 * hidden_s].T
@@ -1195,6 +1231,18 @@
     g_key = late[head_rows : 2 * head_rows].T
     g_value = late[2 * head_rows : 3 * head_rows].T
     g_out = late[3 * head_rows :]
+    both_own = after(
+        both_own, g_query, g_key, g_value, g_out, g_shared_gate, g_shared_up, g_shared_down, small
+    )
+    both_other = core_swap(both_own)
+
+    unsend = (send_slot[:, None] == row_ids[None, :]).astype(jnp.bfloat16)
+
+    def arrive_back(part):
+        own = both_own[:, part].reshape(half_rows, feat_width)
+        other = both_other[:, part].reshape(half_rows, feat_width)
+        return select(unsend, in_order(bit_low, own, other))
+
     d_tokens = arrive_back(slice(0, half_share))
     output = arrive_back(slice(half_share, 2 * half_share))
     return (

time: 406 us -> 380 us (0.936)
  waiting for transfers between devices: 140 us -> 113 us
  starting transfers between devices: 63.8 us -> 73.9 us
  local copies, waits for them, and re-layouts: 29.6 us -> 25.2 us
    ppermute x15, waiting for transfers between devices: 79.1 us -> 51.7 us  [group_swap(): lax.ppermute(values, 'expert', [(i, i ^ 1 << step) for i in range(size)])]
    ppermute x15, starting transfers between devices: 16.7 us -> 27 us  [group_swap(): lax.ppermute(values, 'expert', [(i, i ^ 1 << step) for i in range(size)])]
    ppermute x9, waiting for transfers between devices: 23.5 us -> 31.8 us  [far_swap(): return lax.ppermute(values, 'tensor', [(i, i ^ 2) for i in range(4)])]
    unnamed x115 -> x117, local copies, waits for them, and re-layouts: 12.5 us -> 10 us
  transfers between devices with their start and end apart: 48 -> 48, of which waited for: 22 -> 22; matrix products, arithmetic and copies ran while one was open for 20% -> 20% of each run, Pallas kernels for 20% -> 24%
where the time goes in v3:
time: 380 us; the launch traced here: 375 us
  waiting for transfers between devices  113 us (30%)
  Pallas kernels  88.5 us (23%)
  starting transfers between devices  73.9 us (19%)
  matrix products  38.5 us (10%)
  other arithmetic  33.5 us (9%)
  local copies, waits for them, and re-layouts  25.2 us (7%)
    pallas_call x6, Pallas kernels, call_whole(): pl.pallas_call(kernel, grid_spec=pltpu.PrefetchScalarGridSpec(num_scalar_...  58.2 us
    ppermute x15, waiting for transfers between devices, group_swap(): lax.ppermute(values, 'expert', [(i, i ^ 1 << step) for i in range(size)])  51.7 us
    all_to_all x7, starting transfers between devices, exchange(): lax.all_to_all(values, 'expert', split_axis=0, concat_axis=0, tiled=True)  35.3 us
    ppermute x9, waiting for transfers between devices, far_swap(): return lax.ppermute(values, 'tensor', [(i, i ^ 2) for i in range(4)])  31.8 us
    ppermute x15, starting transfers between devices, group_swap(): lax.ppermute(values, 'expert', [(i, i ^ 1 << step) for i in range(size)])  27 us
    all_to_all x7, waiting for transfers between devices, exchange(): lax.all_to_all(values, 'expert', split_axis=0, concat_axis=0, tiled=True)  24.5 us
    pallas_call x2, Pallas kernels, run_expert(): pl.pallas_call(functools.partial(expert_kernel, half_slots, block), grid_...  18.4 us
    dot_general x9, matrix products, matmul_at(): lax.dot_general(left_side, right_side, (((0,), (0,)), ((), ())), preferre...  15.1 us
  transfers between devices with their start and end apart: 48, of which 22 were waited for; matrix products, arithmetic and copies ran while one was open for 20% of the time, Pallas kernels for 24%

profile of v3, /device:TPU:0, one launch (start us, length us, event | category | flops | bytes accessed | tf_op | source)
XLA Modules:
  0.0 374.9 jit_solution(6525467011836230017)
XLA Ops:
  4.1 7.4 %all-to-all-start = ((bf16[8,48,768]{2,1,0:T(8,128)(2,1)}), bf16[8,48,768]{2,1,0:T(8,128)(2,1)S(1)}, u32[]{:S(2)}, u32[]{:S(2)}) async-start(bf16[8,48,768]{2,1,0:T(8,128)(2,1)} %bitcast.5), calls=%async_computation | async-start | bytes 1179648 | tf_op jit(solution)/shard_map/all_to_all | solution.py:62
  17.2 2.5 fusion.82
  22.6 4.8 %all-to-all-done = bf16[8,48,768]{2,1,0:T(8,128)(2,1)S(1)} async-done(((bf16[8,48,768]{2,1,0:T(8,128)(2,1)}), bf16[8,48,768]{2,1,0:T(8,128)(2,1)S(1)}, u32[]{:S(2)}, u32[]{:S(2)}) %all-to-all-start) | async-done | bytes 589856 | tf_op jit(solution)/shard_map/all_to_all | solution.py:62
  27.4 4.2 %all-to-all-start.1 = ((bf16[8,48,768]{2,1,0:T(8,128)(2,1)}), bf16[8,48,768]{2,1,0:T(8,128)(2,1)S(1)}, u32[]{:S(2)}, u32[]{:S(2)}) async-start(bf16[8,48,768]{2,1,0:T(8,128)(2,1)} %bitcast.15), calls=%async_computation.1 | async-start | bytes 1179648 | tf_op jit(solution)/shard_map/all_to_all | solution.py:62
  34.0 2.1 bitcast_compare_fusion
  38.6 9.8 %attention_near.1 = (bf16[768,768]{1,0:T(8,128)(2,1)}, bf16[768,768]{1,0:T(8,128)(2,1)}, bf16[768,256]{1,0:T(8,128)(2,1)}, bf16[768,256]{1,0:T(8,128)(2,1)}, bf1...) custom-call(bf16[384,768]{1,0:T(8,128)(2,1)} %bitcast.152, bf16[384,768]{1,0:T(8,128)(2,1)} %copy-done.51, ...), custom_call_target="tpu_custom_call" | custom-call | flops 2415919104 | bytes 8752128 | tf_op jit(solution)/shard_map/attention_near/pallas_call | solution.py:479
  48.4 7.4 %attention_far.1 = (bf16[768,256]{1,0:T(8,128)(2,1)}, bf16[768,256]{1,0:T(8,128)(2,1)}, bf16[768,256]{1,0:T(8,128)(2,1)}, bf16[768,256]{1,0:T(8,128)(2,1)}, f32[768,128]{1,0:T(8,128)}) custom-call(bf16[768,768]{1,0:T(8,128)(2,1)} %get-tuple-element.102.hidden_ref, bf16[192,768]{1,0:T(8,128)(2,1)} %collective-permute-done.2.wq_ref, ...), custom_call_target="tpu_custom_call" | custom-call | flops 1509949440 | bytes 5210112 | tf_op jit(solution)/shard_map/attention_far/pallas_call | solution.py:479
  59.7 6.0 %all-to-all-start.3 = ((bf16[8,64,768]{2,1,0:T(8,128)(2,1)}), bf16[8,64,768]{2,1,0:T(8,128)(2,1)}, u32[]{:S(2)}, u32[]{:S(2)}) async-start(bf16[8,64,768]{2,1,0:T(8,128)(2,1)} %bitcast.20), calls=%async_computation.3 | async-start | bytes 1572864 | tf_op jit(solution)/shard_map/all_to_all | solution.py:62
  67.3 8.1 %middle.1 = (f32[768,768]{1,0:T(8,128)}, bf16[768,768]{1,0:T(8,128)(2,1)}, bf16[1024,768]{1,0:T(8,128)(2,1)}, f32[8,768]{1,0:T(8,128)}) custom-call(s32[1]{0:T(128)} %bitcast.turn_ref, bf16[768,256]{1,0:T(8,128)(2,1)} %get-tuple-element.101.m0_ref.mixed_ref, bf16[768,256]{1,0:T(8,128)(2,1)} %copy-done.53, bf16[768,256]{1,0:T(8,128)(2,1)} %get-tuple-element.106.m2_ref, ...), custom_call_target="tpu_custom_call" | custom-call | flops 2415919104 | bytes 10816512 | tf_op jit(solution)/shard_map/middle/pallas_call | solution.py:479
  79.2 7.0 %all-to-all-done.3 = bf16[8,64,768]{2,1,0:T(8,128)(2,1)} async-done(((bf16[8,64,768]{2,1,0:T(8,128)(2,1)}), bf16[8,64,768]{2,1,0:T(8,128)(2,1)}, u32[]{:S(2)}, u32[]{:S(2)}) %all-to-all-start.3) | async-done | bytes 786464 | tf_op jit(solution)/shard_map/all_to_all | solution.py:62
  86.2 4.6 %all-to-all-start.2 = ((bf16[8,128,768]{2,1,0:T(8,128)(2,1)}), bf16[8,128,768]{2,1,0:T(8,128)(2,1)}, u32[]{:S(2)}, u32[]{:S(2)}) async-start(bf16[8,128,768]{2,1,0:T(8,128)(2,1)} %bitcast.18), calls=%async_computation.2 | async-start | bytes 3145728 | tf_op jit(solution)/shard_map/all_to_all | solution.py:62
  90.9 2.3 fusion.127
  100.3 2.0 collective-permute-start.13
  103.0 12.7 %collective-permute-done.10 = bf16[8,64,768]{2,1,0:T(8,128)(2,1)S(1)} collective-permute-done((bf16[8,64,768]{2,1,0:T(8,128)(2,1)}, bf16[8,64,768]{2,1,0:T(8,128)(2,1)S(1)}, u32[]{:S(2)}, u32[]{:S(2)}) %collective-permute-start.10) | collective-permute-done | bytes 786464 | tf_op jit(solution)/shard_map/ppermute | solution.py:58
  115.7 3.1 maximum_select_fusion.1
  123.1 2.3 convolution_add_fusion
  127.6 8.2 %collective-permute-done.13 = bf16[4,192,768]{2,1,0:T(8,128)(2,1)} collective-permute-done((bf16[4,192,768]{2,1,0:T(8,128)(2,1)}, bf16[4,192,768]{2,1,0:T(8,128)(2,1)}, u32[]{:S(2)}, u32[]{:S(2)}) %collective-permute-start.13) | collective-permute-done | bytes 1179680 | tf_op jit(solution)/shard_map/ppermute | solution.py:96
  140.2 9.4 %expert_rows.2 = (bf16[1024,768]{1,0:T(8,128)(2,1)}, bf16[1024,768]{1,0:T(8,128)(2,1)}, bf16[1024,512]{1,0:T(8,128)(2,1)S(1)}, bf16[1024,512]{1,0:T(8,128)(2,1)S(1)}, bf16[1024,512]{1,0:T(8,128)(2,1)S(1)}) custom-call(s32[1]{0:T(128)} %bitcast.24.which_ref, bf16[1024,768]{1,0:T(8,128)(2,1)} %collective-permute-done.12.rows_ref.rows_other, ...), custom_call_target="tpu_custom_call" | custom-call | flops 4831838208 | bytes 11796480 | tf_op jit(solution)/shard_map/expert_rows/pallas_call | solution.py:239
  150.6 2.1 collective-permute-done.14
  153.8 4.8 %collective-permute-start.16 = (bf16[1,192,768]{2,1,0:T(8,128)(2,1)S(1)}, bf16[1,192,768]{2,1,0:T(8,128)(2,1)S(1)}, u32[]{:S(2)}, u32[]{:S(2)}) collective-permute-start(bf16[1,192,768]{2,1,0:T(8,128)(2,1)S(1)} %constant_dynamic-slice_fusion.3), channel_id=1, source_target_pairs={{0,16},{4,20},{8,24},{12,28},{16,0},{20,4},{24,8},{28,12},{1,17},{... | collective-permute-start | bytes 884744 | tf_op jit(solution)/shard_map/ppermute | solution.py:96
  158.6 8.9 %expert_rows.3 = (bf16[1024,768]{1,0:T(8,128)(2,1)}, bf16[1024,768]{1,0:T(8,128)(2,1)}, bf16[1024,512]{1,0:T(8,128)(2,1)S(1)}, bf16[1024,512]{1,0:T(8,128)(2,1)S(1)}, bf16[1024,512]{1,0:T(8,128)(2,1)S(1)}) custom-call(s32[1]{0:T(128)} %bitcast.4.which_ref, bf16[1024,768]{1,0:T(8,128)(2,1)} %bitcast.19.rows_ref.rows_own, ...), custom_call_target="tpu_custom_call" | custom-call | flops 4831838208 | bytes 11796480 | tf_op jit(solution)/shard_map/expert_rows/pallas_call | solution.py:239
  167.5 2.9 convert_add_fusion
  172.7 4.9 %all-to-all-start.4 = ((bf16[8,128,768]{2,1,0:T(8,128)(2,1)}), bf16[8,128,768]{2,1,0:T(8,128)(2,1)}, u32[]{:S(2)}, u32[]{:S(2)}) async-start(bf16[8,128,768]{2,1,0:T(8,128)(2,1)} %bitcast.35), calls=%async_computation.4 | async-start | bytes 3145728 | tf_op jit(solution)/shard_map/all_to_all | solution.py:62
  177.6 2.3 add_convert_fusion
  182.3 11.9 %expert_weights.1 = (f32[2,768,512]{2,1,0:T(8,128)}, f32[2,768,512]{2,1,0:T(8,128)}, f32[2,512,768]{2,1,0:T(8,128)}) custom-call(s32[1]{0:T(128)} %bitcast.37.which_ref, bf16[1024,768]{1,0:T(8,128)(2,1)} %bitcast.19.rows_ref.rows_own, bf16[1024,768]{1,0:T(8,128)(2,1)} %collective-permute-done.12.rows_ref.rows_other, ...), custom_call_target="tpu_custom_call" | custom-call | flops 4831838208 | bytes 22020096 | tf_op jit(solution)/shard_map/expert_weights/pallas_call | solution.py:309
  194.2 6.5 %collective-permute-done.18 = bf16[8,64,768]{2,1,0:T(8,128)(2,1)} collective-permute-done((bf16[8,64,768]{2,1,0:T(8,128)(2,1)}, bf16[8,64,768]{2,1,0:T(8,128)(2,1)}, u32[]{:S(2)}, u32[]{:S(2)}) %collective-permute-start.18) | collective-permute-done | bytes 786464 | tf_op jit(solution)/shard_map/ppermute | solution.py:58
  200.7 2.2 add_convert_fusion.3
  202.9 12.4 %all-to-all-done.4 = bf16[8,128,768]{2,1,0:T(8,128)(2,1)} async-done(((bf16[8,128,768]{2,1,0:T(8,128)(2,1)}), bf16[8,128,768]{2,1,0:T(8,128)(2,1)}, u32[]{:S(2)}, u32[]{:S(2)}) %all-to-all-start.4) | async-done | bytes 1572896 | tf_op jit(solution)/shard_map/all_to_all | solution.py:62
  215.3 4.1 %add_convert_fusion.1 = bf16[768,768]{1,0:T(8,128)(2,1)S(1)} fusion(f32[768,768]{1,0:T(8,128)} %convolution_add_fusion, pred[1024,768]{1,0:T(32,128)(4,1)} %get-tuple-element.269, bf16[1024,768]{1,0:T(8,128)(2,1)} %bitcast.36), kind=kOutput, calls=%fused_computation.14 | convolution fusion | flops 1209139200 | bytes 5898240 | tf_op jit(solution)/shard_map/dot_general | solution.py:35
  228.0 11.8 %collective-permute-done.23 = f32[8,768]{1,0:T(8,128)S(1)} collective-permute-done((f32[8,768]{1,0:T(8,128)S(1)}, f32[8,768]{1,0:T(8,128)S(1)}, u32[]{:S(2)}, u32[]{:S(2)}) %collective-permute-start.23) | collective-permute-done | bytes 24608 | tf_op jit(solution)/shard_map/ppermute | solution.py:58
  241.8 3.7 all-to-all-start.5
  248.4 16.1 %back_near.1 = (f32[768,768]{1,0:T(8,128)}, bf16[768,768]{1,0:T(8,128)(2,1)}, f32[1,768]{1,0:T(1,128)}, f32[16,768]{1,0:T(8,128)}, bf16[768,768]{1,0:T(8,128)(2,1)}, /*index=5*/f32[768,768]{1,0:T(8,128)}) custom-call(s32[1]{0:T(128)} %bitcast.turn_ref, bf16[384,768]{1,0:T(8,128)(2,1)} %copy-done.31, bf16[384,768]{1,0:T(8,128)(2,1)} %copy-done.52, ...), custom_call_target="tpu_custom_call" | custom-call | flops 3925868544 | bytes 18708480 | tf_op jit(solution)/shard_map/back_near/pallas_call | solution.py:479
  264.5 2.0 dynamic-slice_bitcast_fusion.1
  268.1 2.1 collective-permute-start.27
  275.0 9.7 %back_far.1.all_ref = bf16[768,768]{1,0:T(8,128)(2,1)} custom-call(bf16[768,768]{1,0:T(8,128)(2,1)} %get-tuple-element.154.d_proj_ref, s32[768,128]{1,0:T(8,128)} %broadcast_in_dim.143.start_ref, f32[768,128]{1,0:T(8,128)} %get-tuple-element.274.cos_ref, f32[768,128]{1,0:T(8,128)} %get-tuple-element.273.sin_ref, f32[768,128]{1,0:T(8,128)} %get-tuple-element.155.lse_ref, ...), custom_call_target="tpu_custom_call" | custom-call | flops 1811939328 | bytes 5406720 | tf_op jit(solution)/shard_map/back_far/pallas_call | solution.py:479
  289.7 7.2 %back_rows.1 = (bf16[384,768]{1,0:T(8,128)(2,1)}, bf16[384,768]{1,0:T(8,128)(2,1)}, f32[384,768]{1,0:T(8,128)}) custom-call(bf16[768,768]{1,0:T(8,128)(2,1)} %back_far.1.all_ref, f32[768,768]{1,0:T(8,128)} %get-tuple-element.161.d_resid_ref, f32[768,768]{1,0:T(8,128)} %get-tuple-element.162.term_ref, bf16[768,384]{1,0:T(8,128)(2,1)} %get-tuple-element.283.place_own_ref, ...), custom_call_target="tpu_custom_call" | custom-call | flops 2717908992 | bytes 10321920 | tf_op jit(solution)/shard_map/back_rows/pallas_call | solution.py:479
  297.8 2.4 collective-permute-start.32
  302.9 11.2 %collective-permute-done.32 = bf16[1,192,768]{2,1,0:T(8,128)(2,1)S(1)} collective-permute-done((bf16[1,192,768]{2,1,0:T(8,128)(2,1)S(1)}, bf16[1,192,768]{2,1,0:T(8,128)(2,1)S(1)}, u32[]{:S(2)}, u32[]{:S(2)}) %collective-permute-start.32) | collective-permute-done | bytes 294944 | tf_op jit(solution)/shard_map/ppermute | solution.py:96
  315.9 7.7 %collective-permute-done.33 = bf16[1,192,768]{2,1,0:T(8,128)(2,1)S(1)} collective-permute-done((bf16[1,192,768]{2,1,0:T(8,128)(2,1)S(1)}, bf16[1,192,768]{2,1,0:T(8,128)(2,1)S(1)}, u32[]{:S(2)}, u32[]{:S(2)}) %collective-permute-start.33) | collective-permute-done | bytes 294944 | tf_op jit(solution)/shard_map/ppermute | solution.py:96
  324.6 4.5 %all-to-all-start.6 = ((bf16[8,96,768]{2,1,0:T(8,128)(2,1)}), bf16[8,96,768]{2,1,0:T(8,128)(2,1)}, u32[]{:S(2)}, u32[]{:S(2)}) async-start(bf16[8,96,768]{2,1,0:T(8,128)(2,1)} %pad_maximum_fusion.1), calls=%async_computation.6 | async-start | bytes 2359296 | tf_op jit(solution)/shard_map/all_to_all | solution.py:62
  329.1 2.0 collective-permute-start.35
  331.7 9.4 %collective-permute-done.35 = f32[24,768]{1,0:T(8,128)S(1)} collective-permute-done((f32[24,768]{1,0:T(8,128)}, f32[24,768]{1,0:T(8,128)S(1)}, u32[]{:S(2)}, u32[]{:S(2)}) %collective-permute-start.35) | collective-permute-done | bytes 73760 | tf_op jit(solution)/shard_map/ppermute | solution.py:96
  342.3 2.4 collective-permute-start.36
  345.2 5.3 %collective-permute-done.38 = f32[24,768]{1,0:T(8,128)S(1)} collective-permute-done((f32[24,768]{1,0:T(8,128)S(1)}, f32[24,768]{1,0:T(8,128)S(1)}, u32[]{:S(2)}, u32[]{:S(2)}) %collective-permute-start.38) | collective-permute-done | bytes 73760 | tf_op jit(solution)/shard_map/ppermute | solution.py:96
  350.5 4.1 %collective-permute-start.39 = (f32[24,768]{1,0:T(8,128)S(1)}, f32[24,768]{1,0:T(8,128)S(1)}, u32[]{:S(2)}, u32[]{:S(2)}) collective-permute-start(f32[24,768]{1,0:T(8,128)S(1)} %add.297), channel_id=1, source_target_pairs={{0,16},{4,20},{8,24},{12,28},{16,0},{20,4},{24,8},{28,12},{1,17},{... | collective-permute-start | bytes 221192 | tf_op jit(solution)/shard_map/ppermute | solution.py:96
  356.0 4.8 %collective-permute-done.39 = f32[24,768]{1,0:T(8,128)S(1)} collective-permute-done((f32[24,768]{1,0:T(8,128)S(1)}, f32[24,768]{1,0:T(8,128)S(1)}, u32[]{:S(2)}, u32[]{:S(2)}) %collective-permute-start.39) | collective-permute-done | bytes 73760 | tf_op jit(solution)/shard_map/ppermute | solution.py:96
  369.9 2.3 fusion.13
  372.3 2.3 fusion.14
  (305 shorter events, 95.0 us)
Async XLA Ops:
  4.1 23.3 %all-to-all-start = ((bf16[8,48,768]{2,1,0:T(8,128)(2,1)}), bf16[8,48,768]{2,1,0:T(8,128)(2,1)S(1)}, u32[]{:S(2)}, u32[]{:S(2)}) async-start(bf16[8,48,768]{2,1,0:T(8,128)(2,1)} %bitcast.5), calls=%async_computation | async-start | bytes 1179648 | tf_op jit(solution)/shard_map/all_to_all | solution.py:62
  11.5 36.9 %collective-permute-start.2 = (bf16[192,768]{1,0:T(8,128)(2,1)}, bf16[192,768]{1,0:T(8,128)(2,1)}, u32[]{:S(2)}, u32[]{:S(2)}) collective-permute-start(bf16[192,768]{1,0:T(8,128)(2,1)} %bitcast.8.wq_ref), channel_id=1, source_target_pairs={{0,2},{1,3},{2,0},{3,1},{4,6},{5,7},{6,4},{7,5},{8,10},{9,11},{10,... | collective-permute-start | bytes 884744 | tf_op jit(solution)/shard_map/ppermute | solution.py:58
  13.0 23.1 %collective-permute-start.3 = (bf16[192,768]{1,0:T(8,128)(2,1)}, bf16[192,768]{1,0:T(8,128)(2,1)}, u32[]{:S(2)}, u32[]{:S(2)}) collective-permute-start(bf16[192,768]{1,0:T(8,128)(2,1)} %bitcast.9.wk_ref), channel_id=1, source_target_pairs={{0,2},{1,3},{2,0},{3,1},{4,6},{5,7},{6,4},{7,5},{8,10},{9,11},{10,... | collective-permute-start | bytes 884744 | tf_op jit(solution)/shard_map/ppermute | solution.py:58
  13.5 34.8 %collective-permute-start.4 = (bf16[192,768]{1,0:T(8,128)(2,1)}, bf16[192,768]{1,0:T(8,128)(2,1)}, u32[]{:S(2)}, u32[]{:S(2)}) collective-permute-start(bf16[192,768]{1,0:T(8,128)(2,1)} %bitcast.10.wv_ref), channel_id=1, source_target_pairs={{0,2},{1,3},{2,0},{3,1},{4,6},{5,7},{6,4},{7,5},{8,10},{9,11},{10,... | collective-permute-start | bytes 884744 | tf_op jit(solution)/shard_map/ppermute | solution.py:58
  15.0 51.4 %collective-permute-start.7 = (bf16[192,768]{1,0:T(8,128)(2,1)}, bf16[192,768]{1,0:T(8,128)(2,1)}, u32[]{:S(2)}, u32[]{:S(2)}) collective-permute-start(bf16[192,768]{1,0:T(8,128)(2,1)} %w_out_ref.1), channel_id=1, source_target_pairs={{0,1},{1,0},{2,3},{3,2},{4,5},{5,4},{6,7},{7,6},{8,9},{9,8},{10,11... | collective-permute-start | bytes 884744 | tf_op jit(solution)/shard_map/ppermute | solution.py:54
  27.4 10.2 %collective-permute-start = (bf16[384,768]{1,0:T(8,128)(2,1)S(1)}, bf16[384,768]{1,0:T(8,128)(2,1)S(1)}, u32[]{:S(2)}, u32[]{:S(2)}) collective-permute-start(bf16[384,768]{1,0:T(8,128)(2,1)S(1)} %bitcast.151), channel_id=1, source_target_pairs={{0,1},{1,0},{2,3},{3,2},{4,5},{5,4},{6,7},{7,6},{8,9},{9,8},{10,11... | collective-permute-start | bytes 1769480 | tf_op jit(solution)/shard_map/ppermute | solution.py:54
  27.4 28.3 %all-to-all-start.1 = ((bf16[8,48,768]{2,1,0:T(8,128)(2,1)}), bf16[8,48,768]{2,1,0:T(8,128)(2,1)S(1)}, u32[]{:S(2)}, u32[]{:S(2)}) async-start(bf16[8,48,768]{2,1,0:T(8,128)(2,1)} %bitcast.15), calls=%async_computation.1 | async-start | bytes 1179648 | tf_op jit(solution)/shard_map/all_to_all | solution.py:62
  36.1 20.4 %collective-permute-start.8 = (bf16[192,768]{1,0:T(8,128)(2,1)}, bf16[192,768]{1,0:T(8,128)(2,1)}, u32[]{:S(2)}, u32[]{:S(2)}) collective-permute-start(bf16[192,768]{1,0:T(8,128)(2,1)} %w_out_ref.1), channel_id=1, source_target_pairs={{0,2},{1,3},{2,0},{3,1},{4,6},{5,7},{6,4},{7,5},{8,10},{9,11},{10,... | collective-permute-start | bytes 884744 | tf_op jit(solution)/shard_map/ppermute | solution.py:58
  55.7 2.5 collective-permute-start.6
  56.5 9.9 %collective-permute-start.9 = (bf16[192,768]{1,0:T(8,128)(2,1)}, bf16[192,768]{1,0:T(8,128)(2,1)S(1)}, u32[]{:S(2)}, u32[]{:S(2)}) collective-permute-start(bf16[192,768]{1,0:T(8,128)(2,1)} %collective-permute-done.8.o2_ref.w_out_ref), channel_id=1, source_target_pairs={{0,1},{1,0},{2,3},{3,2},{4,5},{5,4},{6,7},{7,6},{8,9},{9,8},{10,11... | collective-permute-start | bytes 884744 | tf_op jit(solution)/shard_map/ppermute | solution.py:54
  57.0 9.5 %collective-permute-start.1 = (bf16[768,256]{1,0:T(8,128)(2,1)}, bf16[768,256]{1,0:T(8,128)(2,1)S(1)}, u32[]{:S(2)}, u32[]{:S(2)}) collective-permute-start(bf16[768,256]{1,0:T(8,128)(2,1)} %get-tuple-element.101.m0_ref.mixed_ref), channel_id=1, source_target_pairs={{0,1},{1,0},{2,3},{3,2},{4,5},{5,4},{6,7},{7,6},{8,9},{9,8},{10,11... | collective-permute-start | bytes 1179656 | tf_op jit(solution)/shard_map/ppermute | solution.py:54
  57.1 9.3 %collective-permute-start.5 = (bf16[768,256]{1,0:T(8,128)(2,1)}, bf16[768,256]{1,0:T(8,128)(2,1)}, u32[]{:S(2)}, u32[]{:S(2)}) collective-permute-start(bf16[768,256]{1,0:T(8,128)(2,1)} %get-tuple-element.106.m2_ref), channel_id=1, source_target_pairs={{0,1},{1,0},{2,3},{3,2},{4,5},{5,4},{6,7},{7,6},{8,9},{9,8},{10,11... | collective-permute-start | bytes 1179656 | tf_op jit(solution)/shard_map/ppermute | solution.py:54
  59.7 26.5 %all-to-all-start.3 = ((bf16[8,64,768]{2,1,0:T(8,128)(2,1)}), bf16[8,64,768]{2,1,0:T(8,128)(2,1)}, u32[]{:S(2)}, u32[]{:S(2)}) async-start(bf16[8,64,768]{2,1,0:T(8,128)(2,1)} %bitcast.20), calls=%async_computation.3 | async-start | bytes 1572864 | tf_op jit(solution)/shard_map/all_to_all | solution.py:62
  86.2 41.2 %all-to-all-start.2 = ((bf16[8,128,768]{2,1,0:T(8,128)(2,1)}), bf16[8,128,768]{2,1,0:T(8,128)(2,1)}, u32[]{:S(2)}, u32[]{:S(2)}) async-start(bf16[8,128,768]{2,1,0:T(8,128)(2,1)} %bitcast.18), calls=%async_computation.2 | async-start | bytes 3145728 | tf_op jit(solution)/shard_map/all_to_all | solution.py:62
  96.9 18.8 %collective-permute-start.10 = (bf16[8,64,768]{2,1,0:T(8,128)(2,1)}, bf16[8,64,768]{2,1,0:T(8,128)(2,1)S(1)}, u32[]{:S(2)}, u32[]{:S(2)}) collective-permute-start(bf16[8,64,768]{2,1,0:T(8,128)(2,1)} %all-to-all-done.3), channel_id=1, source_target_pairs={{0,2},{1,3},{2,0},{3,1},{4,6},{5,7},{6,4},{7,5},{8,10},{9,11},{10,... | collective-permute-start | bytes 2359304 | tf_op jit(solution)/shard_map/ppermute | solution.py:58
  100.3 35.5 %collective-permute-start.13 = (bf16[4,192,768]{2,1,0:T(8,128)(2,1)}, bf16[4,192,768]{2,1,0:T(8,128)(2,1)}, u32[]{:S(2)}, u32[]{:S(2)}) collective-permute-start(bf16[4,192,768]{2,1,0:T(8,128)(2,1)} %dynamic-slice_bitcast_fusion), channel_id=1, source_target_pairs={{0,4},{4,0},{8,12},{12,8},{16,20},{20,16},{24,28},{28,24},{1,5},{5... | collective-permute-start | bytes 3538952 | tf_op jit(solution)/shard_map/ppermute | solution.py:96
  118.8 8.7 %collective-permute-start.11 = (bf16[1024,768]{1,0:T(8,128)(2,1)}, bf16[1024,768]{1,0:T(8,128)(2,1)}, u32[]{:S(2)}, u32[]{:S(2)}) collective-permute-start(bf16[1024,768]{1,0:T(8,128)(2,1)} %bitcast.21.cot_ref.cot_own), channel_id=1, source_target_pairs={{0,1},{1,0},{2,3},{3,2},{4,5},{5,4},{6,7},{7,6},{8,9},{9,8},{10,11... | collective-permute-start | bytes 4718600 | tf_op jit(solution)/shard_map/ppermute | solution.py:54
  127.4 12.7 %collective-permute-start.12 = (bf16[1024,768]{1,0:T(8,128)(2,1)}, bf16[1024,768]{1,0:T(8,128)(2,1)}, u32[]{:S(2)}, u32[]{:S(2)}) collective-permute-start(bf16[1024,768]{1,0:T(8,128)(2,1)} %bitcast.19.rows_ref.rows_own), channel_id=1, source_target_pairs={{0,1},{1,0},{2,3},{3,2},{4,5},{5,4},{6,7},{7,6},{8,9},{9,8},{10,11... | collective-permute-start | bytes 4718600 | tf_op jit(solution)/shard_map/ppermute | solution.py:54
  138.4 14.2 %collective-permute-start.14 = (bf16[2,192,768]{2,1,0:T(8,128)(2,1)S(1)}, bf16[2,192,768]{2,1,0:T(8,128)(2,1)S(1)}, u32[]{:S(2)}, u32[]{:S(2)}) collective-permute-start(bf16[2,192,768]{2,1,0:T(8,128)(2,1)S(1)} %dynamic-slice_bitcast_fusion.2), channel_id=1, source_target_pairs={{0,8},{4,12},{8,0},{12,4},{16,24},{20,28},{24,16},{28,20},{1,9},{5... | collective-permute-start | bytes 1769480 | tf_op jit(solution)/shard_map/ppermute | solution.py:96
  153.7 13.9 %collective-permute-start.15 = (bf16[1024,768]{1,0:T(8,128)(2,1)}, bf16[1024,768]{1,0:T(8,128)(2,1)S(1)}, u32[]{:S(2)}, u32[]{:S(2)}) collective-permute-start(bf16[1024,768]{1,0:T(8,128)(2,1)} %get-tuple-element.126), channel_id=1, source_target_pairs={{0,1},{1,0},{2,3},{3,2},{4,5},{5,4},{6,7},{7,6},{8,9},{9,8},{10,11... | collective-permute-start | bytes 4718600 | tf_op jit(solution)/shard_map/ppermute | solution.py:54
  153.8 18.8 %collective-permute-start.16 = (bf16[1,192,768]{2,1,0:T(8,128)(2,1)S(1)}, bf16[1,192,768]{2,1,0:T(8,128)(2,1)S(1)}, u32[]{:S(2)}, u32[]{:S(2)}) collective-permute-start(bf16[1,192,768]{2,1,0:T(8,128)(2,1)S(1)} %constant_dynamic-slice_fusion.3), channel_id=1, source_target_pairs={{0,16},{4,20},{8,24},{12,28},{16,0},{20,4},{24,8},{28,12},{1,17},{... | collective-permute-start | bytes 884744 | tf_op jit(solution)/shard_map/ppermute | solution.py:96
  172.6 5.0 %collective-permute-start.17 = (bf16[1024,768]{1,0:T(8,128)(2,1)}, bf16[1024,768]{1,0:T(8,128)(2,1)}, u32[]{:S(2)}, u32[]{:S(2)}) collective-permute-start(bf16[1024,768]{1,0:T(8,128)(2,1)} %get-tuple-element.132), channel_id=1, source_target_pairs={{0,1},{1,0},{2,3},{3,2},{4,5},{5,4},{6,7},{7,6},{8,9},{9,8},{10,11... | collective-permute-start | bytes 4718600 | tf_op jit(solution)/shard_map/ppermute | solution.py:54
  172.7 42.6 %all-to-all-start.4 = ((bf16[8,128,768]{2,1,0:T(8,128)(2,1)}), bf16[8,128,768]{2,1,0:T(8,128)(2,1)}, u32[]{:S(2)}, u32[]{:S(2)}) async-start(bf16[8,128,768]{2,1,0:T(8,128)(2,1)} %bitcast.35), calls=%async_computation.4 | async-start | bytes 3145728 | tf_op jit(solution)/shard_map/all_to_all | solution.py:62
  180.8 19.9 %collective-permute-start.18 = (bf16[8,64,768]{2,1,0:T(8,128)(2,1)}, bf16[8,64,768]{2,1,0:T(8,128)(2,1)}, u32[]{:S(2)}, u32[]{:S(2)}) collective-permute-start(bf16[8,64,768]{2,1,0:T(8,128)(2,1)} %constant_dynamic-slice_fusion.2), channel_id=1, source_target_pairs={{0,2},{1,3},{2,0},{3,1},{4,6},{5,7},{6,4},{7,5},{8,10},{9,11},{10,... | collective-permute-start | bytes 2359304 | tf_op jit(solution)/shard_map/ppermute | solution.py:58
  220.3 2.3 collective-permute-start.19
  223.8 17.8 %collective-permute-start.20 = (bf16[384,768]{1,0:T(8,128)(2,1)S(1)}, bf16[384,768]{1,0:T(8,128)(2,1)S(1)}, u32[]{:S(2)}, u32[]{:S(2)}) collective-permute-start(bf16[384,768]{1,0:T(8,128)(2,1)S(1)} %add_convert_fusion.8), channel_id=1, source_target_pairs={{0,2},{1,3},{2,0},{3,1},{4,6},{5,7},{6,4},{7,5},{8,10},{9,11},{10,... | collective-permute-start | bytes 1769480 | tf_op jit(solution)/shard_map/ppermute | solution.py:58
  226.0 15.7 %collective-permute-start.21 = (bf16[1,192,768]{2,1,0:T(8,128)(2,1)S(1)}, bf16[1,192,768]{2,1,0:T(8,128)(2,1)S(1)}, u32[]{:S(2)}, u32[]{:S(2)}) collective-permute-start(bf16[1,192,768]{2,1,0:T(8,128)(2,1)S(1)} %add_convert_fusion.11), channel_id=1, source_target_pairs={{0,16},{4,20},{8,24},{12,28},{16,0},{20,4},{24,8},{28,12},{1,17},{... | collective-permute-start | bytes 884744 | tf_op jit(solution)/shard_map/ppermute | solution.py:96
  226.1 1.3 collective-permute-start.22
  227.3 12.4 %collective-permute-start.23 = (f32[8,768]{1,0:T(8,128)S(1)}, f32[8,768]{1,0:T(8,128)S(1)}, u32[]{:S(2)}, u32[]{:S(2)}) collective-permute-start(f32[8,768]{1,0:T(8,128)S(1)} %fusion.115), channel_id=1, source_target_pairs={{0,2},{1,3},{2,0},{3,1},{4,6},{5,7},{6,4},{7,5},{8,10},{9,11},{10,... | collective-permute-start | bytes 73736 | tf_op jit(solution)/shard_map/ppermute | solution.py:58
  241.8 24.7 %all-to-all-start.5 = ((bf16[8,64,768]{2,1,0:T(8,128)(2,1)}), bf16[8,64,768]{2,1,0:T(8,128)(2,1)S(1)}, u32[]{:S(2)}, u32[]{:S(2)}) async-start(bf16[8,64,768]{2,1,0:T(8,128)(2,1)} %bitcast.42), calls=%async_computation.5 | async-start | bytes 1572864 | tf_op jit(solution)/shard_map/all_to_all | solution.py:62
  245.6 2.0 collective-permute-start.24
  267.8 5.0 %collective-permute-start.25 = (bf16[384,768]{1,0:T(8,128)(2,1)}, bf16[384,768]{1,0:T(8,128)(2,1)}, u32[]{:S(2)}, u32[]{:S(2)}) collective-permute-start(bf16[384,768]{1,0:T(8,128)(2,1)} %fusion.24), channel_id=1, source_target_pairs={{0,1},{1,0},{2,3},{3,2},{4,5},{5,4},{6,7},{7,6},{8,9},{9,8},{10,11... | collective-permute-start | bytes 1769480 | tf_op jit(solution)/shard_map/ppermute | solution.py:54
  268.1 16.6 %collective-permute-start.27 = (bf16[2,192,768]{2,1,0:T(8,128)(2,1)}, bf16[2,192,768]{2,1,0:T(8,128)(2,1)S(1)}, u32[]{:S(2)}, u32[]{:S(2)}) collective-permute-start(bf16[2,192,768]{2,1,0:T(8,128)(2,1)} %dynamic-slice_bitcast_fusion.1), channel_id=1, source_target_pairs={{0,4},{4,0},{8,12},{12,8},{16,20},{20,16},{24,28},{28,24},{1,5},{5... | collective-permute-start | bytes 1769480 | tf_op jit(solution)/shard_map/ppermute | solution.py:96
  270.1 15.4 %collective-permute-start.28 = (bf16[2,192,768]{2,1,0:T(8,128)(2,1)S(1)}, bf16[2,192,768]{2,1,0:T(8,128)(2,1)S(1)}, u32[]{:S(2)}, u32[]{:S(2)}) collective-permute-start(bf16[2,192,768]{2,1,0:T(8,128)(2,1)S(1)} %maximum_select_fusion.9), channel_id=1, source_target_pairs={{0,8},{4,12},{8,0},{12,4},{16,24},{20,28},{24,16},{28,20},{1,9},{5... | collective-permute-start | bytes 1769480 | tf_op jit(solution)/shard_map/ppermute | solution.py:96
  274.4 15.1 %collective-permute-start.26 = (bf16[384,768]{1,0:T(8,128)(2,1)S(1)}, bf16[384,768]{1,0:T(8,128)(2,1)S(1)}, u32[]{:S(2)}, u32[]{:S(2)}) collective-permute-start(bf16[384,768]{1,0:T(8,128)(2,1)S(1)} %add_convert_fusion.6), channel_id=1, source_target_pairs={{0,2},{1,3},{2,0},{3,1},{4,6},{5,7},{6,4},{7,5},{8,10},{9,11},{10,... | collective-permute-start | bytes 1769480 | tf_op jit(solution)/shard_map/ppermute | solution.py:58
  285.9 11.1 %collective-permute-start.29 = (bf16[4,48,768]{2,1,0:T(8,128)(2,1)S(1)}, bf16[4,48,768]{2,1,0:T(8,128)(2,1)S(1)}, u32[]{:S(2)}, u32[]{:S(2)}) collective-permute-start(bf16[4,48,768]{2,1,0:T(8,128)(2,1)S(1)} %slice.84), channel_id=1, source_target_pairs={{0,4},{4,0},{8,12},{12,8},{16,20},{20,16},{24,28},{28,24},{1,5},{5... | collective-permute-start | bytes 884744 | tf_op jit(solution)/shard_map/ppermute | solution.py:96
  287.2 10.5 %collective-permute-start.31 = (bf16[1,192,768]{2,1,0:T(8,128)(2,1)S(1)}, bf16[1,192,768]{2,1,0:T(8,128)(2,1)S(1)}, u32[]{:S(2)}, u32[]{:S(2)}) collective-permute-start(bf16[1,192,768]{2,1,0:T(8,128)(2,1)S(1)} %constant_dynamic-slice_fusion), channel_id=1, source_target_pairs={{0,8},{4,12},{8,0},{12,4},{16,24},{20,28},{24,16},{28,20},{1,9},{5... | collective-permute-start | bytes 884744 | tf_op jit(solution)/shard_map/ppermute | solution.py:96
  296.9 3.9 %collective-permute-start.30 = (bf16[384,768]{1,0:T(8,128)(2,1)}, bf16[384,768]{1,0:T(8,128)(2,1)S(1)}, u32[]{:S(2)}, u32[]{:S(2)}) collective-permute-start(bf16[384,768]{1,0:T(8,128)(2,1)} %get-tuple-element.170), channel_id=1, source_target_pairs={{0,1},{1,0},{2,3},{3,2},{4,5},{5,4},{6,7},{7,6},{8,9},{9,8},{10,11... | collective-permute-start | bytes 1769480 | tf_op jit(solution)/shard_map/ppermute | solution.py:54
  297.8 16.3 %collective-permute-start.32 = (bf16[1,192,768]{2,1,0:T(8,128)(2,1)S(1)}, bf16[1,192,768]{2,1,0:T(8,128)(2,1)S(1)}, u32[]{:S(2)}, u32[]{:S(2)}) collective-permute-start(bf16[1,192,768]{2,1,0:T(8,128)(2,1)S(1)} %add_convert_fusion.10), channel_id=1, source_target_pairs={{0,16},{4,20},{8,24},{12,28},{16,0},{20,4},{24,8},{28,12},{1,17},{... | collective-permute-start | bytes 884744 | tf_op jit(solution)/shard_map/ppermute | solution.py:96
  300.2 31.0 %collective-permute-start.37 = (bf16[4,144,768]{2,1,0:T(8,128)(2,1)S(1)}, bf16[4,144,768]{2,1,0:T(8,128)(2,1)S(1)}, u32[]{:S(2)}, u32[]{:S(2)}) collective-permute-start(bf16[4,144,768]{2,1,0:T(8,128)(2,1)S(1)} %slice.89), channel_id=1, source_target_pairs={{0,4},{4,0},{8,12},{12,8},{16,20},{20,16},{24,28},{28,24},{1,5},{5... | collective-permute-start | bytes 2654216 | tf_op jit(solution)/shard_map/ppermute | solution.py:96
  314.1 1.2 collective-permute-start.34
  314.2 9.5 %collective-permute-start.33 = (bf16[1,192,768]{2,1,0:T(8,128)(2,1)S(1)}, bf16[1,192,768]{2,1,0:T(8,128)(2,1)S(1)}, u32[]{:S(2)}, u32[]{:S(2)}) collective-permute-start(bf16[1,192,768]{2,1,0:T(8,128)(2,1)S(1)} %add_convert_fusion.9), channel_id=1, source_target_pairs={{0,8},{4,12},{8,0},{12,4},{16,24},{20,28},{24,16},{28,20},{1,9},{5... | collective-permute-start | bytes 884744 | tf_op jit(solution)/shard_map/ppermute | solution.py:96
  324.6 38.2 %all-to-all-start.6 = ((bf16[8,96,768]{2,1,0:T(8,128)(2,1)}), bf16[8,96,768]{2,1,0:T(8,128)(2,1)}, u32[]{:S(2)}, u32[]{:S(2)}) async-start(bf16[8,96,768]{2,1,0:T(8,128)(2,1)} %pad_maximum_fusion.1), calls=%async_computation.6 | async-start | bytes 2359296 | tf_op jit(solution)/shard_map/all_to_all | solution.py:62
  329.1 12.0 %collective-permute-start.35 = (f32[24,768]{1,0:T(8,128)}, f32[24,768]{1,0:T(8,128)S(1)}, u32[]{:S(2)}, u32[]{:S(2)}) collective-permute-start(f32[24,768]{1,0:T(8,128)} %select_maximum_fusion), channel_id=1, source_target_pairs={{0,4},{4,0},{8,12},{12,8},{16,20},{20,16},{24,28},{28,24},{1,5},{5... | collective-permute-start | bytes 221192 | tf_op jit(solution)/shard_map/ppermute | solution.py:96
  341.1 9.4 %collective-permute-start.38 = (f32[24,768]{1,0:T(8,128)S(1)}, f32[24,768]{1,0:T(8,128)S(1)}, u32[]{:S(2)}, u32[]{:S(2)}) collective-permute-start(f32[24,768]{1,0:T(8,128)S(1)} %add.296), channel_id=1, source_target_pairs={{0,8},{4,12},{8,0},{12,4},{16,24},{20,28},{24,16},{28,20},{1,9},{5... | collective-permute-start | bytes 221192 | tf_op jit(solution)/shard_map/ppermute | solution.py:96
  342.3 18.6 %collective-permute-start.36 = (bf16[2,192,768]{2,1,0:T(8,128)(2,1)S(1)}, bf16[2,192,768]{2,1,0:T(8,128)(2,1)S(1)}, u32[]{:S(2)}, u32[]{:S(2)}) collective-permute-start(bf16[2,192,768]{2,1,0:T(8,128)(2,1)S(1)} %copy-done.32), channel_id=1, source_target_pairs={{0,4},{4,0},{8,12},{12,8},{16,20},{20,16},{24,28},{28,24},{1,5},{5... | collective-permute-start | bytes 1769480 | tf_op jit(solution)/shard_map/ppermute | solution.py:96
  350.5 10.4 %collective-permute-start.39 = (f32[24,768]{1,0:T(8,128)S(1)}, f32[24,768]{1,0:T(8,128)S(1)}, u32[]{:S(2)}, u32[]{:S(2)}) collective-permute-start(f32[24,768]{1,0:T(8,128)S(1)} %add.297), channel_id=1, source_target_pairs={{0,16},{4,20},{8,24},{12,28},{16,0},{20,4},{24,8},{28,12},{1,17},{... | collective-permute-start | bytes 221192 | tf_op jit(solution)/shard_map/ppermute | solution.py:96
  362.8 5.8 %collective-permute-start.40 = (bf16[8,96,768]{2,1,0:T(8,128)(2,1)}, bf16[8,96,768]{2,1,0:T(8,128)(2,1)}, u32[]{:S(2)}, u32[]{:S(2)}) collective-permute-start(bf16[8,96,768]{2,1,0:T(8,128)(2,1)} %all-to-all-done.6), channel_id=1, source_target_pairs={{0,1},{1,0},{2,3},{3,2},{4,5},{5,4},{6,7},{7,6},{8,9},{9,8},{10,11... | collective-permute-start | bytes 3538952 | tf_op jit(solution)/shard_map/ppermute | solution.py:54
  (57 other events, 301.3 us)

commit v4 on v3

--- a/solution.py
+++ b/solution.py
@@ -1111,10 +1111,18 @@
         g_expert_down = matmul_at(wide[2], wide[1])[None]
 
 
-    back_own = after(back_own, g_expert_gate, out_send)
-    d_hidden_part = (matmul_at(slots_one, back_own) + d_hidden_shared).astype(jnp.bfloat16)
-    kept = lax.dynamic_slice_in_dim(d_hidden_part, bit_low * half_rows, half_rows, 0)
-    given = lax.dynamic_slice_in_dim(d_hidden_part, (1 - bit_low) * half_rows, half_rows, 0)
+    halves = [
+        tuple(
+            lax.dynamic_slice_in_dim(values, bit * half_rows, half_rows, axis)
+            for values, axis in ((slots_one, 1), (d_hidden_shared, 0))
+        )
+        for bit in (1 - bit_low, bit_low)
+    ]
+    back_own, *halves = tie(back_own, *halves, g_expert_gate, out_send)[:3]
+    given, kept = (
+        (matmul_at(slots, back_own) + shared).astype(jnp.bfloat16) for slots, shared in halves
+    )
+    kept = after(kept, given)
     dg_lines = back_own.reshape(group_count, block, feat_width)[:, half_slots, :384]
     dg_lines = dg_lines.reshape(group_count, 3, 128)[:, :, :block]
     dg_of = jnp.einsum("dps,dsr->dpr", dg_lines, slots_cube, preferred_element_type=jnp.float32)
@@ -1188,7 +1196,6 @@
     late.end(d_one_given)
     late.start()
     early.first, d_one_given = tie(early.first, d_one_given)
-    early.start_second()
     d_one = d_one_kept.astype(jnp.float32) + core_swap(d_one_given).astype(jnp.float32)
     resid = in_tokens.astype(jnp.float32)
     scale_one = rms_scale(resid)
@@ -1206,17 +1213,20 @@
     )
     small = jnp.concatenate([g_router, g_ffn_gain, g_attn_gain + core_swap(g_attn_gain)], axis=0)
     small = jnp.pad(small, ((0, -small.shape[0] % 8), (0, 0)))
-    late.end(both_send)
+    small = small + group_swap(small, 0)
+    early.start_second(small)
+    late.came, both_send, small_came = tie(late.came, both_send, group_swap(small, 1))
+    small = small + small_came
+    late.end()
     late.start()
+    late.came, small_came = tie(late.came, group_swap(small, 2))
+    small = small + small_came
+    for step in range(3, group_count.bit_length() - 1):
+        small = small + group_swap(small, step)
     late.end()
     both_own = exchange(after(both_send, late.part))
-    small = after(small, late.part)
-    small = small + group_swap(small, 0)
-    late.start(small)
+    late.start()
     early.end_second(late.part)
-
-    for step in range(1, group_count.bit_length() - 1):
-        small = small + group_swap(small, step)
     g_router = small[:EXPERTS].T
     g_ffn_gain = small[EXPERTS]
     g_attn_gain = small[EXPERTS + 1]

time: 380 us -> 370 us (0.974)
  waiting for transfers between devices: 113 us -> 108 us
    all_to_all x7, waiting for transfers between devices: 24.5 us -> 30.4 us  [exchange(): lax.all_to_all(values, 'expert', split_axis=0, concat_axis=0, tiled=True)]
    ppermute x15, waiting for transfers between devices: 51.7 us -> 46.9 us  [group_swap(): lax.ppermute(values, 'expert', [(i, i ^ 1 << step) for i in range(size)])]
    ppermute x9, waiting for transfers between devices: 31.8 us -> 27.2 us  [far_swap(): return lax.ppermute(values, 'tensor', [(i, i ^ 2) for i in range(4)])]
    ppermute x15, starting transfers between devices: 27 us -> 23.2 us  [group_swap(): lax.ppermute(values, 'expert', [(i, i ^ 1 << step) for i in range(size)])]
    dot_general x9 -> x10, matrix products: 15.1 us -> 11.6 us  [matmul_at(): lax.dot_general(left_side, right_side, (((0,), (0,)), ((), ())), preferre...]
    unnamed x117 -> x125, local copies, waits for them, and re-layouts: 10 us -> 11.4 us
  transfers between devices with their start and end apart: 48 -> 48, of which waited for: 22 -> 25; matrix products, arithmetic and copies ran while one was open for 20% -> 20% of each run, Pallas kernels for 24% -> 24%
where the time goes in v4:
time: 370 us; the launch traced here: 365 us
  waiting for transfers between devices  108 us (29%)
  Pallas kernels  88.5 us (24%)
  starting transfers between devices  70.6 us (19%)
  matrix products  36 us (10%)
  other arithmetic  32.9 us (9%)
  local copies, waits for them, and re-layouts  26.6 us (7%)
    pallas_call x6, Pallas kernels, call_whole(): pl.pallas_call(kernel, grid_spec=pltpu.PrefetchScalarGridSpec(num_scalar_...  58.2 us
    ppermute x15, waiting for transfers between devices, group_swap(): lax.ppermute(values, 'expert', [(i, i ^ 1 << step) for i in range(size)])  46.9 us
    all_to_all x7, starting transfers between devices, exchange(): lax.all_to_all(values, 'expert', split_axis=0, concat_axis=0, tiled=True)  35.4 us
    all_to_all x7, waiting for transfers between devices, exchange(): lax.all_to_all(values, 'expert', split_axis=0, concat_axis=0, tiled=True)  30.4 us
    ppermute x9, waiting for transfers between devices, far_swap(): return lax.ppermute(values, 'tensor', [(i, i ^ 2) for i in range(4)])  27.2 us
    ppermute x15, starting transfers between devices, group_swap(): lax.ppermute(values, 'expert', [(i, i ^ 1 << step) for i in range(size)])  23.2 us
    pallas_call x2, Pallas kernels, run_expert(): pl.pallas_call(functools.partial(expert_kernel, half_slots, block), grid_...  18.3 us
    pallas_call x1, Pallas kernels, run_weights(): pl.pallas_call(weight_kernel, grid_spec=pltpu.PrefetchScalarGridSpec(num_...  12 us
  transfers between devices with their start and end apart: 48, of which 25 were waited for; matrix products, arithmetic and copies ran while one was open for 20% of the time, Pallas kernels for 24%

profile of v4, /device:TPU:0, one launch (start us, length us, event | category | flops | bytes accessed | tf_op | source)
XLA Modules:
  0.0 365.2 jit_solution(17509038312264290324)
XLA Ops:
  4.1 7.4 %all-to-all-start = ((bf16[8,48,768]{2,1,0:T(8,128)(2,1)}), bf16[8,48,768]{2,1,0:T(8,128)(2,1)S(1)}, u32[]{:S(2)}, u32[]{:S(2)}) async-start(bf16[8,48,768]{2,1,0:T(8,128)(2,1)} %bitcast.3), calls=%async_computation | async-start | bytes 1179648 | tf_op jit(solution)/shard_map/all_to_all | solution.py:62
  17.3 2.5 fusion.83
  21.2 2.8 fusion.26
  24.0 3.5 all-to-all-done
  27.4 4.2 %all-to-all-start.1 = ((bf16[8,48,768]{2,1,0:T(8,128)(2,1)}), bf16[8,48,768]{2,1,0:T(8,128)(2,1)S(1)}, u32[]{:S(2)}, u32[]{:S(2)}) async-start(bf16[8,48,768]{2,1,0:T(8,128)(2,1)} %bitcast.13), calls=%async_computation.1 | async-start | bytes 1179648 | tf_op jit(solution)/shard_map/all_to_all | solution.py:62
  38.0 9.8 %attention_near.1 = (bf16[768,768]{1,0:T(8,128)(2,1)}, bf16[768,768]{1,0:T(8,128)(2,1)}, bf16[768,256]{1,0:T(8,128)(2,1)}, bf16[768,256]{1,0:T(8,128)(2,1)}, bf1...) custom-call(bf16[384,768]{1,0:T(8,128)(2,1)} %bitcast.156, bf16[384,768]{1,0:T(8,128)(2,1)} %copy-done.52, ...), custom_call_target="tpu_custom_call" | custom-call | flops 2415919104 | bytes 8752128 | tf_op jit(solution)/shard_map/attention_near/pallas_call | solution.py:479
  47.8 7.4 %attention_far.1 = (bf16[768,256]{1,0:T(8,128)(2,1)}, bf16[768,256]{1,0:T(8,128)(2,1)}, bf16[768,256]{1,0:T(8,128)(2,1)}, bf16[768,256]{1,0:T(8,128)(2,1)}, f32[768,128]{1,0:T(8,128)}) custom-call(bf16[768,768]{1,0:T(8,128)(2,1)} %get-tuple-element.109.hidden_ref, bf16[192,768]{1,0:T(8,128)(2,1)} %collective-permute-done.2.wq_ref, ...), custom_call_target="tpu_custom_call" | custom-call | flops 1509949440 | bytes 5210112 | tf_op jit(solution)/shard_map/attention_far/pallas_call | solution.py:479
  59.2 6.0 %all-to-all-start.3 = ((bf16[8,64,768]{2,1,0:T(8,128)(2,1)}), bf16[8,64,768]{2,1,0:T(8,128)(2,1)S(1)}, u32[]{:S(2)}, u32[]{:S(2)}) async-start(bf16[8,64,768]{2,1,0:T(8,128)(2,1)} %bitcast.20), calls=%async_computation.3 | async-start | bytes 1572864 | tf_op jit(solution)/shard_map/all_to_all | solution.py:62
  66.7 8.1 %middle.1 = (f32[768,768]{1,0:T(8,128)}, bf16[768,768]{1,0:T(8,128)(2,1)}, bf16[1024,768]{1,0:T(8,128)(2,1)}, f32[8,768]{1,0:T(8,128)}) custom-call(s32[1]{0:T(128)} %bitcast.turn_ref, bf16[768,256]{1,0:T(8,128)(2,1)} %get-tuple-element.108.m0_ref.mixed_ref, bf16[768,256]{1,0:T(8,128)(2,1)} %collective-permute-done.1.m1_ref, ...), custom_call_target="tpu_custom_call" | custom-call | flops 2415919104 | bytes 10816512 | tf_op jit(solution)/shard_map/middle/pallas_call | solution.py:479
  76.6 2.0 fusion.127
  78.6 7.0 %all-to-all-done.3 = bf16[8,64,768]{2,1,0:T(8,128)(2,1)S(1)} async-done(((bf16[8,64,768]{2,1,0:T(8,128)(2,1)}), bf16[8,64,768]{2,1,0:T(8,128)(2,1)S(1)}, u32[]{:S(2)}, u32[]{:S(2)}) %all-to-all-start.3) | async-done | bytes 786464 | tf_op jit(solution)/shard_map/all_to_all | solution.py:62
  85.6 4.6 %all-to-all-start.2 = ((bf16[8,128,768]{2,1,0:T(8,128)(2,1)}), bf16[8,128,768]{2,1,0:T(8,128)(2,1)}, u32[]{:S(2)}, u32[]{:S(2)}) async-start(bf16[8,128,768]{2,1,0:T(8,128)(2,1)} %bitcast.18), calls=%async_computation.2 | async-start | bytes 3145728 | tf_op jit(solution)/shard_map/all_to_all | solution.py:62
  90.3 2.3 fusion.128
  99.3 2.0 collective-permute-start.13
  102.1 12.8 %collective-permute-done.10 = bf16[8,64,768]{2,1,0:T(8,128)(2,1)S(1)} collective-permute-done((bf16[8,64,768]{2,1,0:T(8,128)(2,1)S(1)}, bf16[8,64,768]{2,1,0:T(8,128)(2,1)S(1)}, u32[]{:S(2)}, u32[]{:S(2)}) %collective-permute-start.10) | collective-permute-done | bytes 786464 | tf_op jit(solution)/shard_map/ppermute | solution.py:58
  114.9 1.8 maximum_select_fusion.1
  121.1 2.2 convolution_add_fusion
  126.8 8.3 %collective-permute-done.13 = bf16[4,192,768]{2,1,0:T(8,128)(2,1)} collective-permute-done((bf16[4,192,768]{2,1,0:T(8,128)(2,1)}, bf16[4,192,768]{2,1,0:T(8,128)(2,1)}, u32[]{:S(2)}, u32[]{:S(2)}) %collective-permute-start.13) | collective-permute-done | bytes 1179680 | tf_op jit(solution)/shard_map/ppermute | solution.py:96
  138.2 9.4 %expert_rows.2 = (bf16[1024,768]{1,0:T(8,128)(2,1)}, bf16[1024,768]{1,0:T(8,128)(2,1)}, bf16[1024,512]{1,0:T(8,128)(2,1)S(1)}, bf16[1024,512]{1,0:T(8,128)(2,1)S(1)}, bf16[1024,512]{1,0:T(8,128)(2,1)S(1)}) custom-call(s32[1]{0:T(128)} %bitcast.24.which_ref, bf16[1024,768]{1,0:T(8,128)(2,1)} %collective-permute-done.12.rows_ref.rows_other, ...), custom_call_target="tpu_custom_call" | custom-call | flops 4831838208 | bytes 11796480 | tf_op jit(solution)/shard_map/expert_rows/pallas_call | solution.py:239
  148.6 2.6 collective-permute-done.14
  151.5 4.3 %collective-permute-start.16 = (bf16[1,192,768]{2,1,0:T(8,128)(2,1)S(1)}, bf16[1,192,768]{2,1,0:T(8,128)(2,1)S(1)}, u32[]{:S(2)}, u32[]{:S(2)}) collective-permute-start(bf16[1,192,768]{2,1,0:T(8,128)(2,1)S(1)} %constant_dynamic-slice_fusion.6), channel_id=1, source_target_pairs={{0,16},{4,20},{8,24},{12,28},{16,0},{20,4},{24,8},{28,12},{1,17},{... | collective-permute-start | bytes 884744 | tf_op jit(solution)/shard_map/ppermute | solution.py:96
  155.8 8.9 %expert_rows.3 = (bf16[1024,768]{1,0:T(8,128)(2,1)}, bf16[1024,768]{1,0:T(8,128)(2,1)}, bf16[1024,512]{1,0:T(8,128)(2,1)S(1)}, bf16[1024,512]{1,0:T(8,128)(2,1)S(1)}, bf16[1024,512]{1,0:T(8,128)(2,1)S(1)}) custom-call(s32[1]{0:T(128)} %bitcast.2.which_ref, bf16[1024,768]{1,0:T(8,128)(2,1)} %bitcast.19.rows_ref.rows_own, ...), custom_call_target="tpu_custom_call" | custom-call | flops 4831838208 | bytes 11796480 | tf_op jit(solution)/shard_map/expert_rows/pallas_call | solution.py:239
  164.8 2.9 convert_add_fusion
  170.6 5.0 %all-to-all-start.4 = ((bf16[8,128,768]{2,1,0:T(8,128)(2,1)}), bf16[8,128,768]{2,1,0:T(8,128)(2,1)S(1)}, u32[]{:S(2)}, u32[]{:S(2)}) async-start(bf16[8,128,768]{2,1,0:T(8,128)(2,1)} %bitcast.35), calls=%async_computation.4 | async-start | bytes 3145728 | tf_op jit(solution)/shard_map/all_to_all | solution.py:62
  175.6 1.8 add_convert_fusion
  184.4 12.0 %expert_weights.1 = (f32[2,768,512]{2,1,0:T(8,128)}, f32[2,768,512]{2,1,0:T(8,128)}, f32[2,512,768]{2,1,0:T(8,128)}) custom-call(s32[1]{0:T(128)} %bitcast.37.which_ref, bf16[1024,768]{1,0:T(8,128)(2,1)} %bitcast.19.rows_ref.rows_own, bf16[1024,768]{1,0:T(8,128)(2,1)} %collective-permute-done.12.rows_ref.rows_other, ...), custom_call_target="tpu_custom_call" | custom-call | flops 4831838208 | bytes 22020096 | tf_op jit(solution)/shard_map/expert_weights/pallas_call | solution.py:309
  196.5 2.9 collective-permute-done.18
  199.4 2.2 add_convert_fusion.2
  201.6 11.6 %all-to-all-done.4 = bf16[8,128,768]{2,1,0:T(8,128)(2,1)S(1)} async-done(((bf16[8,128,768]{2,1,0:T(8,128)(2,1)}), bf16[8,128,768]{2,1,0:T(8,128)(2,1)S(1)}, u32[]{:S(2)}, u32[]{:S(2)}) %all-to-all-start.4) | async-done | bytes 1572896 | tf_op jit(solution)/shard_map/all_to_all | solution.py:62
  221.4 11.4 %collective-permute-done.23 = f32[8,768]{1,0:T(8,128)S(1)} collective-permute-done((f32[8,768]{1,0:T(8,128)S(1)}, f32[8,768]{1,0:T(8,128)S(1)}, u32[]{:S(2)}, u32[]{:S(2)}) %collective-permute-start.23) | collective-permute-done | bytes 24608 | tf_op jit(solution)/shard_map/ppermute | solution.py:58
  232.8 2.0 collective-permute-done.21
  235.0 3.7 %all-to-all-start.5 = ((bf16[8,64,768]{2,1,0:T(8,128)(2,1)}), bf16[8,64,768]{2,1,0:T(8,128)(2,1)S(1)}, u32[]{:S(2)}, u32[]{:S(2)}) async-start(bf16[8,64,768]{2,1,0:T(8,128)(2,1)} %bitcast.45), calls=%async_computation.5 | async-start | bytes 1572864 | tf_op jit(solution)/shard_map/all_to_all | solution.py:62
  241.6 16.1 %back_near.1 = (f32[768,768]{1,0:T(8,128)}, bf16[768,768]{1,0:T(8,128)(2,1)}, f32[1,768]{1,0:T(1,128)}, f32[16,768]{1,0:T(8,128)}, bf16[768,768]{1,0:T(8,128)(2,1)}, /*index=5*/f32[768,768]{1,0:T(8,128)}) custom-call(s32[1]{0:T(128)} %bitcast.turn_ref, bf16[384,768]{1,0:T(8,128)(2,1)} %copy-done.37, bf16[384,768]{1,0:T(8,128)(2,1)} %copy-done.53, ...), custom_call_target="tpu_custom_call" | custom-call | flops 3925868544 | bytes 18708480 | tf_op jit(solution)/shard_map/back_near/pallas_call | solution.py:479
  260.5 2.0 collective-permute-start.30
  265.3 9.7 %back_far.1.all_ref = bf16[768,768]{1,0:T(8,128)(2,1)} custom-call(bf16[768,768]{1,0:T(8,128)(2,1)} %get-tuple-element.166.d_proj_ref, s32[768,128]{1,0:T(8,128)} %broadcast_in_dim.141.start_ref, f32[768,128]{1,0:T(8,128)} %get-tuple-element.290.cos_ref, f32[768,128]{1,0:T(8,128)} %get-tuple-element.289.sin_ref, f32[768,128]{1,0:T(8,128)} %get-tuple-element.167.lse_ref, ...), custom_call_target="tpu_custom_call" | custom-call | flops 1811939328 | bytes 5406720 | tf_op jit(solution)/shard_map/back_far/pallas_call | solution.py:479
  276.7 1.8 collective-permute-start.31
  280.4 7.2 %back_rows.1 = (bf16[384,768]{1,0:T(8,128)(2,1)}, bf16[384,768]{1,0:T(8,128)(2,1)}, f32[384,768]{1,0:T(8,128)}) custom-call(bf16[768,768]{1,0:T(8,128)(2,1)} %back_far.1.all_ref, f32[768,768]{1,0:T(8,128)} %get-tuple-element.173.d_resid_ref, f32[768,768]{1,0:T(8,128)} %get-tuple-element.174.term_ref, bf16[768,384]{1,0:T(8,128)(2,1)} %get-tuple-element.299.place_own_ref, ...), custom_call_target="tpu_custom_call" | custom-call | flops 2717908992 | bytes 10321920 | tf_op jit(solution)/shard_map/back_rows/pallas_call | solution.py:479
  288.5 2.4 collective-permute-start.29
  294.3 2.9 collective-permute-done.34
  299.9 5.0 %collective-permute-done.29 = bf16[1,192,768]{2,1,0:T(8,128)(2,1)S(1)} collective-permute-done((bf16[1,192,768]{2,1,0:T(8,128)(2,1)S(1)}, bf16[1,192,768]{2,1,0:T(8,128)(2,1)S(1)}, u32[]{:S(2)}, u32[]{:S(2)}) %collective-permute-start.29) | collective-permute-done | bytes 294944 | tf_op jit(solution)/shard_map/ppermute | solution.py:96
  307.2 2.1 collective-permute-start.37
  309.3 5.6 %collective-permute-done.37 = f32[24,768]{1,0:T(8,128)} collective-permute-done((f32[24,768]{1,0:T(8,128)}, f32[24,768]{1,0:T(8,128)}, u32[]{:S(2)}, u32[]{:S(2)}) %collective-permute-start.37) | collective-permute-done | bytes 73760 | tf_op jit(solution)/shard_map/ppermute | solution.py:96
  315.0 2.1 collective-permute-done.36
  320.6 4.5 %all-to-all-start.6 = ((bf16[8,96,768]{2,1,0:T(8,128)(2,1)}), bf16[8,96,768]{2,1,0:T(8,128)(2,1)}, u32[]{:S(2)}, u32[]{:S(2)}) async-start(bf16[8,96,768]{2,1,0:T(8,128)(2,1)} %pad_maximum_fusion.1), calls=%async_computation.6 | async-start | bytes 2359296 | tf_op jit(solution)/shard_map/all_to_all | solution.py:62
  328.5 15.3 %collective-permute-done.38 = bf16[2,192,768]{2,1,0:T(8,128)(2,1)} collective-permute-done((bf16[2,192,768]{2,1,0:T(8,128)(2,1)}, bf16[2,192,768]{2,1,0:T(8,128)(2,1)}, u32[]{:S(2)}, u32[]{:S(2)}) %collective-permute-start.38) | collective-permute-done | bytes 589856 | tf_op jit(solution)/shard_map/ppermute | solution.py:96
  346.9 6.3 %all-to-all-done.6 = bf16[8,96,768]{2,1,0:T(8,128)(2,1)} async-done(((bf16[8,96,768]{2,1,0:T(8,128)(2,1)}), bf16[8,96,768]{2,1,0:T(8,128)(2,1)}, u32[]{:S(2)}, u32[]{:S(2)}) %all-to-all-start.6) | async-done | bytes 1179680 | tf_op jit(solution)/shard_map/all_to_all | solution.py:62
  360.3 2.3 fusion.15
  362.6 2.3 fusion.14
  (317 shorter events, 100.0 us)
Async XLA Ops:
  4.1 23.3 %all-to-all-start = ((bf16[8,48,768]{2,1,0:T(8,128)(2,1)}), bf16[8,48,768]{2,1,0:T(8,128)(2,1)S(1)}, u32[]{:S(2)}, u32[]{:S(2)}) async-start(bf16[8,48,768]{2,1,0:T(8,128)(2,1)} %bitcast.3), calls=%async_computation | async-start | bytes 1179648 | tf_op jit(solution)/shard_map/all_to_all | solution.py:62
  11.5 24.0 %collective-permute-start.3 = (bf16[192,768]{1,0:T(8,128)(2,1)S(1)}, bf16[192,768]{1,0:T(8,128)(2,1)}, u32[]{:S(2)}, u32[]{:S(2)}) collective-permute-start(bf16[192,768]{1,0:T(8,128)(2,1)S(1)} %bitcast.200), channel_id=1, source_target_pairs={{0,2},{1,3},{2,0},{3,1},{4,6},{5,7},{6,4},{7,5},{8,10},{9,11},{10,... | collective-permute-start | bytes 884744 | tf_op jit(solution)/shard_map/ppermute | solution.py:58
  13.1 34.7 %collective-permute-start.2 = (bf16[192,768]{1,0:T(8,128)(2,1)S(1)}, bf16[192,768]{1,0:T(8,128)(2,1)}, u32[]{:S(2)}, u32[]{:S(2)}) collective-permute-start(bf16[192,768]{1,0:T(8,128)(2,1)S(1)} %bitcast.197), channel_id=1, source_target_pairs={{0,2},{1,3},{2,0},{3,1},{4,6},{5,7},{6,4},{7,5},{8,10},{9,11},{10,... | collective-permute-start | bytes 884744 | tf_op jit(solution)/shard_map/ppermute | solution.py:58
  13.6 34.2 %collective-permute-start.4 = (bf16[192,768]{1,0:T(8,128)(2,1)}, bf16[192,768]{1,0:T(8,128)(2,1)}, u32[]{:S(2)}, u32[]{:S(2)}) collective-permute-start(bf16[192,768]{1,0:T(8,128)(2,1)} %bitcast.8.wv_ref), channel_id=1, source_target_pairs={{0,2},{1,3},{2,0},{3,1},{4,6},{5,7},{6,4},{7,5},{8,10},{9,11},{10,... | collective-permute-start | bytes 884744 | tf_op jit(solution)/shard_map/ppermute | solution.py:58
  15.1 50.8 %collective-permute-start.7 = (bf16[192,768]{1,0:T(8,128)(2,1)}, bf16[192,768]{1,0:T(8,128)(2,1)}, u32[]{:S(2)}, u32[]{:S(2)}) collective-permute-start(bf16[192,768]{1,0:T(8,128)(2,1)} %w_out_ref.1), channel_id=1, source_target_pairs={{0,1},{1,0},{2,3},{3,2},{4,5},{5,4},{6,7},{7,6},{8,9},{9,8},{10,11... | collective-permute-start | bytes 884744 | tf_op jit(solution)/shard_map/ppermute | solution.py:54
  27.4 9.6 %collective-permute-start = (bf16[384,768]{1,0:T(8,128)(2,1)S(1)}, bf16[384,768]{1,0:T(8,128)(2,1)S(1)}, u32[]{:S(2)}, u32[]{:S(2)}) collective-permute-start(bf16[384,768]{1,0:T(8,128)(2,1)S(1)} %bitcast.155), channel_id=1, source_target_pairs={{0,1},{1,0},{2,3},{3,2},{4,5},{5,4},{6,7},{7,6},{8,9},{9,8},{10,11... | collective-permute-start | bytes 1769480 | tf_op jit(solution)/shard_map/ppermute | solution.py:54
  27.4 27.7 %all-to-all-start.1 = ((bf16[8,48,768]{2,1,0:T(8,128)(2,1)}), bf16[8,48,768]{2,1,0:T(8,128)(2,1)S(1)}, u32[]{:S(2)}, u32[]{:S(2)}) async-start(bf16[8,48,768]{2,1,0:T(8,128)(2,1)} %bitcast.13), calls=%async_computation.1 | async-start | bytes 1179648 | tf_op jit(solution)/shard_map/all_to_all | solution.py:62
  35.5 20.5 %collective-permute-start.8 = (bf16[192,768]{1,0:T(8,128)(2,1)}, bf16[192,768]{1,0:T(8,128)(2,1)S(1)}, u32[]{:S(2)}, u32[]{:S(2)}) collective-permute-start(bf16[192,768]{1,0:T(8,128)(2,1)} %w_out_ref.1), channel_id=1, source_target_pairs={{0,2},{1,3},{2,0},{3,1},{4,6},{5,7},{6,4},{7,5},{8,10},{9,11},{10,... | collective-permute-start | bytes 884744 | tf_op jit(solution)/shard_map/ppermute | solution.py:58
  55.2 2.6 collective-permute-start.6
  56.1 9.9 %collective-permute-start.9 = (bf16[192,768]{1,0:T(8,128)(2,1)S(1)}, bf16[192,768]{1,0:T(8,128)(2,1)}, u32[]{:S(2)}, u32[]{:S(2)}) collective-permute-start(bf16[192,768]{1,0:T(8,128)(2,1)S(1)} %collective-permute-done.8.o2_ref.w_out_ref), channel_id=1, source_target_pairs={{0,1},{1,0},{2,3},{3,2},{4,5},{5,4},{6,7},{7,6},{8,9},{9,8},{10,11... | collective-permute-start | bytes 884744 | tf_op jit(solution)/shard_map/ppermute | solution.py:54
  56.5 9.4 %collective-permute-start.5 = (bf16[768,256]{1,0:T(8,128)(2,1)}, bf16[768,256]{1,0:T(8,128)(2,1)S(1)}, u32[]{:S(2)}, u32[]{:S(2)}) collective-permute-start(bf16[768,256]{1,0:T(8,128)(2,1)} %get-tuple-element.113.m2_ref), channel_id=1, source_target_pairs={{0,1},{1,0},{2,3},{3,2},{4,5},{5,4},{6,7},{7,6},{8,9},{9,8},{10,11... | collective-permute-start | bytes 1179656 | tf_op jit(solution)/shard_map/ppermute | solution.py:54
  56.6 9.3 %collective-permute-start.1 = (bf16[768,256]{1,0:T(8,128)(2,1)S(1)}, bf16[768,256]{1,0:T(8,128)(2,1)}, u32[]{:S(2)}, u32[]{:S(2)}) collective-permute-start(bf16[768,256]{1,0:T(8,128)(2,1)S(1)} %copy-done.54), channel_id=1, source_target_pairs={{0,1},{1,0},{2,3},{3,2},{4,5},{5,4},{6,7},{7,6},{8,9},{9,8},{10,11... | collective-permute-start | bytes 1179656 | tf_op jit(solution)/shard_map/ppermute | solution.py:54
  59.2 26.4 %all-to-all-start.3 = ((bf16[8,64,768]{2,1,0:T(8,128)(2,1)}), bf16[8,64,768]{2,1,0:T(8,128)(2,1)S(1)}, u32[]{:S(2)}, u32[]{:S(2)}) async-start(bf16[8,64,768]{2,1,0:T(8,128)(2,1)} %bitcast.20), calls=%async_computation.3 | async-start | bytes 1572864 | tf_op jit(solution)/shard_map/all_to_all | solution.py:62
  85.6 41.2 %all-to-all-start.2 = ((bf16[8,128,768]{2,1,0:T(8,128)(2,1)}), bf16[8,128,768]{2,1,0:T(8,128)(2,1)}, u32[]{:S(2)}, u32[]{:S(2)}) async-start(bf16[8,128,768]{2,1,0:T(8,128)(2,1)} %bitcast.18), calls=%async_computation.2 | async-start | bytes 3145728 | tf_op jit(solution)/shard_map/all_to_all | solution.py:62
  96.3 18.6 %collective-permute-start.10 = (bf16[8,64,768]{2,1,0:T(8,128)(2,1)S(1)}, bf16[8,64,768]{2,1,0:T(8,128)(2,1)S(1)}, u32[]{:S(2)}, u32[]{:S(2)}) collective-permute-start(bf16[8,64,768]{2,1,0:T(8,128)(2,1)S(1)} %all-to-all-done.3), channel_id=1, source_target_pairs={{0,2},{1,3},{2,0},{3,1},{4,6},{5,7},{6,4},{7,5},{8,10},{9,11},{10,... | collective-permute-start | bytes 2359304 | tf_op jit(solution)/shard_map/ppermute | solution.py:58
  99.3 35.8 %collective-permute-start.13 = (bf16[4,192,768]{2,1,0:T(8,128)(2,1)}, bf16[4,192,768]{2,1,0:T(8,128)(2,1)}, u32[]{:S(2)}, u32[]{:S(2)}) collective-permute-start(bf16[4,192,768]{2,1,0:T(8,128)(2,1)} %dynamic-slice_bitcast_fusion), channel_id=1, source_target_pairs={{0,4},{4,0},{8,12},{12,8},{16,20},{20,16},{24,28},{28,24},{1,5},{5... | collective-permute-start | bytes 3538952 | tf_op jit(solution)/shard_map/ppermute | solution.py:96
  116.7 10.1 %collective-permute-start.11 = (bf16[1024,768]{1,0:T(8,128)(2,1)}, bf16[1024,768]{1,0:T(8,128)(2,1)}, u32[]{:S(2)}, u32[]{:S(2)}) collective-permute-start(bf16[1024,768]{1,0:T(8,128)(2,1)} %bitcast.21.cot_ref.cot_own), channel_id=1, source_target_pairs={{0,1},{1,0},{2,3},{3,2},{4,5},{5,4},{6,7},{7,6},{8,9},{9,8},{10,11... | collective-permute-start | bytes 4718600 | tf_op jit(solution)/shard_map/ppermute | solution.py:54
  126.8 11.4 %collective-permute-start.12 = (bf16[1024,768]{1,0:T(8,128)(2,1)}, bf16[1024,768]{1,0:T(8,128)(2,1)}, u32[]{:S(2)}, u32[]{:S(2)}) collective-permute-start(bf16[1024,768]{1,0:T(8,128)(2,1)} %bitcast.19.rows_ref.rows_own), channel_id=1, source_target_pairs={{0,1},{1,0},{2,3},{3,2},{4,5},{5,4},{6,7},{7,6},{8,9},{9,8},{10,11... | collective-permute-start | bytes 4718600 | tf_op jit(solution)/shard_map/ppermute | solution.py:54
  136.8 14.4 %collective-permute-start.14 = (bf16[2,192,768]{2,1,0:T(8,128)(2,1)S(1)}, bf16[2,192,768]{2,1,0:T(8,128)(2,1)S(1)}, u32[]{:S(2)}, u32[]{:S(2)}) collective-permute-start(bf16[2,192,768]{2,1,0:T(8,128)(2,1)S(1)} %dynamic-slice_bitcast_fusion.2), channel_id=1, source_target_pairs={{0,8},{4,12},{8,0},{12,4},{16,24},{20,28},{24,16},{28,20},{1,9},{5... | collective-permute-start | bytes 1769480 | tf_op jit(solution)/shard_map/ppermute | solution.py:96
  151.4 13.4 %collective-permute-start.15 = (bf16[1024,768]{1,0:T(8,128)(2,1)}, bf16[1024,768]{1,0:T(8,128)(2,1)S(1)}, u32[]{:S(2)}, u32[]{:S(2)}) collective-permute-start(bf16[1024,768]{1,0:T(8,128)(2,1)} %get-tuple-element.133), channel_id=1, source_target_pairs={{0,1},{1,0},{2,3},{3,2},{4,5},{5,4},{6,7},{7,6},{8,9},{9,8},{10,11... | collective-permute-start | bytes 4718600 | tf_op jit(solution)/shard_map/ppermute | solution.py:54
  151.5 18.3 %collective-permute-start.16 = (bf16[1,192,768]{2,1,0:T(8,128)(2,1)S(1)}, bf16[1,192,768]{2,1,0:T(8,128)(2,1)S(1)}, u32[]{:S(2)}, u32[]{:S(2)}) collective-permute-start(bf16[1,192,768]{2,1,0:T(8,128)(2,1)S(1)} %constant_dynamic-slice_fusion.6), channel_id=1, source_target_pairs={{0,16},{4,20},{8,24},{12,28},{16,0},{20,4},{24,8},{28,12},{1,17},{... | collective-permute-start | bytes 884744 | tf_op jit(solution)/shard_map/ppermute | solution.py:96
  170.6 5.0 %collective-permute-start.17 = (bf16[1024,768]{1,0:T(8,128)(2,1)}, bf16[1024,768]{1,0:T(8,128)(2,1)}, u32[]{:S(2)}, u32[]{:S(2)}) collective-permute-start(bf16[1024,768]{1,0:T(8,128)(2,1)} %get-tuple-element.139), channel_id=1, source_target_pairs={{0,1},{1,0},{2,3},{3,2},{4,5},{5,4},{6,7},{7,6},{8,9},{9,8},{10,11... | collective-permute-start | bytes 4718600 | tf_op jit(solution)/shard_map/ppermute | solution.py:54
  170.6 42.6 %all-to-all-start.4 = ((bf16[8,128,768]{2,1,0:T(8,128)(2,1)}), bf16[8,128,768]{2,1,0:T(8,128)(2,1)S(1)}, u32[]{:S(2)}, u32[]{:S(2)}) async-start(bf16[8,128,768]{2,1,0:T(8,128)(2,1)} %bitcast.35), calls=%async_computation.4 | async-start | bytes 3145728 | tf_op jit(solution)/shard_map/all_to_all | solution.py:62
  179.5 19.9 %collective-permute-start.18 = (bf16[8,64,768]{2,1,0:T(8,128)(2,1)}, bf16[8,64,768]{2,1,0:T(8,128)(2,1)}, u32[]{:S(2)}, u32[]{:S(2)}) collective-permute-start(bf16[8,64,768]{2,1,0:T(8,128)(2,1)} %constant_dynamic-slice_fusion.1), channel_id=1, source_target_pairs={{0,2},{1,3},{2,0},{3,1},{4,6},{5,7},{6,4},{7,5},{8,10},{9,11},{10,... | collective-permute-start | bytes 2359304 | tf_op jit(solution)/shard_map/ppermute | solution.py:58
  214.6 2.1 collective-permute-start.19
  216.9 18.0 %collective-permute-start.20 = (bf16[384,768]{1,0:T(8,128)(2,1)S(1)}, bf16[384,768]{1,0:T(8,128)(2,1)S(1)}, u32[]{:S(2)}, u32[]{:S(2)}) collective-permute-start(bf16[384,768]{1,0:T(8,128)(2,1)S(1)} %add_convert_fusion.7), channel_id=1, source_target_pairs={{0,2},{1,3},{2,0},{3,1},{4,6},{5,7},{6,4},{7,5},{8,10},{9,11},{10,... | collective-permute-start | bytes 1769480 | tf_op jit(solution)/shard_map/ppermute | solution.py:58
  219.1 15.7 %collective-permute-start.21 = (bf16[1,192,768]{2,1,0:T(8,128)(2,1)S(1)}, bf16[1,192,768]{2,1,0:T(8,128)(2,1)S(1)}, u32[]{:S(2)}, u32[]{:S(2)}) collective-permute-start(bf16[1,192,768]{2,1,0:T(8,128)(2,1)S(1)} %copy-done.22), channel_id=1, source_target_pairs={{0,16},{4,20},{8,24},{12,28},{16,0},{20,4},{24,8},{28,12},{1,17},{... | collective-permute-start | bytes 884744 | tf_op jit(solution)/shard_map/ppermute | solution.py:96
  219.2 1.3 collective-permute-start.22
  220.5 12.3 %collective-permute-start.23 = (f32[8,768]{1,0:T(8,128)S(1)}, f32[8,768]{1,0:T(8,128)S(1)}, u32[]{:S(2)}, u32[]{:S(2)}) collective-permute-start(f32[8,768]{1,0:T(8,128)S(1)} %fusion.116), channel_id=1, source_target_pairs={{0,2},{1,3},{2,0},{3,1},{4,6},{5,7},{6,4},{7,5},{8,10},{9,11},{10,... | collective-permute-start | bytes 73736 | tf_op jit(solution)/shard_map/ppermute | solution.py:58
  235.0 24.1 %all-to-all-start.5 = ((bf16[8,64,768]{2,1,0:T(8,128)(2,1)}), bf16[8,64,768]{2,1,0:T(8,128)(2,1)S(1)}, u32[]{:S(2)}, u32[]{:S(2)}) async-start(bf16[8,64,768]{2,1,0:T(8,128)(2,1)} %bitcast.45), calls=%async_computation.5 | async-start | bytes 1572864 | tf_op jit(solution)/shard_map/all_to_all | solution.py:62
  238.7 2.0 collective-permute-start.24
  260.4 3.7 %collective-permute-start.26 = (bf16[384,768]{1,0:T(8,128)(2,1)}, bf16[384,768]{1,0:T(8,128)(2,1)S(1)}, u32[]{:S(2)}, u32[]{:S(2)}) collective-permute-start(bf16[384,768]{1,0:T(8,128)(2,1)} %fusion.25), channel_id=1, source_target_pairs={{0,1},{1,0},{2,3},{3,2},{4,5},{5,4},{6,7},{7,6},{8,9},{9,8},{10,11... | collective-permute-start | bytes 1769480 | tf_op jit(solution)/shard_map/ppermute | solution.py:54
  260.5 15.8 %collective-permute-start.30 = (bf16[2,192,768]{2,1,0:T(8,128)(2,1)S(1)}, bf16[2,192,768]{2,1,0:T(8,128)(2,1)S(1)}, u32[]{:S(2)}, u32[]{:S(2)}) collective-permute-start(bf16[2,192,768]{2,1,0:T(8,128)(2,1)S(1)} %maximum_select_fusion.9), channel_id=1, source_target_pairs={{0,8},{4,12},{8,0},{12,4},{16,24},{20,28},{24,16},{28,20},{1,9},{5... | collective-permute-start | bytes 1769480 | tf_op jit(solution)/shard_map/ppermute | solution.py:96
  262.6 15.9 %collective-permute-start.25 = (bf16[2,192,768]{2,1,0:T(8,128)(2,1)S(1)}, bf16[2,192,768]{2,1,0:T(8,128)(2,1)S(1)}, u32[]{:S(2)}, u32[]{:S(2)}) collective-permute-start(bf16[2,192,768]{2,1,0:T(8,128)(2,1)S(1)} %dynamic-slice_bitcast_fusion.1), channel_id=1, source_target_pairs={{0,4},{4,0},{8,12},{12,8},{16,20},{20,16},{24,28},{28,24},{1,5},{5... | collective-permute-start | bytes 1769480 | tf_op jit(solution)/shard_map/ppermute | solution.py:96
  264.6 15.6 %collective-permute-start.28 = (bf16[384,768]{1,0:T(8,128)(2,1)S(1)}, bf16[384,768]{1,0:T(8,128)(2,1)S(1)}, u32[]{:S(2)}, u32[]{:S(2)}) collective-permute-start(bf16[384,768]{1,0:T(8,128)(2,1)S(1)} %add_convert_fusion.5), channel_id=1, source_target_pairs={{0,2},{1,3},{2,0},{3,1},{4,6},{5,7},{6,4},{7,5},{8,10},{9,11},{10,... | collective-permute-start | bytes 1769480 | tf_op jit(solution)/shard_map/ppermute | solution.py:58
  276.7 11.0 %collective-permute-start.31 = (bf16[4,48,768]{2,1,0:T(8,128)(2,1)S(1)}, bf16[4,48,768]{2,1,0:T(8,128)(2,1)S(1)}, u32[]{:S(2)}, u32[]{:S(2)}) collective-permute-start(bf16[4,48,768]{2,1,0:T(8,128)(2,1)S(1)} %slice.84), channel_id=1, source_target_pairs={{0,4},{4,0},{8,12},{12,8},{16,20},{20,16},{24,28},{28,24},{1,5},{5... | collective-permute-start | bytes 884744 | tf_op jit(solution)/shard_map/ppermute | solution.py:96
  278.7 9.7 %collective-permute-start.27 = (bf16[1,192,768]{2,1,0:T(8,128)(2,1)S(1)}, bf16[1,192,768]{2,1,0:T(8,128)(2,1)S(1)}, u32[]{:S(2)}, u32[]{:S(2)}) collective-permute-start(bf16[1,192,768]{2,1,0:T(8,128)(2,1)S(1)} %constant_dynamic-slice_fusion), channel_id=1, source_target_pairs={{0,8},{4,12},{8,0},{12,4},{16,24},{20,28},{24,16},{28,20},{1,9},{5... | collective-permute-start | bytes 884744 | tf_op jit(solution)/shard_map/ppermute | solution.py:96
  287.6 3.2 collective-permute-start.32
  288.5 16.5 %collective-permute-start.29 = (bf16[1,192,768]{2,1,0:T(8,128)(2,1)S(1)}, bf16[1,192,768]{2,1,0:T(8,128)(2,1)S(1)}, u32[]{:S(2)}, u32[]{:S(2)}) collective-permute-start(bf16[1,192,768]{2,1,0:T(8,128)(2,1)S(1)} %add_convert_fusion.11), channel_id=1, source_target_pairs={{0,16},{4,20},{8,24},{12,28},{16,0},{20,4},{24,8},{28,12},{1,17},{... | collective-permute-start | bytes 884744 | tf_op jit(solution)/shard_map/ppermute | solution.py:96
  291.4 1.2 collective-permute-start.33
  292.7 4.4 %collective-permute-start.34 = (f32[24,768]{1,0:T(8,128)S(1)}, f32[24,768]{1,0:T(8,128)S(1)}, u32[]{:S(2)}, u32[]{:S(2)}) collective-permute-start(f32[24,768]{1,0:T(8,128)S(1)} %select_maximum_fusion), channel_id=1, source_target_pairs={{0,4},{4,0},{8,12},{12,8},{16,20},{20,16},{24,28},{28,24},{1,5},{5... | collective-permute-start | bytes 221192 | tf_op jit(solution)/shard_map/ppermute | solution.py:96
  297.1 9.3 %collective-permute-start.35 = (f32[24,768]{1,0:T(8,128)S(1)}, f32[24,768]{1,0:T(8,128)S(1)}, u32[]{:S(2)}, u32[]{:S(2)}) collective-permute-start(f32[24,768]{1,0:T(8,128)S(1)} %fusion.121), channel_id=1, source_target_pairs={{0,8},{4,12},{8,0},{12,4},{16,24},{20,28},{24,16},{28,20},{1,9},{5... | collective-permute-start | bytes 221192 | tf_op jit(solution)/shard_map/ppermute | solution.py:96
  297.8 27.4 %collective-permute-start.39 = (bf16[4,144,768]{2,1,0:T(8,128)(2,1)S(1)}, bf16[4,144,768]{2,1,0:T(8,128)(2,1)S(1)}, u32[]{:S(2)}, u32[]{:S(2)}) collective-permute-start(bf16[4,144,768]{2,1,0:T(8,128)(2,1)S(1)} %slice.89), channel_id=1, source_target_pairs={{0,4},{4,0},{8,12},{12,8},{16,20},{20,16},{24,28},{28,24},{1,5},{5... | collective-permute-start | bytes 2654216 | tf_op jit(solution)/shard_map/ppermute | solution.py:96
  306.5 10.6 %collective-permute-start.36 = (bf16[1,192,768]{2,1,0:T(8,128)(2,1)S(1)}, bf16[1,192,768]{2,1,0:T(8,128)(2,1)S(1)}, u32[]{:S(2)}, u32[]{:S(2)}) collective-permute-start(bf16[1,192,768]{2,1,0:T(8,128)(2,1)S(1)} %add_convert_fusion.10), channel_id=1, source_target_pairs={{0,8},{4,12},{8,0},{12,4},{16,24},{20,28},{24,16},{28,20},{1,9},{5... | collective-permute-start | bytes 884744 | tf_op jit(solution)/shard_map/ppermute | solution.py:96
  307.2 7.8 %collective-permute-start.37 = (f32[24,768]{1,0:T(8,128)}, f32[24,768]{1,0:T(8,128)}, u32[]{:S(2)}, u32[]{:S(2)}) collective-permute-start(f32[24,768]{1,0:T(8,128)} %add.303), channel_id=1, source_target_pairs={{0,16},{4,20},{8,24},{12,28},{16,0},{20,4},{24,8},{28,12},{1,17},{... | collective-permute-start | bytes 221192 | tf_op jit(solution)/shard_map/ppermute | solution.py:96
  319.5 24.2 %collective-permute-start.38 = (bf16[2,192,768]{2,1,0:T(8,128)(2,1)}, bf16[2,192,768]{2,1,0:T(8,128)(2,1)}, u32[]{:S(2)}, u32[]{:S(2)}) collective-permute-start(bf16[2,192,768]{2,1,0:T(8,128)(2,1)} %maximum_select_fusion.10), channel_id=1, source_target_pairs={{0,4},{4,0},{8,12},{12,8},{16,20},{20,16},{24,28},{28,24},{1,5},{5... | collective-permute-start | bytes 1769480 | tf_op jit(solution)/shard_map/ppermute | solution.py:96
  320.6 32.6 %all-to-all-start.6 = ((bf16[8,96,768]{2,1,0:T(8,128)(2,1)}), bf16[8,96,768]{2,1,0:T(8,128)(2,1)}, u32[]{:S(2)}, u32[]{:S(2)}) async-start(bf16[8,96,768]{2,1,0:T(8,128)(2,1)} %pad_maximum_fusion.1), calls=%async_computation.6 | async-start | bytes 2359296 | tf_op jit(solution)/shard_map/all_to_all | solution.py:62
  353.2 5.8 %collective-permute-start.40 = (bf16[8,96,768]{2,1,0:T(8,128)(2,1)}, bf16[8,96,768]{2,1,0:T(8,128)(2,1)}, u32[]{:S(2)}, u32[]{:S(2)}) collective-permute-start(bf16[8,96,768]{2,1,0:T(8,128)(2,1)} %all-to-all-done.6), channel_id=1, source_target_pairs={{0,1},{1,0},{2,3},{3,2},{4,5},{5,4},{6,7},{7,6},{8,9},{9,8},{10,11... | collective-permute-start | bytes 3538952 | tf_op jit(solution)/shard_map/ppermute | solution.py:54
  (61 other events, 287.9 us)

commit v5 on v4

--- a/solution.py
+++ b/solution.py
@@ -1219,12 +1219,12 @@
     small = small + small_came
     late.end()
     late.start()
-    late.came, small_came = tie(late.came, group_swap(small, 2))
+    late.came, small_came, both_send = tie(late.came, group_swap(small, 2), both_send)
+    both_own = exchange(both_send)
     small = small + small_came
     for step in range(3, group_count.bit_length() - 1):
         small = small + group_swap(small, step)
     late.end()
-    both_own = exchange(after(both_send, late.part))
     late.start()
     early.end_second(late.part)
     g_router = small[:EXPERTS].T

time: 370 us -> 368 us (level)
    all_to_all x7, waiting for transfers between devices: 30.4 us -> 24.1 us  [exchange(): lax.all_to_all(values, 'expert', split_axis=0, concat_axis=0, tiled=True)]
    ppermute x15, waiting for transfers between devices: 46.9 us -> 52.6 us  [group_swap(): lax.ppermute(values, 'expert', [(i, i ^ 1 << step) for i in range(size)])]
  transfers between devices with their start and end apart: 48 -> 48, of which waited for: 25 -> 24; matrix products, arithmetic and copies ran while one was open for 20% -> 20% of each run, Pallas kernels for 24% -> 24%
where the time goes in v5:
time: 368 us; the launch traced here: 363 us
  waiting for transfers between devices  108 us (29%)
  Pallas kernels  88.5 us (24%)
  starting transfers between devices  71.4 us (19%)
  matrix products  36 us (10%)
  other arithmetic  30.6 us (8%)
  local copies, waits for them, and re-layouts  25.9 us (7%)
    pallas_call x6, Pallas kernels, call_whole(): pl.pallas_call(kernel, grid_spec=pltpu.PrefetchScalarGridSpec(num_scalar_...  58.2 us
    ppermute x15, waiting for transfers between devices, group_swap(): lax.ppermute(values, 'expert', [(i, i ^ 1 << step) for i in range(size)])  52.6 us
    all_to_all x7, starting transfers between devices, exchange(): lax.all_to_all(values, 'expert', split_axis=0, concat_axis=0, tiled=True)  35.4 us
    ppermute x9, waiting for transfers between devices, far_swap(): return lax.ppermute(values, 'tensor', [(i, i ^ 2) for i in range(4)])  27.2 us
    all_to_all x7, waiting for transfers between devices, exchange(): lax.all_to_all(values, 'expert', split_axis=0, concat_axis=0, tiled=True)  24.1 us
    ppermute x15, starting transfers between devices, group_swap(): lax.ppermute(values, 'expert', [(i, i ^ 1 << step) for i in range(size)])  24.1 us
    pallas_call x2, Pallas kernels, run_expert(): pl.pallas_call(functools.partial(expert_kernel, half_slots, block), grid_...  18.3 us
    pallas_call x1, Pallas kernels, run_weights(): pl.pallas_call(weight_kernel, grid_spec=pltpu.PrefetchScalarGridSpec(num_...  12 us
  transfers between devices with their start and end apart: 48, of which 24 were waited for; matrix products, arithmetic and copies ran while one was open for 20% of the time, Pallas kernels for 24%

profile of v5, /device:TPU:0, one launch (start us, length us, event | category | flops | bytes accessed | tf_op | source)
XLA Modules:
  0.0 362.6 jit_solution(8491161047429795001)
XLA Ops:
  4.1 7.4 %all-to-all-start = ((bf16[8,48,768]{2,1,0:T(8,128)(2,1)}), bf16[8,48,768]{2,1,0:T(8,128)(2,1)S(1)}, u32[]{:S(2)}, u32[]{:S(2)}) async-start(bf16[8,48,768]{2,1,0:T(8,128)(2,1)} %bitcast.3), calls=%async_computation | async-start | bytes 1179648 | tf_op jit(solution)/shard_map/all_to_all | solution.py:62
  17.3 2.5 fusion.84
  21.2 2.8 fusion.26
  24.0 3.5 all-to-all-done
  27.4 4.2 %all-to-all-start.1 = ((bf16[8,48,768]{2,1,0:T(8,128)(2,1)}), bf16[8,48,768]{2,1,0:T(8,128)(2,1)S(1)}, u32[]{:S(2)}, u32[]{:S(2)}) async-start(bf16[8,48,768]{2,1,0:T(8,128)(2,1)} %bitcast.13), calls=%async_computation.1 | async-start | bytes 1179648 | tf_op jit(solution)/shard_map/all_to_all | solution.py:62
  38.0 9.8 %attention_near.1 = (bf16[768,768]{1,0:T(8,128)(2,1)}, bf16[768,768]{1,0:T(8,128)(2,1)}, bf16[768,256]{1,0:T(8,128)(2,1)}, bf16[768,256]{1,0:T(8,128)(2,1)}, bf1...) custom-call(bf16[384,768]{1,0:T(8,128)(2,1)} %bitcast.154, bf16[384,768]{1,0:T(8,128)(2,1)} %copy-done.52, ...), custom_call_target="tpu_custom_call" | custom-call | flops 2415919104 | bytes 8752128 | tf_op jit(solution)/shard_map/attention_near/pallas_call | solution.py:479
  47.8 7.4 %attention_far.1 = (bf16[768,256]{1,0:T(8,128)(2,1)}, bf16[768,256]{1,0:T(8,128)(2,1)}, bf16[768,256]{1,0:T(8,128)(2,1)}, bf16[768,256]{1,0:T(8,128)(2,1)}, f32[768,128]{1,0:T(8,128)}) custom-call(bf16[768,768]{1,0:T(8,128)(2,1)} %get-tuple-element.109.hidden_ref, bf16[192,768]{1,0:T(8,128)(2,1)} %collective-permute-done.2.wq_ref, ...), custom_call_target="tpu_custom_call" | custom-call | flops 1509949440 | bytes 5210112 | tf_op jit(solution)/shard_map/attention_far/pallas_call | solution.py:479
  59.2 6.0 %all-to-all-start.3 = ((bf16[8,64,768]{2,1,0:T(8,128)(2,1)}), bf16[8,64,768]{2,1,0:T(8,128)(2,1)S(1)}, u32[]{:S(2)}, u32[]{:S(2)}) async-start(bf16[8,64,768]{2,1,0:T(8,128)(2,1)} %bitcast.20), calls=%async_computation.3 | async-start | bytes 1572864 | tf_op jit(solution)/shard_map/all_to_all | solution.py:62
  66.7 8.1 %middle.1 = (f32[768,768]{1,0:T(8,128)}, bf16[768,768]{1,0:T(8,128)(2,1)}, bf16[1024,768]{1,0:T(8,128)(2,1)}, f32[8,768]{1,0:T(8,128)}) custom-call(s32[1]{0:T(128)} %bitcast.turn_ref, bf16[768,256]{1,0:T(8,128)(2,1)} %get-tuple-element.108.m0_ref.mixed_ref, bf16[768,256]{1,0:T(8,128)(2,1)} %collective-permute-done.1.m1_ref, ...), custom_call_target="tpu_custom_call" | custom-call | flops 2415919104 | bytes 10816512 | tf_op jit(solution)/shard_map/middle/pallas_call | solution.py:479
  76.6 2.0 fusion.128
  78.6 7.0 %all-to-all-done.3 = bf16[8,64,768]{2,1,0:T(8,128)(2,1)S(1)} async-done(((bf16[8,64,768]{2,1,0:T(8,128)(2,1)}), bf16[8,64,768]{2,1,0:T(8,128)(2,1)S(1)}, u32[]{:S(2)}, u32[]{:S(2)}) %all-to-all-start.3) | async-done | bytes 786464 | tf_op jit(solution)/shard_map/all_to_all | solution.py:62
  85.6 4.6 %all-to-all-start.2 = ((bf16[8,128,768]{2,1,0:T(8,128)(2,1)}), bf16[8,128,768]{2,1,0:T(8,128)(2,1)}, u32[]{:S(2)}, u32[]{:S(2)}) async-start(bf16[8,128,768]{2,1,0:T(8,128)(2,1)} %bitcast.18), calls=%async_computation.2 | async-start | bytes 3145728 | tf_op jit(solution)/shard_map/all_to_all | solution.py:62
  90.3 2.3 fusion.129
  99.3 2.0 collective-permute-start.13
  102.1 12.8 %collective-permute-done.10 = bf16[8,64,768]{2,1,0:T(8,128)(2,1)S(1)} collective-permute-done((bf16[8,64,768]{2,1,0:T(8,128)(2,1)S(1)}, bf16[8,64,768]{2,1,0:T(8,128)(2,1)S(1)}, u32[]{:S(2)}, u32[]{:S(2)}) %collective-permute-start.10) | collective-permute-done | bytes 786464 | tf_op jit(solution)/shard_map/ppermute | solution.py:58
  114.9 1.8 maximum_select_fusion.1
  121.1 2.2 convolution_add_fusion
  126.8 8.3 %collective-permute-done.13 = bf16[4,192,768]{2,1,0:T(8,128)(2,1)} collective-permute-done((bf16[4,192,768]{2,1,0:T(8,128)(2,1)}, bf16[4,192,768]{2,1,0:T(8,128)(2,1)}, u32[]{:S(2)}, u32[]{:S(2)}) %collective-permute-start.13) | collective-permute-done | bytes 1179680 | tf_op jit(solution)/shard_map/ppermute | solution.py:96
  138.2 9.4 %expert_rows.2 = (bf16[1024,768]{1,0:T(8,128)(2,1)}, bf16[1024,768]{1,0:T(8,128)(2,1)}, bf16[1024,512]{1,0:T(8,128)(2,1)S(1)}, bf16[1024,512]{1,0:T(8,128)(2,1)S(1)}, bf16[1024,512]{1,0:T(8,128)(2,1)S(1)}) custom-call(s32[1]{0:T(128)} %bitcast.24.which_ref, bf16[1024,768]{1,0:T(8,128)(2,1)} %collective-permute-done.12.rows_ref.rows_other, ...), custom_call_target="tpu_custom_call" | custom-call | flops 4831838208 | bytes 11796480 | tf_op jit(solution)/shard_map/expert_rows/pallas_call | solution.py:239
  148.6 2.6 collective-permute-done.14
  151.5 4.3 %collective-permute-start.16 = (bf16[1,192,768]{2,1,0:T(8,128)(2,1)S(1)}, bf16[1,192,768]{2,1,0:T(8,128)(2,1)S(1)}, u32[]{:S(2)}, u32[]{:S(2)}) collective-permute-start(bf16[1,192,768]{2,1,0:T(8,128)(2,1)S(1)} %constant_dynamic-slice_fusion.6), channel_id=1, source_target_pairs={{0,16},{4,20},{8,24},{12,28},{16,0},{20,4},{24,8},{28,12},{1,17},{... | collective-permute-start | bytes 884744 | tf_op jit(solution)/shard_map/ppermute | solution.py:96
  155.8 8.9 %expert_rows.3 = (bf16[1024,768]{1,0:T(8,128)(2,1)}, bf16[1024,768]{1,0:T(8,128)(2,1)}, bf16[1024,512]{1,0:T(8,128)(2,1)S(1)}, bf16[1024,512]{1,0:T(8,128)(2,1)S(1)}, bf16[1024,512]{1,0:T(8,128)(2,1)S(1)}) custom-call(s32[1]{0:T(128)} %bitcast.2.which_ref, bf16[1024,768]{1,0:T(8,128)(2,1)} %bitcast.19.rows_ref.rows_own, ...), custom_call_target="tpu_custom_call" | custom-call | flops 4831838208 | bytes 11796480 | tf_op jit(solution)/shard_map/expert_rows/pallas_call | solution.py:239
  164.8 2.9 convert_add_fusion
  170.6 5.0 %all-to-all-start.4 = ((bf16[8,128,768]{2,1,0:T(8,128)(2,1)}), bf16[8,128,768]{2,1,0:T(8,128)(2,1)S(1)}, u32[]{:S(2)}, u32[]{:S(2)}) async-start(bf16[8,128,768]{2,1,0:T(8,128)(2,1)} %bitcast.35), calls=%async_computation.4 | async-start | bytes 3145728 | tf_op jit(solution)/shard_map/all_to_all | solution.py:62
  175.6 1.8 add_convert_fusion
  184.4 12.0 %expert_weights.1 = (f32[2,768,512]{2,1,0:T(8,128)}, f32[2,768,512]{2,1,0:T(8,128)}, f32[2,512,768]{2,1,0:T(8,128)}) custom-call(s32[1]{0:T(128)} %bitcast.37.which_ref, bf16[1024,768]{1,0:T(8,128)(2,1)} %bitcast.19.rows_ref.rows_own, bf16[1024,768]{1,0:T(8,128)(2,1)} %collective-permute-done.12.rows_ref.rows_other, ...), custom_call_target="tpu_custom_call" | custom-call | flops 4831838208 | bytes 22020096 | tf_op jit(solution)/shard_map/expert_weights/pallas_call | solution.py:309
  196.5 2.9 collective-permute-done.18
  199.4 2.2 add_convert_fusion.2
  201.6 11.6 %all-to-all-done.4 = bf16[8,128,768]{2,1,0:T(8,128)(2,1)S(1)} async-done(((bf16[8,128,768]{2,1,0:T(8,128)(2,1)}), bf16[8,128,768]{2,1,0:T(8,128)(2,1)S(1)}, u32[]{:S(2)}, u32[]{:S(2)}) %all-to-all-start.4) | async-done | bytes 1572896 | tf_op jit(solution)/shard_map/all_to_all | solution.py:62
  221.4 11.4 %collective-permute-done.23 = f32[8,768]{1,0:T(8,128)S(1)} collective-permute-done((f32[8,768]{1,0:T(8,128)S(1)}, f32[8,768]{1,0:T(8,128)S(1)}, u32[]{:S(2)}, u32[]{:S(2)}) %collective-permute-start.23) | collective-permute-done | bytes 24608 | tf_op jit(solution)/shard_map/ppermute | solution.py:58
  232.8 2.0 collective-permute-done.21
  235.0 3.7 %all-to-all-start.5 = ((bf16[8,64,768]{2,1,0:T(8,128)(2,1)}), bf16[8,64,768]{2,1,0:T(8,128)(2,1)S(1)}, u32[]{:S(2)}, u32[]{:S(2)}) async-start(bf16[8,64,768]{2,1,0:T(8,128)(2,1)} %bitcast.45), calls=%async_computation.5 | async-start | bytes 1572864 | tf_op jit(solution)/shard_map/all_to_all | solution.py:62
  241.6 16.1 %back_near.1 = (f32[768,768]{1,0:T(8,128)}, bf16[768,768]{1,0:T(8,128)(2,1)}, f32[1,768]{1,0:T(1,128)}, f32[16,768]{1,0:T(8,128)}, bf16[768,768]{1,0:T(8,128)(2,1)}, /*index=5*/f32[768,768]{1,0:T(8,128)}) custom-call(s32[1]{0:T(128)} %bitcast.turn_ref, bf16[384,768]{1,0:T(8,128)(2,1)} %copy-done.37, bf16[384,768]{1,0:T(8,128)(2,1)} %copy-done.53, ...), custom_call_target="tpu_custom_call" | custom-call | flops 3925868544 | bytes 18708480 | tf_op jit(solution)/shard_map/back_near/pallas_call | solution.py:479
  260.5 2.0 collective-permute-start.30
  265.3 9.7 %back_far.1.all_ref = bf16[768,768]{1,0:T(8,128)(2,1)} custom-call(bf16[768,768]{1,0:T(8,128)(2,1)} %get-tuple-element.166.d_proj_ref, s32[768,128]{1,0:T(8,128)} %broadcast_in_dim.141.start_ref, f32[768,128]{1,0:T(8,128)} %get-tuple-element.290.cos_ref, f32[768,128]{1,0:T(8,128)} %get-tuple-element.289.sin_ref, f32[768,128]{1,0:T(8,128)} %get-tuple-element.167.lse_ref, ...), custom_call_target="tpu_custom_call" | custom-call | flops 1811939328 | bytes 5406720 | tf_op jit(solution)/shard_map/back_far/pallas_call | solution.py:479
  276.7 1.8 collective-permute-start.31
  280.4 7.2 %back_rows.1 = (bf16[384,768]{1,0:T(8,128)(2,1)}, bf16[384,768]{1,0:T(8,128)(2,1)}, f32[384,768]{1,0:T(8,128)}) custom-call(bf16[768,768]{1,0:T(8,128)(2,1)} %back_far.1.all_ref, f32[768,768]{1,0:T(8,128)} %get-tuple-element.173.d_resid_ref, f32[768,768]{1,0:T(8,128)} %get-tuple-element.174.term_ref, bf16[768,384]{1,0:T(8,128)(2,1)} %get-tuple-element.299.place_own_ref, ...), custom_call_target="tpu_custom_call" | custom-call | flops 2717908992 | bytes 10321920 | tf_op jit(solution)/shard_map/back_rows/pallas_call | solution.py:479
  288.5 2.4 collective-permute-start.29
  294.3 2.9 collective-permute-done.34
  299.9 5.0 %collective-permute-done.29 = bf16[1,192,768]{2,1,0:T(8,128)(2,1)S(1)} collective-permute-done((bf16[1,192,768]{2,1,0:T(8,128)(2,1)S(1)}, bf16[1,192,768]{2,1,0:T(8,128)(2,1)S(1)}, u32[]{:S(2)}, u32[]{:S(2)}) %collective-permute-start.29) | collective-permute-done | bytes 294944 | tf_op jit(solution)/shard_map/ppermute | solution.py:96
  307.2 2.1 collective-permute-start.37
  309.3 5.6 %collective-permute-done.37 = f32[24,768]{1,0:T(8,128)} collective-permute-done((f32[24,768]{1,0:T(8,128)}, f32[24,768]{1,0:T(8,128)}, u32[]{:S(2)}, u32[]{:S(2)}) %collective-permute-start.37) | collective-permute-done | bytes 73760 | tf_op jit(solution)/shard_map/ppermute | solution.py:96
  315.0 2.1 collective-permute-done.36
  317.1 4.5 %all-to-all-start.6 = ((bf16[8,96,768]{2,1,0:T(8,128)(2,1)}), bf16[8,96,768]{2,1,0:T(8,128)(2,1)}, u32[]{:S(2)}, u32[]{:S(2)}) async-start(bf16[8,96,768]{2,1,0:T(8,128)(2,1)} %pad_maximum_fusion.1), calls=%async_computation.6 | async-start | bytes 2359296 | tf_op jit(solution)/shard_map/all_to_all | solution.py:62
  323.2 2.0 collective-permute-start.38
  327.7 21.0 %collective-permute-done.38 = bf16[2,192,768]{2,1,0:T(8,128)(2,1)S(1)} collective-permute-done((bf16[2,192,768]{2,1,0:T(8,128)(2,1)S(1)}, bf16[2,192,768]{2,1,0:T(8,128)(2,1)S(1)}, u32[]{:S(2)}, u32[]{:S(2)}) %collective-permute-start.38) | collective-permute-done | bytes 589856 | tf_op jit(solution)/shard_map/ppermute | solution.py:96
  357.7 2.3 fusion.15
  360.0 2.3 fusion.14
  (317 shorter events, 96.0 us)
Async XLA Ops:
  4.1 23.3 %all-to-all-start = ((bf16[8,48,768]{2,1,0:T(8,128)(2,1)}), bf16[8,48,768]{2,1,0:T(8,128)(2,1)S(1)}, u32[]{:S(2)}, u32[]{:S(2)}) async-start(bf16[8,48,768]{2,1,0:T(8,128)(2,1)} %bitcast.3), calls=%async_computation | async-start | bytes 1179648 | tf_op jit(solution)/shard_map/all_to_all | solution.py:62
  11.5 24.0 %collective-permute-start.3 = (bf16[192,768]{1,0:T(8,128)(2,1)S(1)}, bf16[192,768]{1,0:T(8,128)(2,1)}, u32[]{:S(2)}, u32[]{:S(2)}) collective-permute-start(bf16[192,768]{1,0:T(8,128)(2,1)S(1)} %bitcast.200), channel_id=1, source_target_pairs={{0,2},{1,3},{2,0},{3,1},{4,6},{5,7},{6,4},{7,5},{8,10},{9,11},{10,... | collective-permute-start | bytes 884744 | tf_op jit(solution)/shard_map/ppermute | solution.py:58
  13.1 34.7 %collective-permute-start.2 = (bf16[192,768]{1,0:T(8,128)(2,1)S(1)}, bf16[192,768]{1,0:T(8,128)(2,1)}, u32[]{:S(2)}, u32[]{:S(2)}) collective-permute-start(bf16[192,768]{1,0:T(8,128)(2,1)S(1)} %bitcast.197), channel_id=1, source_target_pairs={{0,2},{1,3},{2,0},{3,1},{4,6},{5,7},{6,4},{7,5},{8,10},{9,11},{10,... | collective-permute-start | bytes 884744 | tf_op jit(solution)/shard_map/ppermute | solution.py:58
  13.6 34.2 %collective-permute-start.4 = (bf16[192,768]{1,0:T(8,128)(2,1)}, bf16[192,768]{1,0:T(8,128)(2,1)}, u32[]{:S(2)}, u32[]{:S(2)}) collective-permute-start(bf16[192,768]{1,0:T(8,128)(2,1)} %bitcast.8.wv_ref), channel_id=1, source_target_pairs={{0,2},{1,3},{2,0},{3,1},{4,6},{5,7},{6,4},{7,5},{8,10},{9,11},{10,... | collective-permute-start | bytes 884744 | tf_op jit(solution)/shard_map/ppermute | solution.py:58
  15.1 50.8 %collective-permute-start.7 = (bf16[192,768]{1,0:T(8,128)(2,1)}, bf16[192,768]{1,0:T(8,128)(2,1)}, u32[]{:S(2)}, u32[]{:S(2)}) collective-permute-start(bf16[192,768]{1,0:T(8,128)(2,1)} %w_out_ref.1), channel_id=1, source_target_pairs={{0,1},{1,0},{2,3},{3,2},{4,5},{5,4},{6,7},{7,6},{8,9},{9,8},{10,11... | collective-permute-start | bytes 884744 | tf_op jit(solution)/shard_map/ppermute | solution.py:54
  27.4 9.6 %collective-permute-start = (bf16[384,768]{1,0:T(8,128)(2,1)S(1)}, bf16[384,768]{1,0:T(8,128)(2,1)S(1)}, u32[]{:S(2)}, u32[]{:S(2)}) collective-permute-start(bf16[384,768]{1,0:T(8,128)(2,1)S(1)} %bitcast.153), channel_id=1, source_target_pairs={{0,1},{1,0},{2,3},{3,2},{4,5},{5,4},{6,7},{7,6},{8,9},{9,8},{10,11... | collective-permute-start | bytes 1769480 | tf_op jit(solution)/shard_map/ppermute | solution.py:54
  27.4 27.7 %all-to-all-start.1 = ((bf16[8,48,768]{2,1,0:T(8,128)(2,1)}), bf16[8,48,768]{2,1,0:T(8,128)(2,1)S(1)}, u32[]{:S(2)}, u32[]{:S(2)}) async-start(bf16[8,48,768]{2,1,0:T(8,128)(2,1)} %bitcast.13), calls=%async_computation.1 | async-start | bytes 1179648 | tf_op jit(solution)/shard_map/all_to_all | solution.py:62
  35.5 20.5 %collective-permute-start.8 = (bf16[192,768]{1,0:T(8,128)(2,1)}, bf16[192,768]{1,0:T(8,128)(2,1)S(1)}, u32[]{:S(2)}, u32[]{:S(2)}) collective-permute-start(bf16[192,768]{1,0:T(8,128)(2,1)} %w_out_ref.1), channel_id=1, source_target_pairs={{0,2},{1,3},{2,0},{3,1},{4,6},{5,7},{6,4},{7,5},{8,10},{9,11},{10,... | collective-permute-start | bytes 884744 | tf_op jit(solution)/shard_map/ppermute | solution.py:58
  55.2 2.6 collective-permute-start.6
  56.1 9.9 %collective-permute-start.9 = (bf16[192,768]{1,0:T(8,128)(2,1)S(1)}, bf16[192,768]{1,0:T(8,128)(2,1)}, u32[]{:S(2)}, u32[]{:S(2)}) collective-permute-start(bf16[192,768]{1,0:T(8,128)(2,1)S(1)} %collective-permute-done.8.o2_ref.w_out_ref), channel_id=1, source_target_pairs={{0,1},{1,0},{2,3},{3,2},{4,5},{5,4},{6,7},{7,6},{8,9},{9,8},{10,11... | collective-permute-start | bytes 884744 | tf_op jit(solution)/shard_map/ppermute | solution.py:54
  56.5 9.4 %collective-permute-start.5 = (bf16[768,256]{1,0:T(8,128)(2,1)}, bf16[768,256]{1,0:T(8,128)(2,1)S(1)}, u32[]{:S(2)}, u32[]{:S(2)}) collective-permute-start(bf16[768,256]{1,0:T(8,128)(2,1)} %get-tuple-element.113.m2_ref), channel_id=1, source_target_pairs={{0,1},{1,0},{2,3},{3,2},{4,5},{5,4},{6,7},{7,6},{8,9},{9,8},{10,11... | collective-permute-start | bytes 1179656 | tf_op jit(solution)/shard_map/ppermute | solution.py:54
  56.6 9.3 %collective-permute-start.1 = (bf16[768,256]{1,0:T(8,128)(2,1)S(1)}, bf16[768,256]{1,0:T(8,128)(2,1)}, u32[]{:S(2)}, u32[]{:S(2)}) collective-permute-start(bf16[768,256]{1,0:T(8,128)(2,1)S(1)} %copy-done.54), channel_id=1, source_target_pairs={{0,1},{1,0},{2,3},{3,2},{4,5},{5,4},{6,7},{7,6},{8,9},{9,8},{10,11... | collective-permute-start | bytes 1179656 | tf_op jit(solution)/shard_map/ppermute | solution.py:54
  59.2 26.4 %all-to-all-start.3 = ((bf16[8,64,768]{2,1,0:T(8,128)(2,1)}), bf16[8,64,768]{2,1,0:T(8,128)(2,1)S(1)}, u32[]{:S(2)}, u32[]{:S(2)}) async-start(bf16[8,64,768]{2,1,0:T(8,128)(2,1)} %bitcast.20), calls=%async_computation.3 | async-start | bytes 1572864 | tf_op jit(solution)/shard_map/all_to_all | solution.py:62
  85.6 41.2 %all-to-all-start.2 = ((bf16[8,128,768]{2,1,0:T(8,128)(2,1)}), bf16[8,128,768]{2,1,0:T(8,128)(2,1)}, u32[]{:S(2)}, u32[]{:S(2)}) async-start(bf16[8,128,768]{2,1,0:T(8,128)(2,1)} %bitcast.18), calls=%async_computation.2 | async-start | bytes 3145728 | tf_op jit(solution)/shard_map/all_to_all | solution.py:62
  96.3 18.6 %collective-permute-start.10 = (bf16[8,64,768]{2,1,0:T(8,128)(2,1)S(1)}, bf16[8,64,768]{2,1,0:T(8,128)(2,1)S(1)}, u32[]{:S(2)}, u32[]{:S(2)}) collective-permute-start(bf16[8,64,768]{2,1,0:T(8,128)(2,1)S(1)} %all-to-all-done.3), channel_id=1, source_target_pairs={{0,2},{1,3},{2,0},{3,1},{4,6},{5,7},{6,4},{7,5},{8,10},{9,11},{10,... | collective-permute-start | bytes 2359304 | tf_op jit(solution)/shard_map/ppermute | solution.py:58
  99.3 35.8 %collective-permute-start.13 = (bf16[4,192,768]{2,1,0:T(8,128)(2,1)}, bf16[4,192,768]{2,1,0:T(8,128)(2,1)}, u32[]{:S(2)}, u32[]{:S(2)}) collective-permute-start(bf16[4,192,768]{2,1,0:T(8,128)(2,1)} %dynamic-slice_bitcast_fusion), channel_id=1, source_target_pairs={{0,4},{4,0},{8,12},{12,8},{16,20},{20,16},{24,28},{28,24},{1,5},{5... | collective-permute-start | bytes 3538952 | tf_op jit(solution)/shard_map/ppermute | solution.py:96
  116.7 10.1 %collective-permute-start.11 = (bf16[1024,768]{1,0:T(8,128)(2,1)}, bf16[1024,768]{1,0:T(8,128)(2,1)}, u32[]{:S(2)}, u32[]{:S(2)}) collective-permute-start(bf16[1024,768]{1,0:T(8,128)(2,1)} %bitcast.21.cot_ref.cot_own), channel_id=1, source_target_pairs={{0,1},{1,0},{2,3},{3,2},{4,5},{5,4},{6,7},{7,6},{8,9},{9,8},{10,11... | collective-permute-start | bytes 4718600 | tf_op jit(solution)/shard_map/ppermute | solution.py:54
  126.8 11.4 %collective-permute-start.12 = (bf16[1024,768]{1,0:T(8,128)(2,1)}, bf16[1024,768]{1,0:T(8,128)(2,1)}, u32[]{:S(2)}, u32[]{:S(2)}) collective-permute-start(bf16[1024,768]{1,0:T(8,128)(2,1)} %bitcast.19.rows_ref.rows_own), channel_id=1, source_target_pairs={{0,1},{1,0},{2,3},{3,2},{4,5},{5,4},{6,7},{7,6},{8,9},{9,8},{10,11... | collective-permute-start | bytes 4718600 | tf_op jit(solution)/shard_map/ppermute | solution.py:54
  136.8 14.4 %collective-permute-start.14 = (bf16[2,192,768]{2,1,0:T(8,128)(2,1)S(1)}, bf16[2,192,768]{2,1,0:T(8,128)(2,1)S(1)}, u32[]{:S(2)}, u32[]{:S(2)}) collective-permute-start(bf16[2,192,768]{2,1,0:T(8,128)(2,1)S(1)} %dynamic-slice_bitcast_fusion.2), channel_id=1, source_target_pairs={{0,8},{4,12},{8,0},{12,4},{16,24},{20,28},{24,16},{28,20},{1,9},{5... | collective-permute-start | bytes 1769480 | tf_op jit(solution)/shard_map/ppermute | solution.py:96
  151.4 13.4 %collective-permute-start.15 = (bf16[1024,768]{1,0:T(8,128)(2,1)}, bf16[1024,768]{1,0:T(8,128)(2,1)S(1)}, u32[]{:S(2)}, u32[]{:S(2)}) collective-permute-start(bf16[1024,768]{1,0:T(8,128)(2,1)} %get-tuple-element.133), channel_id=1, source_target_pairs={{0,1},{1,0},{2,3},{3,2},{4,5},{5,4},{6,7},{7,6},{8,9},{9,8},{10,11... | collective-permute-start | bytes 4718600 | tf_op jit(solution)/shard_map/ppermute | solution.py:54
  151.5 18.3 %collective-permute-start.16 = (bf16[1,192,768]{2,1,0:T(8,128)(2,1)S(1)}, bf16[1,192,768]{2,1,0:T(8,128)(2,1)S(1)}, u32[]{:S(2)}, u32[]{:S(2)}) collective-permute-start(bf16[1,192,768]{2,1,0:T(8,128)(2,1)S(1)} %constant_dynamic-slice_fusion.6), channel_id=1, source_target_pairs={{0,16},{4,20},{8,24},{12,28},{16,0},{20,4},{24,8},{28,12},{1,17},{... | collective-permute-start | bytes 884744 | tf_op jit(solution)/shard_map/ppermute | solution.py:96
  170.6 5.0 %collective-permute-start.17 = (bf16[1024,768]{1,0:T(8,128)(2,1)}, bf16[1024,768]{1,0:T(8,128)(2,1)}, u32[]{:S(2)}, u32[]{:S(2)}) collective-permute-start(bf16[1024,768]{1,0:T(8,128)(2,1)} %get-tuple-element.139), channel_id=1, source_target_pairs={{0,1},{1,0},{2,3},{3,2},{4,5},{5,4},{6,7},{7,6},{8,9},{9,8},{10,11... | collective-permute-start | bytes 4718600 | tf_op jit(solution)/shard_map/ppermute | solution.py:54
  170.6 42.6 %all-to-all-start.4 = ((bf16[8,128,768]{2,1,0:T(8,128)(2,1)}), bf16[8,128,768]{2,1,0:T(8,128)(2,1)S(1)}, u32[]{:S(2)}, u32[]{:S(2)}) async-start(bf16[8,128,768]{2,1,0:T(8,128)(2,1)} %bitcast.35), calls=%async_computation.4 | async-start | bytes 3145728 | tf_op jit(solution)/shard_map/all_to_all | solution.py:62
  179.5 19.9 %collective-permute-start.18 = (bf16[8,64,768]{2,1,0:T(8,128)(2,1)}, bf16[8,64,768]{2,1,0:T(8,128)(2,1)}, u32[]{:S(2)}, u32[]{:S(2)}) collective-permute-start(bf16[8,64,768]{2,1,0:T(8,128)(2,1)} %constant_dynamic-slice_fusion.1), channel_id=1, source_target_pairs={{0,2},{1,3},{2,0},{3,1},{4,6},{5,7},{6,4},{7,5},{8,10},{9,11},{10,... | collective-permute-start | bytes 2359304 | tf_op jit(solution)/shard_map/ppermute | solution.py:58
  214.6 2.1 collective-permute-start.19
  216.9 18.0 %collective-permute-start.20 = (bf16[384,768]{1,0:T(8,128)(2,1)S(1)}, bf16[384,768]{1,0:T(8,128)(2,1)S(1)}, u32[]{:S(2)}, u32[]{:S(2)}) collective-permute-start(bf16[384,768]{1,0:T(8,128)(2,1)S(1)} %add_convert_fusion.7), channel_id=1, source_target_pairs={{0,2},{1,3},{2,0},{3,1},{4,6},{5,7},{6,4},{7,5},{8,10},{9,11},{10,... | collective-permute-start | bytes 1769480 | tf_op jit(solution)/shard_map/ppermute | solution.py:58
  219.1 15.7 %collective-permute-start.21 = (bf16[1,192,768]{2,1,0:T(8,128)(2,1)S(1)}, bf16[1,192,768]{2,1,0:T(8,128)(2,1)S(1)}, u32[]{:S(2)}, u32[]{:S(2)}) collective-permute-start(bf16[1,192,768]{2,1,0:T(8,128)(2,1)S(1)} %copy-done.22), channel_id=1, source_target_pairs={{0,16},{4,20},{8,24},{12,28},{16,0},{20,4},{24,8},{28,12},{1,17},{... | collective-permute-start | bytes 884744 | tf_op jit(solution)/shard_map/ppermute | solution.py:96
  219.2 1.3 collective-permute-start.22
  220.5 12.3 %collective-permute-start.23 = (f32[8,768]{1,0:T(8,128)S(1)}, f32[8,768]{1,0:T(8,128)S(1)}, u32[]{:S(2)}, u32[]{:S(2)}) collective-permute-start(f32[8,768]{1,0:T(8,128)S(1)} %fusion.117), channel_id=1, source_target_pairs={{0,2},{1,3},{2,0},{3,1},{4,6},{5,7},{6,4},{7,5},{8,10},{9,11},{10,... | collective-permute-start | bytes 73736 | tf_op jit(solution)/shard_map/ppermute | solution.py:58
  235.0 24.1 %all-to-all-start.5 = ((bf16[8,64,768]{2,1,0:T(8,128)(2,1)}), bf16[8,64,768]{2,1,0:T(8,128)(2,1)S(1)}, u32[]{:S(2)}, u32[]{:S(2)}) async-start(bf16[8,64,768]{2,1,0:T(8,128)(2,1)} %bitcast.45), calls=%async_computation.5 | async-start | bytes 1572864 | tf_op jit(solution)/shard_map/all_to_all | solution.py:62
  238.7 2.0 collective-permute-start.24
  260.4 3.7 %collective-permute-start.26 = (bf16[384,768]{1,0:T(8,128)(2,1)}, bf16[384,768]{1,0:T(8,128)(2,1)S(1)}, u32[]{:S(2)}, u32[]{:S(2)}) collective-permute-start(bf16[384,768]{1,0:T(8,128)(2,1)} %fusion.25), channel_id=1, source_target_pairs={{0,1},{1,0},{2,3},{3,2},{4,5},{5,4},{6,7},{7,6},{8,9},{9,8},{10,11... | collective-permute-start | bytes 1769480 | tf_op jit(solution)/shard_map/ppermute | solution.py:54
  260.5 15.8 %collective-permute-start.30 = (bf16[2,192,768]{2,1,0:T(8,128)(2,1)S(1)}, bf16[2,192,768]{2,1,0:T(8,128)(2,1)S(1)}, u32[]{:S(2)}, u32[]{:S(2)}) collective-permute-start(bf16[2,192,768]{2,1,0:T(8,128)(2,1)S(1)} %maximum_select_fusion.9), channel_id=1, source_target_pairs={{0,8},{4,12},{8,0},{12,4},{16,24},{20,28},{24,16},{28,20},{1,9},{5... | collective-permute-start | bytes 1769480 | tf_op jit(solution)/shard_map/ppermute | solution.py:96
  262.6 15.9 %collective-permute-start.25 = (bf16[2,192,768]{2,1,0:T(8,128)(2,1)S(1)}, bf16[2,192,768]{2,1,0:T(8,128)(2,1)S(1)}, u32[]{:S(2)}, u32[]{:S(2)}) collective-permute-start(bf16[2,192,768]{2,1,0:T(8,128)(2,1)S(1)} %dynamic-slice_bitcast_fusion.1), channel_id=1, source_target_pairs={{0,4},{4,0},{8,12},{12,8},{16,20},{20,16},{24,28},{28,24},{1,5},{5... | collective-permute-start | bytes 1769480 | tf_op jit(solution)/shard_map/ppermute | solution.py:96
  264.6 15.6 %collective-permute-start.28 = (bf16[384,768]{1,0:T(8,128)(2,1)S(1)}, bf16[384,768]{1,0:T(8,128)(2,1)S(1)}, u32[]{:S(2)}, u32[]{:S(2)}) collective-permute-start(bf16[384,768]{1,0:T(8,128)(2,1)S(1)} %add_convert_fusion.5), channel_id=1, source_target_pairs={{0,2},{1,3},{2,0},{3,1},{4,6},{5,7},{6,4},{7,5},{8,10},{9,11},{10,... | collective-permute-start | bytes 1769480 | tf_op jit(solution)/shard_map/ppermute | solution.py:58
  276.7 11.0 %collective-permute-start.31 = (bf16[4,48,768]{2,1,0:T(8,128)(2,1)S(1)}, bf16[4,48,768]{2,1,0:T(8,128)(2,1)S(1)}, u32[]{:S(2)}, u32[]{:S(2)}) collective-permute-start(bf16[4,48,768]{2,1,0:T(8,128)(2,1)S(1)} %slice.84), channel_id=1, source_target_pairs={{0,4},{4,0},{8,12},{12,8},{16,20},{20,16},{24,28},{28,24},{1,5},{5... | collective-permute-start | bytes 884744 | tf_op jit(solution)/shard_map/ppermute | solution.py:96
  278.7 9.7 %collective-permute-start.27 = (bf16[1,192,768]{2,1,0:T(8,128)(2,1)S(1)}, bf16[1,192,768]{2,1,0:T(8,128)(2,1)S(1)}, u32[]{:S(2)}, u32[]{:S(2)}) collective-permute-start(bf16[1,192,768]{2,1,0:T(8,128)(2,1)S(1)} %constant_dynamic-slice_fusion), channel_id=1, source_target_pairs={{0,8},{4,12},{8,0},{12,4},{16,24},{20,28},{24,16},{28,20},{1,9},{5... | collective-permute-start | bytes 884744 | tf_op jit(solution)/shard_map/ppermute | solution.py:96
  287.6 3.2 collective-permute-start.32
  288.5 16.5 %collective-permute-start.29 = (bf16[1,192,768]{2,1,0:T(8,128)(2,1)S(1)}, bf16[1,192,768]{2,1,0:T(8,128)(2,1)S(1)}, u32[]{:S(2)}, u32[]{:S(2)}) collective-permute-start(bf16[1,192,768]{2,1,0:T(8,128)(2,1)S(1)} %add_convert_fusion.11), channel_id=1, source_target_pairs={{0,16},{4,20},{8,24},{12,28},{16,0},{20,4},{24,8},{28,12},{1,17},{... | collective-permute-start | bytes 884744 | tf_op jit(solution)/shard_map/ppermute | solution.py:96
  291.4 1.2 collective-permute-start.33
  292.7 4.4 %collective-permute-start.34 = (f32[24,768]{1,0:T(8,128)S(1)}, f32[24,768]{1,0:T(8,128)S(1)}, u32[]{:S(2)}, u32[]{:S(2)}) collective-permute-start(f32[24,768]{1,0:T(8,128)S(1)} %select_maximum_fusion), channel_id=1, source_target_pairs={{0,4},{4,0},{8,12},{12,8},{16,20},{20,16},{24,28},{28,24},{1,5},{5... | collective-permute-start | bytes 221192 | tf_op jit(solution)/shard_map/ppermute | solution.py:96
  297.1 9.3 %collective-permute-start.35 = (f32[24,768]{1,0:T(8,128)S(1)}, f32[24,768]{1,0:T(8,128)S(1)}, u32[]{:S(2)}, u32[]{:S(2)}) collective-permute-start(f32[24,768]{1,0:T(8,128)S(1)} %fusion.122), channel_id=1, source_target_pairs={{0,8},{4,12},{8,0},{12,4},{16,24},{20,28},{24,16},{28,20},{1,9},{5... | collective-permute-start | bytes 221192 | tf_op jit(solution)/shard_map/ppermute | solution.py:96
  297.8 27.5 %collective-permute-start.39 = (bf16[4,144,768]{2,1,0:T(8,128)(2,1)S(1)}, bf16[4,144,768]{2,1,0:T(8,128)(2,1)S(1)}, u32[]{:S(2)}, u32[]{:S(2)}) collective-permute-start(bf16[4,144,768]{2,1,0:T(8,128)(2,1)S(1)} %slice.89), channel_id=1, source_target_pairs={{0,4},{4,0},{8,12},{12,8},{16,20},{20,16},{24,28},{28,24},{1,5},{5... | collective-permute-start | bytes 2654216 | tf_op jit(solution)/shard_map/ppermute | solution.py:96
  306.5 10.6 %collective-permute-start.36 = (bf16[1,192,768]{2,1,0:T(8,128)(2,1)S(1)}, bf16[1,192,768]{2,1,0:T(8,128)(2,1)S(1)}, u32[]{:S(2)}, u32[]{:S(2)}) collective-permute-start(bf16[1,192,768]{2,1,0:T(8,128)(2,1)S(1)} %add_convert_fusion.10), channel_id=1, source_target_pairs={{0,8},{4,12},{8,0},{12,4},{16,24},{20,28},{24,16},{28,20},{1,9},{5... | collective-permute-start | bytes 884744 | tf_op jit(solution)/shard_map/ppermute | solution.py:96
  307.2 7.8 %collective-permute-start.37 = (f32[24,768]{1,0:T(8,128)}, f32[24,768]{1,0:T(8,128)}, u32[]{:S(2)}, u32[]{:S(2)}) collective-permute-start(f32[24,768]{1,0:T(8,128)} %add.303), channel_id=1, source_target_pairs={{0,16},{4,20},{8,24},{12,28},{16,0},{20,4},{24,8},{28,12},{1,17},{... | collective-permute-start | bytes 221192 | tf_op jit(solution)/shard_map/ppermute | solution.py:96
  317.1 33.5 %all-to-all-start.6 = ((bf16[8,96,768]{2,1,0:T(8,128)(2,1)}), bf16[8,96,768]{2,1,0:T(8,128)(2,1)}, u32[]{:S(2)}, u32[]{:S(2)}) async-start(bf16[8,96,768]{2,1,0:T(8,128)(2,1)} %pad_maximum_fusion.1), calls=%async_computation.6 | async-start | bytes 2359296 | tf_op jit(solution)/shard_map/all_to_all | solution.py:62
  323.2 25.5 %collective-permute-start.38 = (bf16[2,192,768]{2,1,0:T(8,128)(2,1)S(1)}, bf16[2,192,768]{2,1,0:T(8,128)(2,1)S(1)}, u32[]{:S(2)}, u32[]{:S(2)}) collective-permute-start(bf16[2,192,768]{2,1,0:T(8,128)(2,1)S(1)} %maximum_select_fusion.11), channel_id=1, source_target_pairs={{0,4},{4,0},{8,12},{12,8},{16,20},{20,16},{24,28},{28,24},{1,5},{5... | collective-permute-start | bytes 1769480 | tf_op jit(solution)/shard_map/ppermute | solution.py:96
  350.5 5.8 %collective-permute-start.40 = (bf16[8,96,768]{2,1,0:T(8,128)(2,1)}, bf16[8,96,768]{2,1,0:T(8,128)(2,1)}, u32[]{:S(2)}, u32[]{:S(2)}) collective-permute-start(bf16[8,96,768]{2,1,0:T(8,128)(2,1)} %all-to-all-done.6), channel_id=1, source_target_pairs={{0,1},{1,0},{2,3},{3,2},{4,5},{5,4},{6,7},{7,6},{8,9},{9,8},{10,11... | collective-permute-start | bytes 3538952 | tf_op jit(solution)/shard_map/ppermute | solution.py:54
  (61 other events, 284.4 us)
